TPU v7x, 32 devices: a whole 2x2x4 slice. The times are simulated.
32 devices in a mesh: dp: 4 (over z), fsdp: 4 (over x, core), ctx: 2 (over y).
Axes of the slice: x: 2, y: 2, z: 4, core: 2. Of those that a mesh axis runs over, the one named last changes fastest.
Arguments:
- tokens: bfloat16 [16, 1024, 1024], P(('dp', 'fsdp'), 'ctx')
- bounds: int32 [16, 1024], P(('dp', 'fsdp'), 'ctx'), may hold values 0 or 1
- decay_rates: float32 [16], replicated, may hold values from 9.765625e-05 to 0.9
- w_query: bfloat16 [1024, 1024], P('fsdp')
- w_key: bfloat16 [1024, 1024], P('fsdp')
- w_up: bfloat16 [1024, 2048], P('fsdp'), may hold values from -0.1875 to 0.1875
- grad_out: bfloat16 [16, 1024, 2048], P(('dp', 'fsdp'), 'ctx'), may hold values from -6 to 6
Outputs:
- dechunked: bfloat16 [16, 1024, 2048], P(('dp', 'fsdp'), 'ctx')
- grad_tokens: bfloat16 [16, 1024, 1024], P(('dp', 'fsdp'), 'ctx')
- grad_query: float32 [1024, 1024], P('fsdp')
- grad_key: float32 [1024, 1024], P('fsdp')
- grad_up: float32 [1024, 2048], P('fsdp')
All inputs are finite; a program needn't handle non-finite values. No bound on the sum of `bounds` on one device may be relied on, other than what follows from the above.
Results may differ from a plain program's by a relative error of at most 0.0049.
Values may be sent and summed in bfloat16 or wider, within the bound.
A program may use at most 128 MiB of HBM per device.

v0:
```python
import jax
import jax.numpy as jnp
from jax import lax
from jax.sharding import PartitionSpec as P

SPAN = 128


epsilon = 1e-06


def shifted(x, axis, by):
    devices = lax.axis_size(axis)
    pairs = [(i, i + by) for i in range(devices) if 0 <= i + by < devices]
    return lax.ppermute(x, axis, pairs)


def carried_in(part, axis, combine, identity, reverse):
    count = lax.axis_size(axis)
    place = lax.axis_index(axis)
    ahead = count - 1 - place if reverse else place
    gathered = jax.tree.map(lambda a: lax.all_gather(a, axis), part)
    state = jax.tree.map(lambda a, e: jnp.zeros_like(a) + jnp.asarray(e, a.dtype), part, identity)

    def one(turn, state):
        source = count - 1 - turn if reverse else turn
        return combine(
            state, jax.tree.map(lambda a: lax.dynamic_index_in_dim(a, source, 0, False), gathered)
        )

    return lax.fori_loop(0, ahead, one, state)


def chain_pair(earlier, latter):
    decay_first, state_first = earlier
    decay_second, state_second = latter
    return (decay_first * decay_second, decay_second[..., None] * state_first + state_second)


def per_device(tokens, bounds, decay_rates, w_query, w_key, w_up, grad_out):
    batch_local, length, model_width = tokens.shape
    hidden = w_up.shape[1]
    head_count = decay_rates.shape[0]
    channels = hidden // head_count
    blocks = length // SPAN
    columns_all = 2 * model_width + hidden
    flat_tokens = tokens.reshape(batch_local * length, model_width)
    panels = jnp.concatenate([w_query, w_key, w_up], 1)
    full_panels = lax.all_gather(panels, "fsdp", axis=0, tiled=True)
    projected = jnp.dot(flat_tokens, full_panels, preferred_element_type=jnp.float32)
    queries = projected[:, :model_width].reshape(batch_local, length, model_width)
    keys_now = projected[:, model_width : 2 * model_width].reshape(batch_local, length, model_width)
    values = projected[:, 2 * model_width :].reshape(
        batch_local, blocks, SPAN, head_count, channels
    )
    key_before = shifted(keys_now[:, -1:, :], "ctx", 1)
    keys_prev = jnp.concatenate([key_before, keys_now[:, :-1]], 1)
    inv_query = lax.rsqrt(jnp.sum(queries * queries, -1) + epsilon)
    inv_key = lax.rsqrt(jnp.sum(keys_prev * keys_prev, -1) + epsilon)
    cosine = jnp.sum(queries * keys_prev, -1) * inv_query * inv_key
    own_index = lax.axis_index("ctx")
    opening = jnp.logical_and(own_index == 0, jnp.arange(length) == 0)[None, :]
    boundary_prob = jnp.where(opening, 1.0, 0.5 * (1.0 - cosine))
    marked = jnp.where(opening, 1.0, bounds.astype(jnp.float32))
    mix_rate = (marked * boundary_prob)[..., None] * decay_rates
    rate_blocks = mix_rate.reshape(batch_local, blocks, SPAN, head_count)
    log_keep = jnp.cumsum(jnp.log(1.0 - rate_blocks), axis=2)
    keep_heads = jnp.moveaxis(log_keep, 3, 2)
    log_gap = keep_heads[..., :, None] - keep_heads[..., None, :]
    offsets = jnp.arange(SPAN)
    lower_mask = offsets[:, None] >= offsets[None, :]
    upper_mask = offsets[:, None] <= offsets[None, :]
    forward_band = (
        jnp.where(lower_mask, jnp.exp(jnp.where(lower_mask, log_gap, -1e30)), 0.0)
        * jnp.moveaxis(rate_blocks, 3, 2)[..., None, :]
    )
    local_states = jnp.einsum(
        "bnhtu,bnuhc->bnthc", forward_band, values, precision=lax.Precision.HIGHEST
    )
    block_logs = log_keep[:, :, -1]
    block_decay = jnp.exp(block_logs)
    running_logs = jnp.cumsum(block_logs, axis=1)
    decay_before = jnp.exp(running_logs - block_logs)
    decay_after = jnp.exp(running_logs[:, -1:] - running_logs)
    device_decay = jnp.exp(running_logs[:, -1])
    inner_zero = jnp.zeros((batch_local, head_count, channels), jnp.float32)

    def walk_blocks(carried, element):
        decay_now, addition = element
        return (decay_now[..., None] * carried + addition, carried)

    device_state, block_in = lax.scan(
        walk_blocks,
        inner_zero,
        (jnp.moveaxis(block_decay, 1, 0), jnp.moveaxis(local_states[:, :, -1], 1, 0)),
    )
    identity_pair = (jnp.ones_like(device_decay), inner_zero)
    _, state_in = carried_in((device_decay, device_state), "ctx", chain_pair, identity_pair, False)
    block_carry = jnp.moveaxis(block_in, 0, 1) + decay_before[..., None] * state_in[:, None]
    states = local_states + jnp.exp(log_keep)[..., None] * block_carry[:, :, None]
    dechunked = states.reshape(batch_local, length, hidden).astype(jnp.bfloat16)
    state_rows = states.reshape(batch_local, length, head_count, channels)
    states_prev = jnp.concatenate([state_in[:, None], state_rows[:, :-1]], 1)
    cotangent = grad_out.astype(jnp.float32).reshape(
        batch_local, blocks, SPAN, head_count, channels
    )
    backward_band = jnp.where(upper_mask, jnp.exp(jnp.where(upper_mask, -log_gap, -1e30)), 0.0)
    local_adjoint = jnp.einsum(
        "bnhtu,bnuhc->bnthc", backward_band, cotangent, precision=lax.Precision.HIGHEST
    )
    block_heads = (1.0 - rate_blocks[:, :, 0])[..., None] * local_adjoint[:, :, 0]
    device_head, block_out = lax.scan(
        walk_blocks,
        inner_zero,
        (jnp.moveaxis(block_decay, 1, 0), jnp.moveaxis(block_heads, 1, 0)),
        reverse=True,
    )
    _, adjoint_in = carried_in((device_decay, device_head), "ctx", chain_pair, identity_pair, True)
    block_from = jnp.moveaxis(block_out, 0, 1) + decay_after[..., None] * adjoint_in[:, None]
    adjoints = (
        local_adjoint + jnp.exp(log_keep[:, :, -1:] - log_keep)[..., None] * block_from[:, :, None]
    )
    adjoint_rows = adjoints.reshape(batch_local, length, head_count, channels)
    d_values = (
        (mix_rate[..., None] * adjoint_rows)
        .reshape(batch_local, length, hidden)
        .astype(jnp.bfloat16)
    )
    value_rows = values.reshape(batch_local, length, head_count, channels)
    d_rate = jnp.sum(adjoint_rows * (value_rows - states_prev), -1)
    d_prob = jnp.where(opening, 0.0, marked * jnp.sum(d_rate * decay_rates, -1))
    d_cos = -0.5 * d_prob
    pair_scale = inv_query * inv_key
    d_query = (
        d_cos[..., None]
        * (
            keys_prev * pair_scale[..., None]
            - (cosine * inv_query * inv_query)[..., None] * queries
        )
    ).astype(jnp.bfloat16)
    d_prev = d_cos[..., None] * (
        queries * pair_scale[..., None] - (cosine * inv_key * inv_key)[..., None] * keys_prev
    )
    key_after = shifted(d_prev[:, :1, :], "ctx", -1)
    d_key = jnp.concatenate([d_prev[:, 1:], key_after], 1).astype(jnp.bfloat16)
    d_all = jnp.concatenate([d_query, d_key, d_values], 2).reshape(
        batch_local * length, columns_all
    )
    d_flat = lax.dot_general(
        d_all, full_panels, (((1,), (1,)), ((), ())), preferred_element_type=jnp.float32
    )
    grad_tokens = d_flat.reshape(batch_local, length, model_width).astype(jnp.bfloat16)
    grads = lax.dot_general(
        flat_tokens, d_all, (((0,), (0,)), ((), ())), preferred_element_type=jnp.float32
    )
    reduced = lax.psum_scatter(grads, ("fsdp", "ctx"), scatter_dimension=0, tiled=True)
    reduced = lax.psum(reduced, "dp")
    summed = lax.all_gather(reduced, "ctx", axis=0, tiled=True)
    return (
        dechunked,
        grad_tokens,
        summed[:, :model_width],
        summed[:, model_width : 2 * model_width],
        summed[:, 2 * model_width :],
    )


def solution(mesh):
    return jax.shard_map(
        per_device,
        mesh=mesh,
        in_specs=(
            P(("dp", "fsdp"), "ctx", None),
            P(("dp", "fsdp"), "ctx"),
            P(),
            P("fsdp", None),
            P("fsdp", None),
            P("fsdp", None),
            P(("dp", "fsdp"), "ctx", None),
        ),
        out_specs=(
            P(("dp", "fsdp"), "ctx", None),
            P(("dp", "fsdp"), "ctx", None),
            P("fsdp", None),
            P("fsdp", None),
            P("fsdp", None),
        ),
        check_vma=False,
    )
```

profile of v0, /device:TPU:0, one launch (start us, length us, event | category | flops | bytes accessed | tf_op | source)
XLA Modules:
  0.0 478.5 jit_solution(14739115348460215633)
XLA Ops:
  7.2 3.2 pad_maximum_fusion.2
  10.5 1.9 copy.154
  12.5 0.6 iota_compare_fusion.1
  13.1 58.5 %all-gather.5.cloned.1.call-done = bf16[1024,4096]{1,0:T(8,128)(2,1)} async-done(((bf16[256,4096]{1,0:T(8,128)(2,1)}), bf16[1024,4096]{1,0:T(8,128)(2,1)}) %all-gather.5.cloned.1.call-update) | async-done | bytes 8388624 | tf_op jit(solution)/shard_map/all_gather | solution.py:49
  71.6 6.9 %convolution_bitcast_fusion.1 = f32[512,4096]{1,0:T(8,128)S(1)} fusion(bf16[1024,4096]{1,0:T(8,128)(2,1)} %all-gather.5.cloned.1.call-done, bf16[1,512,1024]{2,1,0:T(8,128)(2,1)S(1)} %copy-done), kind=kOutput, calls=%fused_computation.14 | convolution fusion | flops 4294967296 | bytes 17825792 | tf_op jit(solution)/shard_map/dot_general | solution.py:50
  78.7 0.5 slice_bitcast_fusion
  79.3 3.4 collective-permute-start
  82.7 0.3 slice_bitcast_fusion.3
  83.0 2.9 copy.153
  85.9 0.6 multiply_reduce_fusion
  86.4 0.4 fusion.26
  86.8 0.6 multiply_multiply_fusion.1
  87.6 0.8 copy.129
  88.4 1.2 reduce_window_sum.26
  89.7 0.6 copy-done.16
  90.4 7.8 %fusion.21 = f32[1,4,128,16,128]{4,2,3,1,0:T(8,128)S(1)} fusion(f32[4,128,16,128]{3,2,1,0:T(8,128)} %bitcast.152, f32[4,16,128]{2,1,0:T(8,128)S(1)} %get-tuple-element.516, f32[4,16,128]{2,1,0:T(8,128)S(1)} %copy.130, pred[128,128]{1,0:T(8,128)(4,1)} %iota_compare_fusion.1), kind=kOutput, calls=%fused_computation.38 | convolution fusion | flops 1614807040 | bytes 8470528 | tf_op jit(solution)/shard_map/bnhtu,bnuhc->bnthc/dot_general | solution.py:77
  98.2 1.9 copy-done.6
  100.2 0.4 while.58
  100.6 4.4 all-gather
  105.0 4.2 all_gather.25
  109.2 0.9 fusion.50
  110.1 0.6 fusion.53
  110.7 5.0 %fusion.18 = f32[1,4,128,16,128]{4,2,3,1,0:T(8,128)S(1)} fusion(bf16[4,128,16,128]{3,2,1,0:T(8,128)(2,1)} %bitcast.158, f32[4,16,128]{2,1,0:T(8,128)} %copy-done.16, pred[128,128]{1,0:T(8,128)(4,1)S(1)} %iota_compare_fusion), kind=kOutput, calls=%fused_computation.37 | convolution fusion | flops 1614807040 | bytes 6340608 | tf_op jit(solution)/shard_map/bnhtu,bnuhc->bnthc/dot_general | solution.py:108
  115.8 2.0 copy-done.7
  118.0 3.0 while.59
  118.0 0.7 fusion.67
  118.8 0.7 fusion.67
  119.5 0.7 fusion.67
  120.2 0.7 fusion.67
  121.0 4.4 all-gather.1
  125.3 0.9 while.57
  125.3 0.7 dynamic-slice_bitcast_fusion.5
  126.3 0.8 bitcast_add_fusion.4
  127.1 3.8 fusion.59
  130.9 2.4 copy.143
  133.4 2.2 slice.76
  135.7 2.6 pad_maximum_fusion.1
  138.3 0.8 copy-done.3
  139.2 1.3 copy-done.8
  140.5 3.8 fusion.16
  144.5 2.1 multiply_bitcast_fusion
  146.6 1.0 copy-done.9
  147.5 1.3 collective-permute-start.1
  148.8 4.4 copy.146
  153.3 2.8 mul.510
  156.2 9.8 %multiply_convert_fusion = bf16[1,512,2048]{2,0,1:T(2,128)(2,1)} fusion(f32[1,512,2048]{2,0,1:T(1,128)} %bitcast.151, f32[1,512,2048]{2,0,1:T(1,128)} %bitcast.150), kind=kLoop, calls=%fused_computation.34 | loop fusion | flops 2097152 | bytes 10485760 | tf_op jit(solution)/shard_map/convert_element_type | solution.py:127
  166.0 2.2 fusion.47
  168.2 0.3 slice.98
  168.4 1.6 copy.147
  170.2 1.6 copy.148
  171.8 9.9 %pad_maximum_fusion = bf16[1,512,4096]{2,0,1:T(2,128)(2,1)S(1)} fusion(bf16[1,512,2048]{2,0,1:T(2,128)(2,1)S(1)} %copy-done.2, bf16[1,512,1024]{2,0,1:T(2,128)(2,1)S(1)} %copy.148, bf16[1,512,1024]{2,0,1:T(2,128)(2,1)S(1)} %copy.147), kind=kLoop, calls=%fused_computation.13 | loop fusion | flops 12582912 | bytes 8388608 | tf_op jit(solution)/shard_map/concatenate | solution.py:146
  181.7 3.2 copy-done.5
  184.9 15.5 %convolution_bitcast_fusion = f32[1024,4096]{0,1:T(8,128)} fusion(bf16[1,512,4096]{2,0,1:T(2,128)(2,1)S(1)} %pad_maximum_fusion, bf16[1,512,1024]{2,1,0:T(8,128)(2,1)S(1)} %copy-done), kind=kOutput, calls=%fused_computation.12 | convolution fusion | flops 4294967296 | bytes 22020096 | tf_op jit(solution)/shard_map/dot_general | solution.py:153
  200.5 117.2 %reduce-scatter.2.cloned.1.call-done = f32[128,4096]{0,1:T(8,128)} async-done(((f32[1024,4096]{0,1:T(8,128)}), f32[128,4096]{0,1:T(8,128)}) %reduce-scatter.2.cloned.1.call-update) | async-done | bytes 2097168 | tf_op jit(solution)/shard_map/reduce_scatter | solution.py:156
  317.8 88.8 %all-reduce.2.cloned.1.call-done = f32[128,4096]{0,1:T(8,128)} async-done(((f32[128,4096]{0,1:T(8,128)}), f32[128,4096]{0,1:T(8,128)}) %all-reduce.2.cloned.1.call-update) | async-done | bytes 2097168 | tf_op jit(solution)/shard_map/psum | solution.py:157
  406.6 2.7 copy.137
  409.3 4.4 convert_element_type.52
  413.7 15.2 %fusion.44 = bf16[1,512,1024]{2,1,0:T(8,128)(2,1)} fusion(bf16[1024,4096]{1,0:T(8,128)(2,1)} %all-gather.5.cloned.1.call-done, bf16[1,512,4096]{2,0,1:T(2,128)(2,1)} %copy-done.5), kind=kOutput, calls=%fused_computation.64 | convolution fusion | flops 4295491584 | bytes 13631488 | tf_op jit(solution)/shard_map/dot_general | solution.py:149
  428.9 34.8 %all-gather.7.cloned.1.call-done = f32[256,4096]{0,1:T(8,128)} async-done(((f32[128,4096]{0,1:T(8,128)}), f32[256,4096]{0,1:T(8,128)}) %all-gather.7.cloned.1.call-update) | async-done | bytes 4194320 | tf_op jit(solution)/shard_map/all_gather | solution.py:158
  463.8 1.6 slice-done
  465.3 1.8 copy.151
  467.2 1.7 fusion.60
  468.8 1.3 copy.149
  470.1 1.3 copy.150
  (108 shorter events, 2.3 us)
Async XLA Ops:
  7.2 64.4 %copy-start = (bf16[1,512,1024]{2,1,0:T(8,128)(2,1)S(1)}, bf16[1,512,1024]{2,1,0:T(8,128)(2,1)}, u32[]{:S(2)}) copy-start(bf16[1,512,1024]{2,1,0:T(8,128)(2,1)} %param.15) | copy-start | bytes 3145732
  7.2 3.4 copy-start.11
  7.2 64.4 %all-gather.5.cloned.1.call-start = ((), (), s32[]{:S(2)}) async-start(), calls=%async_computation.1 | async-start | bytes 10485760 | tf_op jit(solution)/shard_map/all_gather | solution.py:49
  10.5 307.2 %reduce-scatter.2.cloned.1.call-start = ((), (), s32[]{:S(2)}) async-start(), calls=%async_computation.2 | async-start | bytes 18874368 | tf_op jit(solution)/shard_map/reduce_scatter | solution.py:156
  78.5 7.4 %copy-start.1 = (f32[512,4096]{1,0:T(8,128)}, f32[512,4096]{1,0:T(8,128)S(1)}, u32[]{:S(2)}) copy-start(f32[512,4096]{1,0:T(8,128)S(1)} %convolution_bitcast_fusion.1) | copy-start | bytes 25165828
  79.3 6.6 %collective-permute-start = (f32[1,1,1024]{2,1,0:T(1,128)S(1)}, f32[1,1,1024]{2,1,0:T(1,128)S(1)}, u32[]{:S(2)}, u32[]{:S(2)}) collective-permute-start(f32[1,1,1024]{2,1,0:T(1,128)S(1)} %slice.70), channel_id=1, source_target_pairs={{0,1},{2,3},{4,5},{6,7},{8,9},{10,11},{12,13},{14,15},{16,17},{18,... | collective-permute-start | bytes 12296 | tf_op jit(solution)/shard_map/ppermute | solution.py:15
  85.9 1.6 copy-start.22
  85.9 1.6 copy-start.24
  85.9 1.6 copy-start.14
  87.5 2.2 copy-start.18
  89.7 0.6 copy-start.16
  98.2 2.0 copy-start.6
  100.6 15.1 %copy-start.26 = (f32[4,1,16]{2,1,0:T(1,128)}, f32[4,1,16]{2,1,0:T(1,128)S(1)}, u32[]{:S(2)}) copy-start(f32[4,1,16]{2,1,0:T(1,128)S(1)} %get-tuple-element.762) | copy-start | bytes 772
  109.2 6.5 %copy-start.27 = (f32[2,1,16]{2,1,0:T(1,128)}, f32[2,1,16]{2,1,0:T(1,128)S(1)}, u32[]{:S(2)}) copy-start(f32[2,1,16]{2,1,0:T(1,128)S(1)} %get-tuple-element.764) | copy-start | bytes 388
  110.7 15.5 %copy-start.13 = (f32[4,128,16]{2,1,0:T(8,128)S(1)}, f32[4,128,16]{2,1,0:T(8,128)}, u32[]{:S(2)}) copy-start(f32[4,128,16]{2,1,0:T(8,128)} %get-tuple-element.508) | copy-start | bytes 98308
  115.8 2.0 copy-start.7
  133.4 2.2 copy-start.12
  135.7 3.5 copy-start.3
  135.7 4.7 copy-start.8
  140.4 3.9 copy-start.25
  140.4 4.0 copy-start.23
  140.4 4.0 copy-start.15
  140.4 4.0 copy-start.17
  140.4 4.0 copy-start.21
  146.6 1.0 copy-start.9
  147.5 22.5 %collective-permute-start.1 = (bf16[1,1,1024]{2,1,0:T(2,128)(2,1)S(1)}, bf16[1,1,1024]{2,1,0:T(2,128)(2,1)S(1)}, u32[]{:S(2)}, u32[]{:S(2)}) collective-permute-start(bf16[1,1,1024]{2,1,0:T(2,128)(2,1)S(1)} %slice.78), channel_id=1, source_target_pairs={{1,0},{3,2},{5,4},{7,6},{9,8},{11,10},{13,12},{15,14},{17,16},{19,... | collective-permute-start | bytes 6152 | tf_op jit(solution)/shard_map/ppermute | solution.py:15
  148.8 4.4 copy-start.19
  156.2 9.8 %copy-start.20 = (f32[512]{0:T(512)S(1)}, f32[512]{0:T(512)}, u32[]{:S(2)}) copy-start(f32[512]{0:T(512)} %get-tuple-element.511) | copy-start | bytes 6148
  166.0 2.2 copy-start.10
  168.4 3.4 copy-start.2
  181.7 3.2 copy-start.5
  200.4 206.2 %copy-start.4 = (bf16[1,4,128,16,128]{4,2,3,1,0:T(8,128)(2,1)S(1)}, bf16[1,4,128,16,128]{4,2,3,1,0:T(8,128)(2,1)}, u32[]{:S(2)}) copy-start(bf16[1,4,128,16,128]{4,2,3,1,0:T(8,128)(2,1)} %get-tuple-element.501) | copy-start | bytes 6291460
  200.4 206.2 %all-reduce.2.cloned.1.call-start = ((), (), s32[]{:S(2)}) async-start(), calls=%async_computation.3 | async-start | bytes 4194304 | tf_op jit(solution)/shard_map/psum | solution.py:157
  317.7 146.0 %all-gather.7.cloned.1.call-start = ((), (), s32[]{:S(2)}) async-start(), calls=%async_computation.4 | async-start | bytes 6291456 | tf_op jit(solution)/shard_map/all_gather | solution.py:158
  463.8 1.6 slice-start
Sparse Core Ops, SparseCore 0:
  10.6 60.9 all-gather.4
  200.5 117.0 reduce-scatter.1
  320.1 86.4 all-reduce.1
  408.1 55.6 all-gather.6
where the time goes:
time: 486 us; the launch traced here: 478 us
  waiting for transfers between devices  299 us (62%)
  local copies, waits for them, and re-layouts  51.5 us (11%)
  matrix products  50.4 us (10%)
  other arithmetic  44.5 us (9%)
  between operations  14.8 us (3%)
  blocking collectives  12.9 us (3%)
    reduce_scatter x1, waiting for transfers between devices, per_device(): lax.psum_scatter(grads, ('fsdp', 'ctx'), scatter_dimension=0, tiled=True)  117 us
    psum x1, waiting for transfers between devices, per_device(): reduced = lax.psum(reduced, 'dp')  88.8 us
    all_gather x1, waiting for transfers between devices, per_device(): full_panels = lax.all_gather(panels, 'fsdp', axis=0, tiled=True)  58.5 us
    all_gather x1, waiting for transfers between devices, per_device(): summed = lax.all_gather(reduced, 'ctx', axis=0, tiled=True)  34.8 us
    unnamed x62, local copies, waits for them, and re-layouts  20.7 us
    dot_general x1, matrix products, per_device(): lax.dot_general(flat_tokens, d_all, (((0,), (0,)), ((), ())), preferred_e...  15.5 us
    dot_general x1, matrix products, per_device(): lax.dot_general(d_all, full_panels, (((1,), (1,)), ((), ())), preferred_e...  15.2 us
    all_gather x3, blocking collectives, carried_in(): gathered = jax.tree.map(lambda a: lax.all_gather(a, axis), part)  12.9 us
  transfers between devices with their start and end apart: 6, of which 4 were waited for; matrix products, arithmetic and copies ran while one was open for 10% of the time, Pallas kernels for 0%

commit v1 on v0

v1 whole, which is shorter than its diff:
```python
import functools

import jax
import jax.numpy as jnp
from jax import lax
from jax.experimental import pallas as pl
from jax.experimental.pallas import tpu as pltpu
from jax.sharding import PartitionSpec as P

SPAN = 128
epsilon = 1e-06
F32 = jnp.float32
BF16 = jnp.bfloat16
LIMIT = 48 * 1024 * 1024


def call(kernel, grid, in_specs, out_specs, out_shape, scratch, flops, moved, name):
    return pl.pallas_call(
        kernel,
        grid=grid,
        in_specs=in_specs,
        out_specs=out_specs,
        out_shape=out_shape,
        scratch_shapes=scratch,
        name=name,
        compiler_params=pltpu.CompilerParams(vmem_limit_bytes=LIMIT),
        cost_estimate=pl.CostEstimate(flops=flops, bytes_accessed=moved, transcendentals=0),
    )


def whole(shape):
    return pl.BlockSpec(shape, lambda i: (0,) * len(shape))


def rows_of(tile, width):
    return pl.BlockSpec((tile, width), lambda i: (i, 0))


def mm(a, b):
    return lax.dot_general(a, b, (((1,), (0,)), ((), ())), preferred_element_type=F32)


def route_kernel(parts, width, *refs):
    tok, tok_prev, marked, opening = refs[:4]
    shards = refs[4 : 4 + parts]
    q_out, k_out, iq_out, ik_out, cos_out, mp_out = refs[4 + parts :]
    depth = shards[0].shape[0]
    q = k = None
    for p in range(parts):
        span = slice(p * depth, (p + 1) * depth)
        one_q = mm(tok[:, span], shards[p][:, :width])
        one_k = mm(tok_prev[:, span], shards[p][:, width:])
        q = one_q if q is None else q + one_q
        k = one_k if k is None else k + one_k
    iq = lax.rsqrt(jnp.sum(q * q, -1, keepdims=True) + epsilon)
    ik = lax.rsqrt(jnp.sum(k * k, -1, keepdims=True) + epsilon)
    cosine = jnp.sum(q * k, -1, keepdims=True) * iq * ik
    q_out[...] = q
    k_out[...] = k
    iq_out[...] = iq
    ik_out[...] = ik
    cos_out[...] = cosine
    prob = jnp.where(opening[...] > 0, 1.0, 0.5 * (1.0 - cosine))
    mp_out[...] = marked[...] * prob


def log_sums(rate):
    log_keep = jnp.log(1.0 - rate)
    row = lax.broadcasted_iota(jnp.int32, (SPAN, SPAN), 0)
    col = lax.broadcasted_iota(jnp.int32, (SPAN, SPAN), 1)
    lower = (row >= col).astype(F32)
    sums = jnp.dot(lower, log_keep, precision=lax.Precision.HIGHEST, preferred_element_type=F32)
    return log_keep, sums, row, col


def adjoint_kernel(heads, channels, mp, decay, cot, adj_out, tail_out, head_out, dec_out, carry, run):
    @pl.when(pl.program_id(0) == 0)
    def _():
        carry[...] = jnp.zeros_like(carry)
        run[...] = jnp.zeros_like(run)

    rate = mp[...] * decay[...]
    _, sums, row, col = log_sums(rate)
    sums_t = sums.T
    total = sums[SPAN - 1 : SPAN, :]
    tail = jnp.exp(total - sums)
    tail_out[...] = tail * jnp.exp(run[...])
    keep_first = 1.0 - rate[0:1, :]
    for h in range(heads):
        lanes = slice(h * channels, (h + 1) * channels)
        gap = sums_t[h : h + 1, :] - sums[:, h : h + 1]
        band = jnp.where(col >= row, jnp.exp(jnp.minimum(gap, 0.0)), 0.0)
        high = band.astype(BF16)
        low = (band - high.astype(F32)).astype(BF16)
        c = cot[:, lanes]
        adj = mm(high, c) + mm(low, c) + tail[:, h : h + 1] * carry[:, lanes]
        adj_out[:, lanes] = adj
        carry[:, lanes] = keep_first[:, h : h + 1] * adj[0:1, :]
    run[...] += total
    head_out[...] = carry[...]
    dec_out[...] = jnp.exp(run[...])


def value_grad_kernel(heads, channels, adj, tail, mp, decay, adj_in, dv_out):
    rate = mp[...] * decay[...]
    for h in range(heads):
        lanes = slice(h * channels, (h + 1) * channels)
        full = adj[:, lanes] + tail[:, h : h + 1] * adj_in[:, lanes]
        dv_out[:, lanes] = (rate[:, h : h + 1] * full).astype(BF16)


def state_kernel(heads, channels, mp, decay, values, st_out, diff_out, dec_out, decp_out, last_out, carry, run):
    @pl.when(pl.program_id(0) == 0)
    def _():
        carry[...] = jnp.zeros_like(carry)
        run[...] = jnp.zeros_like(run)

    rate = mp[...] * decay[...]
    log_keep, sums, row, col = log_sums(rate)
    sums_t = sums.T
    from_start = jnp.exp(sums)
    before = jnp.exp(run[...])
    dec_out[...] = from_start * before
    decp_out[...] = jnp.exp(sums - log_keep) * before
    top = lax.broadcasted_iota(jnp.int32, (SPAN, channels), 0) == 0
    for h in range(heads):
        lanes = slice(h * channels, (h + 1) * channels)
        gap = sums[:, h : h + 1] - sums_t[h : h + 1, :]
        band = jnp.where(row >= col, jnp.exp(jnp.minimum(gap, 0.0)), 0.0)
        high = band.astype(BF16)
        low = (band - high.astype(F32)).astype(BF16)
        v = values[:, lanes]
        x = rate[:, h : h + 1] * v
        x_high = x.astype(BF16)
        x_low = (x - x_high.astype(F32)).astype(BF16)
        came = carry[:, lanes]
        state = mm(high, x_high) + mm(low, x_high) + mm(high, x_low) + from_start[:, h : h + 1] * came
        st_out[:, lanes] = state
        diff_out[:, lanes] = v - jnp.where(top, came, pltpu.roll(state, 1, 0))
        carry[:, lanes] = state[SPAN - 1 : SPAN, :]
    run[...] += sums[SPAN - 1 : SPAN, :]
    last_out[...] = carry[...]


def finish_kernel(
    heads, channels, st, diff, adj, tail, dec, decp, decay, adj_in, st_in, q, k, iq, ik, cos, marked, opening,
    out, dq_out, dp_out,
):
    d_prob = None
    for h in range(heads):
        lanes = slice(h * channels, (h + 1) * channels)
        one = slice(h, h + 1)
        came = st_in[:, lanes]
        out[:, lanes] = (st[:, lanes] + dec[:, one] * came).astype(BF16)
        full = adj[:, lanes] + tail[:, one] * adj_in[:, lanes]
        part = decay[:, one] * jnp.sum(full * (diff[:, lanes] - decp[:, one] * came), -1, keepdims=True)
        d_prob = part if d_prob is None else d_prob + part
    d_prob = jnp.where(opening[...] > 0, 0.0, marked[...] * d_prob)
    d_cos = -0.5 * d_prob
    a, b, c = iq[...], ik[...], cos[...]
    scale = a * b
    dq_out[...] = (d_cos * (k[...] * scale - (c * a * a) * q[...])).astype(BF16)
    dp_out[...] = (d_cos * (q[...] * scale - (c * b * b) * k[...])).astype(BF16)


def token_grad_kernel(width, place, dq, dk, dv, *refs):
    del place
    qk, up, out = refs
    dims = (((1,), (1,)), ((), ()))
    total = lax.dot_general(dq[...], qk[:, :width], dims, preferred_element_type=F32)
    total += lax.dot_general(dk[...], qk[:, width:], dims, preferred_element_type=F32)
    total += lax.dot_general(dv[...], up[...], dims, preferred_element_type=F32)
    out[...] = total.astype(BF16)


def flipped(x, bit):
    n = lax.axis_size("fsdp")
    return lax.ppermute(x, "fsdp", [(i, i ^ bit) for i in range(n)])


def turned(x, axis, by):
    n = lax.axis_size(axis)
    return lax.ppermute(x, axis, [(i, (i + by) % n) for i in range(n)])


def shifted(x, axis, by):
    n = lax.axis_size(axis)
    return lax.ppermute(x, axis, [(i, i + by) for i in range(n) if 0 <= i + by < n])


def spread_sum(x, axis):
    n = lax.axis_size(axis)
    me = lax.axis_index(axis)
    k, rows, cols = x.shape
    cut = x.reshape(k, n, rows // n, cols)

    def block(i):
        return lax.dynamic_index_in_dim(cut, i, 1, False)

    total = block(me)
    for d in range(1, n):
        total = total + turned(block(lax.rem(me + d, n)).astype(BF16), axis, d).astype(F32)
    return total


def collect(x, axis):
    n = lax.axis_size(axis)
    me = lax.axis_index(axis)
    got = [x] + [turned(x, axis, n - e) for e in range(1, n)]
    twice = jnp.concatenate(got + got[:-1], 0)
    rows = x.shape[0]
    return lax.dynamic_slice_in_dim(twice, lax.rem(n - me, n) * rows, n * rows, 0)


def halve(x, bit):
    half = x.shape[0] // 2
    return x[:half] + flipped(x[half:].astype(BF16), bit).astype(F32)


def reduce_rows(left, right, bits, parts, ctx_first):
    depth = right.shape[0] * 2 // parts
    x = left + flipped(right, bits[0]).astype(F32)
    x = x.reshape(parts // 2, depth, x.shape[1])
    if ctx_first:
        x = spread_sum(x, "ctx")
    for bit in bits[1:]:
        x = halve(x, bit)
    if not ctx_first:
        x = spread_sum(x, "ctx")
    x = spread_sum(x, "dp")[0].astype(BF16)
    return collect(collect(x, "dp"), "ctx").astype(F32)


def per_device(tokens, bounds, decay_rates, w_query, w_key, w_up, grad_out):
    batch_local, length, width = tokens.shape
    hidden = w_up.shape[1]
    heads = decay_rates.shape[0]
    channels = hidden // heads
    blocks = length // SPAN
    parts = lax.axis_size("fsdp")
    count = lax.axis_size("ctx")
    me = lax.axis_index("fsdp")
    depth = width // parts
    levels = parts.bit_length() - 1
    bits = [1 << s for s in range(levels)]
    order = [sum(((p >> s) & 1) << (levels - 1 - s) for s in range(levels)) for p in range(parts)]

    held = {0: jnp.concatenate([w_query, w_key], 1)}
    held_up = {0: w_up}
    for store in (held, held_up):
        for j in sorted(range(1, parts), key=lambda j: (bin(j).count("1"), -j)):
            bit = j & -j
            store[j] = flipped(store[j ^ bit], bit)
    qk_shards = [held[j] for j in order]
    up_shards = [held_up[j] for j in order]

    tok = tokens.reshape(length, width)
    before = shifted(tok[-1:], "ctx", 1)
    tok_prev = jnp.concatenate([before, tok[:-1]], 0)

    def ordered(x):
        cols = [lax.dynamic_slice_in_dim(x, (me ^ j) * depth, depth, 1) for j in order]
        return jnp.concatenate(cols, 1)

    tok, tok_prev = ordered(tok), ordered(tok_prev)
    tok_t, prev_t = lax.optimization_barrier((tok.T, tok_prev.T))
    first = lax.axis_index("ctx") == 0
    opening_flag = jnp.logical_and(first, jnp.arange(length) == 0)
    marked = jnp.where(opening_flag, 1.0, bounds.reshape(length).astype(F32))[:, None]
    opening = opening_flag.astype(F32)[:, None]
    decay = decay_rates[None, :]
    cot = grad_out.reshape(length, hidden)

    shape = jax.ShapeDtypeStruct
    column = shape((length, 1), F32)
    tile = min(256, length)
    q, k, iq, ik, cosine, mp = call(
        functools.partial(route_kernel, parts, width),
        (length // tile,),
        [rows_of(tile, width)] * 2 + [rows_of(tile, 1)] * 2 + [whole((depth, 2 * width))] * parts,
        [rows_of(tile, width)] * 2 + [rows_of(tile, 1)] * 4,
        [shape((length, width), F32)] * 2 + [column] * 4,
        [],
        4 * length * width * width,
        4 * width * width + 12 * length * width,
        "route",
    )(tok, tok_prev, marked, opening, *qk_shards)

    def back(tile_width):
        return pl.BlockSpec((SPAN, tile_width), lambda i: (blocks - 1 - i, 0))

    by_head = shape((length, heads), F32)
    scratch = [pltpu.VMEM((1, hidden), F32), pltpu.VMEM((1, heads), F32)]
    adj, tail, head_row, device_decay = call(
        functools.partial(adjoint_kernel, heads, channels),
        (blocks,),
        [back(1), whole((1, heads)), back(hidden)],
        [back(hidden), back(heads), whole((1, hidden)), whole((1, heads))],
        [shape((length, hidden), F32), by_head, shape((1, hidden), F32), shape((1, heads), F32)],
        scratch,
        8 * length * SPAN * hidden,
        6 * length * hidden,
        "adjoint",
    )(mp, decay, cot)

    def carried(own, by):
        spread = jnp.repeat(device_decay, channels, axis=1)
        came = shifted(own, "ctx", by)
        for _ in range(count - 2):
            came = shifted(spread * came + own, "ctx", by)
        return came

    adj_in = carried(head_row, -1)
    d_values = call(
        functools.partial(value_grad_kernel, heads, channels),
        (blocks,),
        [rows_of(SPAN, hidden), rows_of(SPAN, heads), rows_of(SPAN, 1), whole((1, heads)), whole((1, hidden))],
        rows_of(SPAN, hidden),
        shape((length, hidden), BF16),
        [],
        4 * length * hidden,
        6 * length * hidden,
        "value_grad",
    )(adj, tail, mp, decay, adj_in)

    half_rows = width // 2

    def chain(x_t, d, ctx_first):
        right = mm(x_t[half_rows:], d).astype(BF16)
        left = mm(x_t[:half_rows], d)
        return reduce_rows(left, right, bits, parts, ctx_first)

    cut = hidden // 2
    up_a = chain(tok_t, d_values[:, :cut], False)
    up_b = chain(tok_t, d_values[:, cut:], True)

    up_full = jnp.concatenate(up_shards, 0)
    values = mm(tok, up_full)
    states, diff, dec, decp, last_row = call(
        functools.partial(state_kernel, heads, channels),
        (blocks,),
        [rows_of(SPAN, 1), whole((1, heads)), rows_of(SPAN, hidden)],
        [rows_of(SPAN, hidden)] * 2 + [rows_of(SPAN, heads)] * 2 + [whole((1, hidden))],
        [shape((length, hidden), F32)] * 2 + [by_head] * 2 + [shape((1, hidden), F32)],
        scratch,
        12 * length * SPAN * hidden,
        12 * length * hidden,
        "state",
    )(mp, decay, values)
    st_in = carried(last_row, 1)

    dechunked, d_query, d_prev = call(
        functools.partial(finish_kernel, heads, channels),
        (blocks,),
        [rows_of(SPAN, hidden)] * 3 + [rows_of(SPAN, heads)] * 3 + [whole((1, heads))]
        + [whole((1, hidden))] * 2 + [rows_of(SPAN, width)] * 2 + [rows_of(SPAN, 1)] * 5,
        [rows_of(SPAN, hidden)] + [rows_of(SPAN, width)] * 2,
        [shape((length, hidden), BF16)] + [shape((length, width), BF16)] * 2,
        [],
        20 * length * hidden,
        20 * length * hidden,
        "finish",
    )(states, diff, adj, tail, dec, decp, decay, adj_in, st_in, q, k, iq, ik, cosine, marked, opening)

    grad_query = chain(tok_t, d_query, False)
    grad_key = chain(prev_t, d_prev, True)

    after = shifted(d_prev[:1], "ctx", -1)
    d_key = jnp.concatenate([d_prev[1:], after], 0)
    qk_full = jnp.concatenate(qk_shards, 0)
    place = jnp.stack([me ^ j for j in order]).astype(jnp.int32)
    grad_tokens = pl.pallas_call(
        functools.partial(token_grad_kernel, width),
        grid_spec=pltpu.PrefetchScalarGridSpec(
            num_scalar_prefetch=1,
            grid=(parts,),
            in_specs=[
                pl.BlockSpec((length, width), lambda i, s: (0, 0)),
                pl.BlockSpec((length, width), lambda i, s: (0, 0)),
                pl.BlockSpec((length, hidden), lambda i, s: (0, 0)),
                pl.BlockSpec((depth, 2 * width), lambda i, s: (i, 0)),
                pl.BlockSpec((depth, hidden), lambda i, s: (i, 0)),
            ],
            out_specs=pl.BlockSpec((length, depth), lambda i, s: (0, s[i])),
        ),
        out_shape=shape((length, width), BF16),
        name="token_grad",
        compiler_params=pltpu.CompilerParams(vmem_limit_bytes=LIMIT),
        cost_estimate=pl.CostEstimate(
            flops=2 * length * width * (2 * width + hidden),
            bytes_accessed=2 * width * (2 * width + hidden),
            transcendentals=0,
        ),
    )(place, d_query, d_key, d_values, qk_full, up_full)
    return (
        dechunked.reshape(batch_local, length, hidden),
        grad_tokens.reshape(batch_local, length, width),
        grad_query,
        grad_key,
        jnp.concatenate([up_a, up_b], 1),
    )


def solution(mesh):
    return jax.shard_map(
        per_device,
        mesh=mesh,
        in_specs=(
            P(("dp", "fsdp"), "ctx", None),
            P(("dp", "fsdp"), "ctx"),
            P(),
            P("fsdp", None),
            P("fsdp", None),
            P("fsdp", None),
            P(("dp", "fsdp"), "ctx", None),
        ),
        out_specs=(
            P(("dp", "fsdp"), "ctx", None),
            P(("dp", "fsdp"), "ctx", None),
            P("fsdp", None),
            P("fsdp", None),
            P("fsdp", None),
        ),
        check_vma=False,
    )
```

time: 486 us -> 249 us (0.51); the launches traced: 478 us -> 249 us
  waiting for transfers between devices: 299 us -> 83.8 us
  starting transfers between devices: 4.82 us -> 65.5 us
  Pallas kernels: 0 us -> 51.1 us
  matrix products: 50.4 us -> 12.4 us
  local copies, waits for them, and re-layouts: 51.5 us -> 16.9 us
  other arithmetic: 44.5 us -> 17.5 us
  between operations: 14.8 us -> 1.43 us
  blocking collectives: 12.9 us -> 0 us
    reduce_scatter x1 -> x0, waiting for transfers between devices: 117 us -> none  [per_device(): lax.psum_scatter(grads, ('fsdp', 'ctx'), scatter_dimension=0, tiled=True)]
    all_gather x2 -> x0, waiting for transfers between devices: 93.3 us -> none  [the longest x1 58.5 us: per_device(): full_panels = lax.all_gather(panels, 'fsdp', axis=0, tiled=True)]
    psum x1 -> x0, waiting for transfers between devices: 88.8 us -> none  [per_device(): reduced = lax.psum(reduced, 'dp')]
    ppermute x2 -> x50, waiting for transfers between devices: 0.01 us -> 83.8 us  [the longest x14 45.4 us: flipped(): return lax.ppermute(x, 'fsdp', [(i, i ^ bit) for i in range(n)])]
    ppermute x2 -> x50, starting transfers between devices: 4.66 us -> 65.5 us  [the longest x32 45.1 us: turned(): return lax.ppermute(x, axis, [(i, (i + by) % n) for i in range(n)])]
    pallas_call x0 -> x6, Pallas kernels: none -> 51.1 us  [the longest x1 18.1 us: per_device(): call(functools.partial(finish_kernel, heads, channels), (blocks,), [rows_...]
    dot_general x5 -> x9, matrix products: 50.4 us -> 12.4 us  [mm(): lax.dot_general(a, b, (((1,), (0,)), ((), ())), preferred_element_type=F32)]
    all_gather x3 -> x0, blocking collectives: 12.9 us -> none  [carried_in(): gathered = jax.tree.map(lambda a: lax.all_gather(a, axis), part)]
  transfers between devices with their start and end apart: 6 -> 50, of which waited for: 4 -> 14; matrix products, arithmetic and copies ran while one was open for 10% -> 15% of each run, Pallas kernels for 0% -> 5%
where the time goes in v1:
time: 249 us
  waiting for transfers between devices  83.8 us (34%)
  starting transfers between devices  65.5 us (26%)
  Pallas kernels  51.1 us (21%)
  other arithmetic  17.5 us (7%)
  local copies, waits for them, and re-layouts  16.9 us (7%)
  matrix products  12.4 us (5%)
    ppermute x14, waiting for transfers between devices, flipped(): return lax.ppermute(x, 'fsdp', [(i, i ^ bit) for i in range(n)])  45.4 us
    ppermute x32, starting transfers between devices, turned(): return lax.ppermute(x, axis, [(i, (i + by) % n) for i in range(n)])  45.1 us
    ppermute x32, waiting for transfers between devices, turned(): return lax.ppermute(x, axis, [(i, (i + by) % n) for i in range(n)])  38.5 us
    pallas_call x1, Pallas kernels, per_device(): call(functools.partial(finish_kernel, heads, channels), (blocks,), [rows_...  18.1 us
    dot_general x9, matrix products, mm(): lax.dot_general(a, b, (((1,), (0,)), ((), ())), preferred_element_type=F32)  12.4 us
    ppermute x4, starting transfers between devices, shifted(): lax.ppermute(x, axis, [(i, i + by) for i in range(n) if 0 <= i + by < n])  11.2 us
    unnamed x48, local copies, waits for them, and re-layouts  9.61 us
    ppermute x14, starting transfers between devices, flipped(): return lax.ppermute(x, 'fsdp', [(i, i ^ bit) for i in range(n)])  9.19 us
  transfers between devices with their start and end apart: 50, of which 14 were waited for; matrix products, arithmetic and copies ran while one was open for 15% of the time, Pallas kernels for 5%

profile of v1, /device:TPU:0, one launch (start us, length us, event | category | flops | bytes accessed | tf_op | source)
XLA Modules:
  0.0 248.6 jit_solution(17099941006998449980)
XLA Ops:
  0.7 1.2 constant_dynamic-update-slice_fusion.1
  1.8 1.1 constant_dynamic-update-slice_fusion.refs_4_
  2.9 3.0 %collective-permute-start.1 = (bf16[256,2048]{1,0:T(8,128)(2,1)S(1)}, bf16[256,2048]{1,0:T(8,128)(2,1)S(1)}, u32[]{:S(2)}, u32[]{:S(2)}) collective-permute-start(bf16[256,2048]{1,0:T(8,128)(2,1)S(1)} %constant_dynamic-update-slice_fusion.refs_4_), channel_id=1, source_target_pairs={{0,4},{2,6},{4,0},{6,2},{1,5},{3,7},{5,1},{7,3},{8,12},{10,14},{12... | collective-permute-start | bytes 3145736 | tf_op jit(solution)/shard_map/ppermute | solution.py:178
  6.4 3.7 %collective-permute-start = (bf16[1,1024]{1,0:T(2,128)(2,1)S(1)}, bf16[1,1024]{1,0:T(2,128)(2,1)S(1)}, u32[]{:S(2)}, u32[]{:S(2)}) collective-permute-start(bf16[1,1024]{1,0:T(2,128)(2,1)S(1)} %slice_bitcast_fusion.3), channel_id=1, source_target_pairs={{0,1},{2,3},{4,5},{6,7},{8,9},{10,11},{12,13},{14,15},{16,17},{18,... | collective-permute-start | bytes 6152 | tf_op jit(solution)/shard_map/ppermute | solution.py:188
  11.1 1.0 slice_bitcast_fusion.2
  12.6 1.1 constant_dynamic-update-slice_fusion.5
  13.7 37.9 %collective-permute-done.4 = bf16[256,2048]{1,0:T(8,128)(2,1)} collective-permute-done((bf16[256,2048]{1,0:T(8,128)(2,1)}, bf16[256,2048]{1,0:T(8,128)(2,1)}, u32[]{:S(2)}, u32[]{:S(2)}) %collective-permute-start.4) | collective-permute-done | bytes 1048608 | tf_op jit(solution)/shard_map/ppermute | solution.py:178
  51.7 2.0 dynamic-slice_bitcast_fusion.3
  53.7 1.9 fusion.31
  56.7 1.1 copy-done.9
  57.9 1.3 constant_dynamic-update-slice_fusion.4
  59.2 1.3 constant_dynamic-update-slice_fusion.3
  60.5 1.3 constant_dynamic-update-slice_fusion.2.refs_1_
  61.9 4.4 %fusion.67.values = f32[512,2048]{1,0:T(8,128)} fusion(bf16[1024,2048]{1,0:T(8,128)(2,1)S(1)} %constant_dynamic-update-slice_fusion.2.refs_1_, bf16[512,256]{1,0:T(8,128)(2,1)S(1)} %get-tuple-element.60, bf16[512,256]{1,0:T(8,128)(2,1)S(1)} %get-tuple-element.61, bf16[512,256]{1,0:T(8,128)(2,1)S(1)} %copy-done.4, bf16[512,256]{1,0:T(8,128)(2,1)S(1)} %get-tuple-element.59), kind=kOutput, calls=%fused_computation.179 | convolution fusion | flops 2151677952 | bytes 9437184 | tf_op jit(solution)/shard_map/dot_general | solution.py:40
  66.3 1.0 copy-done.7
  67.3 5.4 %route.1 = (f32[512,1024]{1,0:T(8,128)}, f32[512,1024]{1,0:T(8,128)}, f32[512,1]{1,0:T(8,128)S(1)}, f32[512,1]{1,0:T(8,128)S(1)}, f32[512,1]{1,0:T(8,128)S(1)}, /*index=5*/f32[512,1]{1,0:T(8,128)S(1)}) custom-call(bf16[512,1024]{1,0:T(8,128)(2,1)S(1)} %get-tuple-element.75.refs_0_, bf16[512,1024]{1,0:T(8,128)(2,1)S(1)} %get-tuple-element.56.refs_1_, ...), custom_call_target="tpu_custom_call" | custom-call | flops 2147483648 | bytes 10485760 | tf_op jit(solution)/shard_map/route/pallas_call | solution.py:277
  72.7 8.6 %state.1 = (f32[512,2048]{1,0:T(8,128)S(1)}, f32[512,2048]{1,0:T(8,128)}, f32[512,16]{1,0:T(8,128)S(1)}, f32[512,16]{1,0:T(8,128)S(1)}, f32[1,2048]{1,0:T(1,128)S(1)}) custom-call(f32[512,1]{1,0:T(8,128)S(1)} %get-tuple-element.24.mp, f32[1,16]{1,0:T(1,128)S(1)} %bitcast.147, f32[512,2048]{1,0:T(8,128)} %fusion.67.values), custom_call_target="tpu_custom_call" | custom-call | flops 1610612736 | bytes 12582912 | tf_op jit(solution)/shard_map/state/pallas_call | solution.py:339
  81.3 1.9 copy-done
  83.3 5.9 %adjoint.1 = (f32[512,2048]{1,0:T(8,128)}, f32[512,16]{1,0:T(8,128)S(1)}, f32[1,2048]{1,0:T(1,128)S(1)}, f32[1,16]{1,0:T(1,128)}) custom-call(f32[512,1]{1,0:T(8,128)S(1)} %get-tuple-element.24.mp, f32[1,16]{1,0:T(1,128)S(1)} %bitcast.148, bf16[512,2048]{1,0:T(8,128)(2,1)S(1)} %bitcast.151), custom_call_target="tpu_custom_call" | custom-call | flops 1073741824 | bytes 6291456 | tf_op jit(solution)/shard_map/adjoint/pallas_call | solution.py:294
  89.2 1.3 collective-permute-start.7
  90.5 4.7 %collective-permute-start.8 = (f32[1,2048]{1,0:T(1,128)S(1)}, f32[1,2048]{1,0:T(1,128)S(1)}, u32[]{:S(2)}, u32[]{:S(2)}) collective-permute-start(f32[1,2048]{1,0:T(1,128)S(1)} %get-tuple-element.32), channel_id=1, source_target_pairs={{0,1},{2,3},{4,5},{6,7},{8,9},{10,11},{12,13},{14,15},{16,17},{18,... | collective-permute-start | bytes 24584 | tf_op jit(solution)/shard_map/ppermute | solution.py:188
  95.2 7.7 %pad_maximum_fusion.refs_0_ = bf16[1024,2048]{1,0:T(8,128)(2,1)} fusion(bf16[256,2048]{1,0:T(8,128)(2,1)S(1)} %copy-done.8, bf16[256,2048]{1,0:T(8,128)(2,1)} %collective-permute-done.2.refs_6_, bf16[256,2048]{1,0:T(8,128)(2,1)S(1)} %collective-permute-done.1.refs_5_, bf16[256,2048]{1,0:T(8,128)(2,1)S(1)} %constant_dynamic-update-slice_fusion.refs_4_), kind=kLoop, calls=%fused_computation | loop fusion | flops 16777216 | bytes 8388608 | tf_op jit(solution)/shard_map/concatenate | solution.py:370
  102.9 18.1 %finish.1 = (bf16[512,2048]{1,0:T(8,128)(2,1)}, bf16[512,1024]{1,0:T(8,128)(2,1)S(1)}, bf16[512,1024]{1,0:T(8,128)(2,1)S(1)}) custom-call(f32[512,2048]{1,0:T(8,128)} %copy-done, f32[512,2048]{1,0:T(8,128)} %get-tuple-element.26.diff, f32[512,2048]{1,0:T(8,128)} %get-tuple-element.27.adj, f32[512,16]{1,0:T(8,128)S(1)} %get-tuple-element.28.tail, ...), custom_call_target="tpu_custom_call" | custom-call | flops 20971520 | bytes 20971520 | tf_op jit(solution)/shard_map/finish/pallas_call | solution.py:352
  121.0 1.5 collective-permute-start.9
  123.4 4.6 %value_grad.1.dv = bf16[512,2048]{1,0:T(8,128)(2,1)S(1)} custom-call(f32[512,2048]{1,0:T(8,128)} %get-tuple-element.27.adj, f32[512,16]{1,0:T(8,128)S(1)} %get-tuple-element.28.tail, f32[512,1]{1,0:T(8,128)S(1)} %get-tuple-element.24.mp, f32[1,16]{1,0:T(1,128)S(1)} %bitcast.150, f32[1,2048]{1,0:T(1,128)S(1)} %collective-permute-done.7.adj_in), custom_call_target="tpu_custom_call" | custom-call | flops 4194304 | bytes 6291456 | tf_op jit(solution)/shard_map/value_grad/pallas_call | solution.py:314
  128.0 1.7 convolution_convert_fusion
  130.5 1.7 convolution_convert_fusion.2
  133.7 8.5 %token_grad.1 = bf16[512,1024]{1,0:T(8,128)(2,1)} custom-call(s32[4]{0:T(128)S(1)} %pad_add_fusion.place, bf16[512,1024]{1,0:T(8,128)(2,1)S(1)} %get-tuple-element.39.dq, bf16[512,1024]{1,0:T(8,128)(2,1)S(1)} %pad_maximum_fusion.3.dk, bf16[512,2048]{1,0:T(8,128)(2,1)S(1)} %value_grad.1.dv, bf16[1024,2048]{1,0:T(8,128)(2,1)} %pad_maximum_fusion.refs_0_, ...), custom_call_target="tpu_custom_call" | custom-call | flops 4294967296 | bytes 8388608 | tf_op jit(solution)/shard_map/token_grad/pallas_call | solution.py:372
  143.0 1.8 collective-permute-start.11
  145.6 2.7 %collective-permute-start.21 = (bf16[2,128,1024]{2,1,0:T(8,128)(2,1)S(1)}, bf16[2,128,1024]{2,1,0:T(8,128)(2,1)S(1)}, u32[]{:S(2)}, u32[]{:S(2)}) collective-permute-start(bf16[2,128,1024]{2,1,0:T(8,128)(2,1)S(1)} %fusion.16), channel_id=1, source_target_pairs={{0,1},{1,0},{2,3},{3,2},{4,5},{5,4},{6,7},{7,6},{8,9},{9,8},{10,11... | collective-permute-start | bytes 1572872 | tf_op jit(solution)/shard_map/ppermute | solution.py:183
  150.4 7.4 %collective-permute-done.11 = bf16[1,256,1024]{2,1,0:T(8,128)(2,1)S(1)} collective-permute-done((bf16[1,256,1024]{2,1,0:T(8,128)(2,1)S(1)}, bf16[1,256,1024]{2,1,0:T(8,128)(2,1)S(1)}, u32[]{:S(2)}, u32[]{:S(2)}) %collective-permute-start.11) | collective-permute-done | bytes 524320 | tf_op jit(solution)/shard_map/ppermute | solution.py:178
  158.0 2.7 %collective-permute-start.12 = (bf16[1,128,1024]{2,1,0:T(8,128)(2,1)S(1)}, bf16[1,128,1024]{2,1,0:T(8,128)(2,1)S(1)}, u32[]{:S(2)}, u32[]{:S(2)}) collective-permute-start(bf16[1,128,1024]{2,1,0:T(8,128)(2,1)S(1)} %fusion.28), channel_id=1, source_target_pairs={{0,1},{1,0},{2,3},{3,2},{4,5},{5,4},{6,7},{7,6},{8,9},{9,8},{10,11... | collective-permute-start | bytes 786440 | tf_op jit(solution)/shard_map/ppermute | solution.py:183
  161.2 1.4 collective-permute-start.22
  162.7 9.6 %collective-permute-done.41 = bf16[2,128,1024]{2,1,0:T(8,128)(2,1)S(1)} collective-permute-done((bf16[2,128,1024]{2,1,0:T(8,128)(2,1)S(1)}, bf16[2,128,1024]{2,1,0:T(8,128)(2,1)S(1)}, u32[]{:S(2)}, u32[]{:S(2)}) %collective-permute-start.41) | collective-permute-done | bytes 524320 | tf_op jit(solution)/shard_map/ppermute | solution.py:183
  173.1 2.1 collective-permute-start.32
  175.2 2.7 %collective-permute-done.12 = bf16[1,128,1024]{2,1,0:T(8,128)(2,1)S(1)} collective-permute-done((bf16[1,128,1024]{2,1,0:T(8,128)(2,1)S(1)}, bf16[1,128,1024]{2,1,0:T(8,128)(2,1)S(1)}, u32[]{:S(2)}, u32[]{:S(2)}) %collective-permute-start.12) | collective-permute-done | bytes 262176 | tf_op jit(solution)/shard_map/ppermute | solution.py:183
  178.0 3.7 %collective-permute-start.15 = (bf16[1,32,1024]{2,1,0:T(8,128)(2,1)S(1)}, bf16[1,32,1024]{2,1,0:T(8,128)(2,1)S(1)}, u32[]{:S(2)}, u32[]{:S(2)}) collective-permute-start(bf16[1,32,1024]{2,1,0:T(8,128)(2,1)S(1)} %get-tuple-element.73), channel_id=1, source_target_pairs={{0,24},{8,0},{16,8},{24,16},{1,25},{9,1},{17,9},{25,17},{2,26},{10... | collective-permute-start | bytes 196616 | tf_op jit(solution)/shard_map/ppermute | solution.py:183
  181.7 1.0 collective-permute-start.13
  182.8 2.9 %collective-permute-start.25 = (bf16[1,32,1024]{2,1,0:T(8,128)(2,1)S(1)}, bf16[1,32,1024]{2,1,0:T(8,128)(2,1)S(1)}, u32[]{:S(2)}, u32[]{:S(2)}) collective-permute-start(bf16[1,32,1024]{2,1,0:T(8,128)(2,1)S(1)} %get-tuple-element.70), channel_id=1, source_target_pairs={{0,24},{8,0},{16,8},{24,16},{1,25},{9,1},{17,9},{25,17},{2,26},{10... | collective-permute-start | bytes 196616 | tf_op jit(solution)/shard_map/ppermute | solution.py:183
  185.8 1.2 collective-permute-start.24
  187.2 2.8 %collective-permute-done.14 = bf16[1,32,1024]{2,1,0:T(8,128)(2,1)S(1)} collective-permute-done((bf16[1,32,1024]{2,1,0:T(8,128)(2,1)S(1)}, bf16[1,32,1024]{2,1,0:T(8,128)(2,1)S(1)}, u32[]{:S(2)}, u32[]{:S(2)}) %collective-permute-start.14) | collective-permute-done | bytes 65568 | tf_op jit(solution)/shard_map/ppermute | solution.py:183
  190.0 1.0 collective-permute-start.45
  191.5 3.0 %collective-permute-start.43 = (bf16[1,32,1024]{2,1,0:T(8,128)(2,1)S(1)}, bf16[1,32,1024]{2,1,0:T(8,128)(2,1)S(1)}, u32[]{:S(2)}, u32[]{:S(2)}) collective-permute-start(bf16[1,32,1024]{2,1,0:T(8,128)(2,1)S(1)} %get-tuple-element.66), channel_id=1, source_target_pairs={{0,8},{8,16},{16,24},{24,0},{1,9},{9,17},{17,25},{25,1},{2,10},{10... | collective-permute-start | bytes 196616 | tf_op jit(solution)/shard_map/ppermute | solution.py:183
  194.5 0.9 collective-permute-done.24
  195.8 2.6 %collective-permute-start.34 = (bf16[1,32,1024]{2,1,0:T(8,128)(2,1)S(1)}, bf16[1,32,1024]{2,1,0:T(8,128)(2,1)S(1)}, u32[]{:S(2)}, u32[]{:S(2)}) collective-permute-start(bf16[1,32,1024]{2,1,0:T(8,128)(2,1)S(1)} %get-tuple-element.65), channel_id=1, source_target_pairs={{0,16},{8,24},{16,0},{24,8},{1,17},{9,25},{17,1},{25,9},{2,18},{10... | collective-permute-start | bytes 196616 | tf_op jit(solution)/shard_map/ppermute | solution.py:183
  199.4 1.6 collective-permute-done.44
  201.0 1.4 collective-permute-start.16
  202.4 2.1 collective-permute-start.17
  204.6 2.0 collective-permute-done.34
  206.6 1.8 collective-permute-start.26
  209.0 0.9 collective-permute-start.28
  209.9 2.3 collective-permute-done.17
  213.0 2.6 %collective-permute-start.47 = (bf16[32,1024]{1,0:T(8,128)(2,1)S(1)}, bf16[32,1024]{1,0:T(8,128)(2,1)S(1)}, u32[]{:S(2)}, u32[]{:S(2)}) collective-permute-start(bf16[32,1024]{1,0:T(8,128)(2,1)S(1)} %get-tuple-element.46), channel_id=1, source_target_pairs={{0,16},{8,24},{16,0},{24,8},{1,17},{9,25},{17,1},{25,9},{2,18},{10... | collective-permute-start | bytes 196616 | tf_op jit(solution)/shard_map/ppermute | solution.py:183
  216.4 1.5 collective-permute-done.27
  217.9 1.7 collective-permute-start.36
  219.9 1.4 collective-permute-start.38
  221.2 2.3 collective-permute-done.47
  223.5 2.4 collective-permute-start.19
  226.1 2.1 collective-permute-start.49
  228.3 1.7 collective-permute-start.39
  230.0 11.9 %collective-permute-done.49 = bf16[128,1024]{1,0:T(8,128)(2,1)S(1)} collective-permute-done((bf16[128,1024]{1,0:T(8,128)(2,1)S(1)}, bf16[128,1024]{1,0:T(8,128)(2,1)S(1)}, u32[]{:S(2)}, u32[]{:S(2)}) %collective-permute-start.49) | collective-permute-done | bytes 262176 | tf_op jit(solution)/shard_map/ppermute | solution.py:183
  242.6 1.6 fusion.15
  245.4 1.6 maximum_convert_fusion
  247.0 1.6 fusion.12
  (152 shorter events, 18.1 us)
Async XLA Ops:
  0.6 5.8 %copy-start.3 = (bf16[1,512,1024]{2,1,0:T(8,128)(2,1)S(1)}, bf16[1,512,1024]{2,1,0:T(8,128)(2,1)}, u32[]{:S(2)}) copy-start(bf16[1,512,1024]{2,1,0:T(8,128)(2,1)} %param.7) | copy-start | bytes 3145732
  0.6 9.5 %copy-start.11 = (s32[1,512]{1,0:T(1,128)S(1)}, s32[1,512]{1,0:T(1,128)}, u32[]{:S(2)}) copy-start(s32[1,512]{1,0:T(1,128)} %param.8) | copy-start | bytes 6148
  2.9 53.2 %collective-permute-start.1 = (bf16[256,2048]{1,0:T(8,128)(2,1)S(1)}, bf16[256,2048]{1,0:T(8,128)(2,1)S(1)}, u32[]{:S(2)}, u32[]{:S(2)}) collective-permute-start(bf16[256,2048]{1,0:T(8,128)(2,1)S(1)} %constant_dynamic-update-slice_fusion.refs_4_), channel_id=1, source_target_pairs={{0,4},{2,6},{4,0},{6,2},{1,5},{3,7},{5,1},{7,3},{8,12},{10,14},{12... | collective-permute-start | bytes 3145736 | tf_op jit(solution)/shard_map/ppermute | solution.py:178
  5.9 60.4 %collective-permute-start.2 = (bf16[256,2048]{1,0:T(8,128)(2,1)S(1)}, bf16[256,2048]{1,0:T(8,128)(2,1)}, u32[]{:S(2)}, u32[]{:S(2)}) collective-permute-start(bf16[256,2048]{1,0:T(8,128)(2,1)S(1)} %constant_dynamic-update-slice_fusion.refs_4_), channel_id=1, source_target_pairs={{0,2},{2,0},{4,6},{6,4},{1,3},{3,1},{5,7},{7,5},{8,10},{10,8},{12,... | collective-permute-start | bytes 3145736 | tf_op jit(solution)/shard_map/ppermute | solution.py:178
  5.9 45.7 %collective-permute-start.4 = (bf16[256,2048]{1,0:T(8,128)(2,1)}, bf16[256,2048]{1,0:T(8,128)(2,1)}, u32[]{:S(2)}, u32[]{:S(2)}) collective-permute-start(bf16[256,2048]{1,0:T(8,128)(2,1)} %param.12), channel_id=1, source_target_pairs={{0,4},{2,6},{4,0},{6,2},{1,5},{3,7},{5,1},{7,3},{8,12},{10,14},{12... | collective-permute-start | bytes 3145736 | tf_op jit(solution)/shard_map/ppermute | solution.py:178
  6.1 53.1 %collective-permute-start.5 = (bf16[256,2048]{1,0:T(8,128)(2,1)}, bf16[256,2048]{1,0:T(8,128)(2,1)}, u32[]{:S(2)}, u32[]{:S(2)}) collective-permute-start(bf16[256,2048]{1,0:T(8,128)(2,1)} %param.12), channel_id=1, source_target_pairs={{0,2},{2,0},{4,6},{6,4},{1,3},{3,1},{5,7},{7,5},{8,10},{10,8},{12,... | collective-permute-start | bytes 3145736 | tf_op jit(solution)/shard_map/ppermute | solution.py:178
  6.4 47.3 %collective-permute-start = (bf16[1,1024]{1,0:T(2,128)(2,1)S(1)}, bf16[1,1024]{1,0:T(2,128)(2,1)S(1)}, u32[]{:S(2)}, u32[]{:S(2)}) collective-permute-start(bf16[1,1024]{1,0:T(2,128)(2,1)S(1)} %slice_bitcast_fusion.3), channel_id=1, source_target_pairs={{0,1},{2,3},{4,5},{6,7},{8,9},{10,11},{12,13},{14,15},{16,17},{18,... | collective-permute-start | bytes 6152 | tf_op jit(solution)/shard_map/ppermute | solution.py:188
  11.0 1.6 copy-start.6
  11.0 2.7 %copy-start.5 = (f32[512,1]{1,0:T(8,128)S(1)}, f32[512,1]{1,0:T(8,128)}, u32[]{:S(2)}) copy-start(f32[512,1]{1,0:T(8,128)} %copy.12) | copy-start | bytes 6148
  51.6 8.9 %collective-permute-start.6 = (bf16[256,2048]{1,0:T(8,128)(2,1)}, bf16[256,2048]{1,0:T(8,128)(2,1)}, u32[]{:S(2)}, u32[]{:S(2)}) collective-permute-start(bf16[256,2048]{1,0:T(8,128)(2,1)} %collective-permute-done.4), channel_id=1, source_target_pairs={{0,2},{2,0},{4,6},{6,4},{1,3},{3,1},{5,7},{7,5},{8,10},{10,8},{12,... | collective-permute-start | bytes 3145736 | tf_op jit(solution)/shard_map/ppermute | solution.py:178
  53.7 2.0 copy-start.4
  55.7 2.2 copy-start.9
  56.2 10.2 %collective-permute-start.3 = (bf16[256,2048]{1,0:T(8,128)(2,1)S(1)}, bf16[256,2048]{1,0:T(8,128)(2,1)S(1)}, u32[]{:S(2)}, u32[]{:S(2)}) collective-permute-start(bf16[256,2048]{1,0:T(8,128)(2,1)S(1)} %collective-permute-done.1.refs_5_), channel_id=1, source_target_pairs={{0,2},{2,0},{4,6},{6,4},{1,3},{3,1},{5,7},{7,5},{8,10},{10,8},{12,... | collective-permute-start | bytes 3145736 | tf_op jit(solution)/shard_map/ppermute | solution.py:178
  61.9 4.5 %copy-start.10 = (bf16[1024,2048]{1,0:T(8,128)(2,1)}, bf16[1024,2048]{1,0:T(8,128)(2,1)S(1)}, u32[]{:S(2)}) copy-start(bf16[1024,2048]{1,0:T(8,128)(2,1)S(1)} %constant_dynamic-update-slice_fusion.2.refs_1_) | copy-start | bytes 12582916
  66.3 1.0 copy-start.7
  67.3 5.4 %copy-start.1 = (f32[16]{0:T(128)S(1)}, f32[16]{0:T(128)}, u32[]{:S(2)}) copy-start(f32[16]{0:T(128)} %param.9) | copy-start | bytes 196
  72.7 10.6 %copy-start.2 = (bf16[1,512,2048]{2,1,0:T(8,128)(2,1)S(1)}, bf16[1,512,2048]{2,1,0:T(8,128)(2,1)}, u32[]{:S(2)}) copy-start(bf16[1,512,2048]{2,1,0:T(8,128)(2,1)} %param.13) | copy-start | bytes 6291460
  81.3 2.0 copy-start
  83.3 11.9 %copy-start.8 = (bf16[256,2048]{1,0:T(8,128)(2,1)S(1)}, bf16[256,2048]{1,0:T(8,128)(2,1)}, u32[]{:S(2)}) copy-start(bf16[256,2048]{1,0:T(8,128)(2,1)} %copy-done.7) | copy-start | bytes 3145732
  89.2 13.8 %collective-permute-start.7 = (f32[1,2048]{1,0:T(1,128)S(1)}, f32[1,2048]{1,0:T(1,128)S(1)}, u32[]{:S(2)}, u32[]{:S(2)}) collective-permute-start(f32[1,2048]{1,0:T(1,128)S(1)} %get-tuple-element.31), channel_id=1, source_target_pairs={{1,0},{3,2},{5,4},{7,6},{9,8},{11,10},{13,12},{15,14},{17,16},{19,... | collective-permute-start | bytes 24584 | tf_op jit(solution)/shard_map/ppermute | solution.py:188
  90.5 12.5 %collective-permute-start.8 = (f32[1,2048]{1,0:T(1,128)S(1)}, f32[1,2048]{1,0:T(1,128)S(1)}, u32[]{:S(2)}, u32[]{:S(2)}) collective-permute-start(f32[1,2048]{1,0:T(1,128)S(1)} %get-tuple-element.32), channel_id=1, source_target_pairs={{0,1},{2,3},{4,5},{6,7},{8,9},{10,11},{12,13},{14,15},{16,17},{18,... | collective-permute-start | bytes 24584 | tf_op jit(solution)/shard_map/ppermute | solution.py:188
  121.0 12.6 %collective-permute-start.9 = (bf16[1,1024]{1,0:T(2,128)(2,1)S(1)}, bf16[1,1024]{1,0:T(2,128)(2,1)S(1)}, u32[]{:S(2)}, u32[]{:S(2)}) collective-permute-start(bf16[1,1024]{1,0:T(2,128)(2,1)S(1)} %slice.81), channel_id=1, source_target_pairs={{1,0},{3,2},{5,4},{7,6},{9,8},{11,10},{13,12},{15,14},{17,16},{19,... | collective-permute-start | bytes 6152 | tf_op jit(solution)/shard_map/ppermute | solution.py:188
  123.3 18.9 %collective-permute-start.10 = (bf16[512,1024]{1,0:T(8,128)(2,1)S(1)}, bf16[512,1024]{1,0:T(8,128)(2,1)S(1)}, u32[]{:S(2)}, u32[]{:S(2)}) collective-permute-start(bf16[512,1024]{1,0:T(8,128)(2,1)S(1)} %convolution_convert_fusion.3), channel_id=1, source_target_pairs={{0,2},{2,0},{4,6},{6,4},{1,3},{3,1},{5,7},{7,5},{8,10},{10,8},{12,... | collective-permute-start | bytes 3145736 | tf_op jit(solution)/shard_map/ppermute | solution.py:178
  132.5 12.3 %collective-permute-start.20 = (bf16[512,1024]{1,0:T(8,128)(2,1)}, bf16[512,1024]{1,0:T(8,128)(2,1)S(1)}, u32[]{:S(2)}, u32[]{:S(2)}) collective-permute-start(bf16[512,1024]{1,0:T(8,128)(2,1)} %convolution_convert_fusion.2), channel_id=1, source_target_pairs={{0,2},{2,0},{4,6},{6,4},{1,3},{3,1},{5,7},{7,5},{8,10},{10,8},{12,... | collective-permute-start | bytes 3145736 | tf_op jit(solution)/shard_map/ppermute | solution.py:178
  133.1 15.2 %collective-permute-start.40 = (bf16[512,1024]{1,0:T(8,128)(2,1)}, bf16[512,1024]{1,0:T(8,128)(2,1)S(1)}, u32[]{:S(2)}, u32[]{:S(2)}) collective-permute-start(bf16[512,1024]{1,0:T(8,128)(2,1)} %convolution_convert_fusion), channel_id=1, source_target_pairs={{0,2},{2,0},{4,6},{6,4},{1,3},{3,1},{5,7},{7,5},{8,10},{10,8},{12,... | collective-permute-start | bytes 3145736 | tf_op jit(solution)/shard_map/ppermute | solution.py:178
  133.1 16.1 %collective-permute-start.30 = (bf16[512,1024]{1,0:T(8,128)(2,1)S(1)}, bf16[512,1024]{1,0:T(8,128)(2,1)S(1)}, u32[]{:S(2)}, u32[]{:S(2)}) collective-permute-start(bf16[512,1024]{1,0:T(8,128)(2,1)S(1)} %convolution_convert_fusion.1), channel_id=1, source_target_pairs={{0,2},{2,0},{4,6},{6,4},{1,3},{3,1},{5,7},{7,5},{8,10},{10,8},{12,... | collective-permute-start | bytes 3145736 | tf_op jit(solution)/shard_map/ppermute | solution.py:178
  143.0 14.8 %collective-permute-start.11 = (bf16[1,256,1024]{2,1,0:T(8,128)(2,1)S(1)}, bf16[1,256,1024]{2,1,0:T(8,128)(2,1)S(1)}, u32[]{:S(2)}, u32[]{:S(2)}) collective-permute-start(bf16[1,256,1024]{2,1,0:T(8,128)(2,1)S(1)} %fusion.18), channel_id=1, source_target_pairs={{0,4},{2,6},{4,0},{6,2},{1,5},{3,7},{5,1},{7,3},{8,12},{10,14},{12... | collective-permute-start | bytes 1572872 | tf_op jit(solution)/shard_map/ppermute | solution.py:178
  145.6 15.5 %collective-permute-start.21 = (bf16[2,128,1024]{2,1,0:T(8,128)(2,1)S(1)}, bf16[2,128,1024]{2,1,0:T(8,128)(2,1)S(1)}, u32[]{:S(2)}, u32[]{:S(2)}) collective-permute-start(bf16[2,128,1024]{2,1,0:T(8,128)(2,1)S(1)} %fusion.16), channel_id=1, source_target_pairs={{0,1},{1,0},{2,3},{3,2},{4,5},{5,4},{6,7},{7,6},{8,9},{9,8},{10,11... | collective-permute-start | bytes 1572872 | tf_op jit(solution)/shard_map/ppermute | solution.py:183
  149.1 23.2 %collective-permute-start.41 = (bf16[2,128,1024]{2,1,0:T(8,128)(2,1)S(1)}, bf16[2,128,1024]{2,1,0:T(8,128)(2,1)S(1)}, u32[]{:S(2)}, u32[]{:S(2)}) collective-permute-start(bf16[2,128,1024]{2,1,0:T(8,128)(2,1)S(1)} %fusion.17), channel_id=1, source_target_pairs={{0,1},{1,0},{2,3},{3,2},{4,5},{5,4},{6,7},{7,6},{8,9},{9,8},{10,11... | collective-permute-start | bytes 1572872 | tf_op jit(solution)/shard_map/ppermute | solution.py:183
  150.0 22.8 %collective-permute-start.31 = (bf16[1,256,1024]{2,1,0:T(8,128)(2,1)S(1)}, bf16[1,256,1024]{2,1,0:T(8,128)(2,1)S(1)}, u32[]{:S(2)}, u32[]{:S(2)}) collective-permute-start(bf16[1,256,1024]{2,1,0:T(8,128)(2,1)S(1)} %fusion.19), channel_id=1, source_target_pairs={{0,4},{2,6},{4,0},{6,2},{1,5},{3,7},{5,1},{7,3},{8,12},{10,14},{12... | collective-permute-start | bytes 1572872 | tf_op jit(solution)/shard_map/ppermute | solution.py:178
  158.0 19.9 %collective-permute-start.12 = (bf16[1,128,1024]{2,1,0:T(8,128)(2,1)S(1)}, bf16[1,128,1024]{2,1,0:T(8,128)(2,1)S(1)}, u32[]{:S(2)}, u32[]{:S(2)}) collective-permute-start(bf16[1,128,1024]{2,1,0:T(8,128)(2,1)S(1)} %fusion.28), channel_id=1, source_target_pairs={{0,1},{1,0},{2,3},{3,2},{4,5},{5,4},{6,7},{7,6},{8,9},{9,8},{10,11... | collective-permute-start | bytes 786440 | tf_op jit(solution)/shard_map/ppermute | solution.py:183
  161.2 20.5 %collective-permute-start.22 = (bf16[1,128,1024]{2,1,0:T(8,128)(2,1)S(1)}, bf16[1,128,1024]{2,1,0:T(8,128)(2,1)S(1)}, u32[]{:S(2)}, u32[]{:S(2)}) collective-permute-start(bf16[1,128,1024]{2,1,0:T(8,128)(2,1)S(1)} %slice.151), channel_id=1, source_target_pairs={{0,4},{2,6},{4,0},{6,2},{1,5},{3,7},{5,1},{7,3},{8,12},{10,14},{12... | collective-permute-start | bytes 786440 | tf_op jit(solution)/shard_map/ppermute | solution.py:178
  172.5 10.3 %collective-permute-start.42 = (bf16[1,128,1024]{2,1,0:T(8,128)(2,1)S(1)}, bf16[1,128,1024]{2,1,0:T(8,128)(2,1)S(1)}, u32[]{:S(2)}, u32[]{:S(2)}) collective-permute-start(bf16[1,128,1024]{2,1,0:T(8,128)(2,1)S(1)} %slice.150), channel_id=1, source_target_pairs={{0,4},{2,6},{4,0},{6,2},{1,5},{3,7},{5,1},{7,3},{8,12},{10,14},{12... | collective-permute-start | bytes 786440 | tf_op jit(solution)/shard_map/ppermute | solution.py:178
  173.1 12.7 %collective-permute-start.32 = (bf16[1,128,1024]{2,1,0:T(8,128)(2,1)S(1)}, bf16[1,128,1024]{2,1,0:T(8,128)(2,1)S(1)}, u32[]{:S(2)}, u32[]{:S(2)}) collective-permute-start(bf16[1,128,1024]{2,1,0:T(8,128)(2,1)S(1)} %fusion.29), channel_id=1, source_target_pairs={{0,1},{1,0},{2,3},{3,2},{4,5},{5,4},{6,7},{7,6},{8,9},{9,8},{10,11... | collective-permute-start | bytes 786440 | tf_op jit(solution)/shard_map/ppermute | solution.py:183
  178.0 9.1 %collective-permute-start.15 = (bf16[1,32,1024]{2,1,0:T(8,128)(2,1)S(1)}, bf16[1,32,1024]{2,1,0:T(8,128)(2,1)S(1)}, u32[]{:S(2)}, u32[]{:S(2)}) collective-permute-start(bf16[1,32,1024]{2,1,0:T(8,128)(2,1)S(1)} %get-tuple-element.73), channel_id=1, source_target_pairs={{0,24},{8,0},{16,8},{24,16},{1,25},{9,1},{17,9},{25,17},{2,26},{10... | collective-permute-start | bytes 196616 | tf_op jit(solution)/shard_map/ppermute | solution.py:183
  181.7 8.3 %collective-permute-start.14 = (bf16[1,32,1024]{2,1,0:T(8,128)(2,1)S(1)}, bf16[1,32,1024]{2,1,0:T(8,128)(2,1)S(1)}, u32[]{:S(2)}, u32[]{:S(2)}) collective-permute-start(bf16[1,32,1024]{2,1,0:T(8,128)(2,1)S(1)} %get-tuple-element.74), channel_id=1, source_target_pairs={{0,16},{8,24},{16,0},{24,8},{1,17},{9,25},{17,1},{25,9},{2,18},{10... | collective-permute-start | bytes 196616 | tf_op jit(solution)/shard_map/ppermute | solution.py:183
  181.7 9.3 %collective-permute-start.13 = (bf16[1,32,1024]{2,1,0:T(8,128)(2,1)S(1)}, bf16[1,32,1024]{2,1,0:T(8,128)(2,1)S(1)}, u32[]{:S(2)}, u32[]{:S(2)}) collective-permute-start(bf16[1,32,1024]{2,1,0:T(8,128)(2,1)S(1)} %get-tuple-element.72), channel_id=1, source_target_pairs={{0,8},{8,16},{16,24},{24,0},{1,9},{9,17},{17,25},{25,1},{2,10},{10... | collective-permute-start | bytes 196616 | tf_op jit(solution)/shard_map/ppermute | solution.py:183
  182.8 8.6 %collective-permute-start.25 = (bf16[1,32,1024]{2,1,0:T(8,128)(2,1)S(1)}, bf16[1,32,1024]{2,1,0:T(8,128)(2,1)S(1)}, u32[]{:S(2)}, u32[]{:S(2)}) collective-permute-start(bf16[1,32,1024]{2,1,0:T(8,128)(2,1)S(1)} %get-tuple-element.70), channel_id=1, source_target_pairs={{0,24},{8,0},{16,8},{24,16},{1,25},{9,1},{17,9},{25,17},{2,26},{10... | collective-permute-start | bytes 196616 | tf_op jit(solution)/shard_map/ppermute | solution.py:183
  185.8 9.5 %collective-permute-start.24 = (bf16[1,32,1024]{2,1,0:T(8,128)(2,1)S(1)}, bf16[1,32,1024]{2,1,0:T(8,128)(2,1)S(1)}, u32[]{:S(2)}, u32[]{:S(2)}) collective-permute-start(bf16[1,32,1024]{2,1,0:T(8,128)(2,1)S(1)} %get-tuple-element.71), channel_id=1, source_target_pairs={{0,16},{8,24},{16,0},{24,8},{1,17},{9,25},{17,1},{25,9},{2,18},{10... | collective-permute-start | bytes 196616 | tf_op jit(solution)/shard_map/ppermute | solution.py:183
  187.1 8.7 %collective-permute-start.23 = (bf16[1,32,1024]{2,1,0:T(8,128)(2,1)S(1)}, bf16[1,32,1024]{2,1,0:T(8,128)(2,1)S(1)}, u32[]{:S(2)}, u32[]{:S(2)}) collective-permute-start(bf16[1,32,1024]{2,1,0:T(8,128)(2,1)S(1)} %get-tuple-element.69), channel_id=1, source_target_pairs={{0,8},{8,16},{16,24},{24,0},{1,9},{9,17},{17,25},{25,1},{2,10},{10... | collective-permute-start | bytes 196616 | tf_op jit(solution)/shard_map/ppermute | solution.py:183
  190.0 8.5 %collective-permute-start.45 = (bf16[1,32,1024]{2,1,0:T(8,128)(2,1)S(1)}, bf16[1,32,1024]{2,1,0:T(8,128)(2,1)S(1)}, u32[]{:S(2)}, u32[]{:S(2)}) collective-permute-start(bf16[1,32,1024]{2,1,0:T(8,128)(2,1)S(1)} %get-tuple-element.67), channel_id=1, source_target_pairs={{0,24},{8,0},{16,8},{24,16},{1,25},{9,1},{17,9},{25,17},{2,26},{10... | collective-permute-start | bytes 196616 | tf_op jit(solution)/shard_map/ppermute | solution.py:183
  191.0 10.0 %collective-permute-start.44 = (bf16[1,32,1024]{2,1,0:T(8,128)(2,1)S(1)}, bf16[1,32,1024]{2,1,0:T(8,128)(2,1)S(1)}, u32[]{:S(2)}, u32[]{:S(2)}) collective-permute-start(bf16[1,32,1024]{2,1,0:T(8,128)(2,1)S(1)} %get-tuple-element.68), channel_id=1, source_target_pairs={{0,16},{8,24},{16,0},{24,8},{1,17},{9,25},{17,1},{25,9},{2,18},{10... | collective-permute-start | bytes 196616 | tf_op jit(solution)/shard_map/ppermute | solution.py:183
  191.5 10.9 %collective-permute-start.43 = (bf16[1,32,1024]{2,1,0:T(8,128)(2,1)S(1)}, bf16[1,32,1024]{2,1,0:T(8,128)(2,1)S(1)}, u32[]{:S(2)}, u32[]{:S(2)}) collective-permute-start(bf16[1,32,1024]{2,1,0:T(8,128)(2,1)S(1)} %get-tuple-element.66), channel_id=1, source_target_pairs={{0,8},{8,16},{16,24},{24,0},{1,9},{9,17},{17,25},{25,1},{2,10},{10... | collective-permute-start | bytes 196616 | tf_op jit(solution)/shard_map/ppermute | solution.py:183
  195.4 9.2 %collective-permute-start.35 = (bf16[1,32,1024]{2,1,0:T(8,128)(2,1)S(1)}, bf16[1,32,1024]{2,1,0:T(8,128)(2,1)S(1)}, u32[]{:S(2)}, u32[]{:S(2)}) collective-permute-start(bf16[1,32,1024]{2,1,0:T(8,128)(2,1)S(1)} %get-tuple-element.64), channel_id=1, source_target_pairs={{0,24},{8,0},{16,8},{24,16},{1,25},{9,1},{17,9},{25,17},{2,26},{10... | collective-permute-start | bytes 196616 | tf_op jit(solution)/shard_map/ppermute | solution.py:183
  195.8 10.8 %collective-permute-start.34 = (bf16[1,32,1024]{2,1,0:T(8,128)(2,1)S(1)}, bf16[1,32,1024]{2,1,0:T(8,128)(2,1)S(1)}, u32[]{:S(2)}, u32[]{:S(2)}) collective-permute-start(bf16[1,32,1024]{2,1,0:T(8,128)(2,1)S(1)} %get-tuple-element.65), channel_id=1, source_target_pairs={{0,16},{8,24},{16,0},{24,8},{1,17},{9,25},{17,1},{25,9},{2,18},{10... | collective-permute-start | bytes 196616 | tf_op jit(solution)/shard_map/ppermute | solution.py:183
  198.5 9.9 %collective-permute-start.33 = (bf16[1,32,1024]{2,1,0:T(8,128)(2,1)S(1)}, bf16[1,32,1024]{2,1,0:T(8,128)(2,1)S(1)}, u32[]{:S(2)}, u32[]{:S(2)}) collective-permute-start(bf16[1,32,1024]{2,1,0:T(8,128)(2,1)S(1)} %get-tuple-element.63), channel_id=1, source_target_pairs={{0,8},{8,16},{16,24},{24,0},{1,9},{9,17},{17,25},{25,1},{2,10},{10... | collective-permute-start | bytes 196616 | tf_op jit(solution)/shard_map/ppermute | solution.py:183
  201.0 8.0 %collective-permute-start.16 = (bf16[32,1024]{1,0:T(8,128)(2,1)S(1)}, bf16[32,1024]{1,0:T(8,128)(2,1)S(1)}, u32[]{:S(2)}, u32[]{:S(2)}) collective-permute-start(bf16[32,1024]{1,0:T(8,128)(2,1)S(1)} %get-tuple-element.50), channel_id=1, source_target_pairs={{0,24},{8,0},{16,8},{24,16},{1,25},{9,1},{17,9},{25,17},{2,26},{10... | collective-permute-start | bytes 196616 | tf_op jit(solution)/shard_map/ppermute | solution.py:183
  202.4 9.9 %collective-permute-start.17 = (bf16[32,1024]{1,0:T(8,128)(2,1)S(1)}, bf16[32,1024]{1,0:T(8,128)(2,1)S(1)}, u32[]{:S(2)}, u32[]{:S(2)}) collective-permute-start(bf16[32,1024]{1,0:T(8,128)(2,1)S(1)} %get-tuple-element.50), channel_id=1, source_target_pairs={{0,16},{8,24},{16,0},{24,8},{1,17},{9,25},{17,1},{25,9},{2,18},{10... | collective-permute-start | bytes 196616 | tf_op jit(solution)/shard_map/ppermute | solution.py:183
  204.5 8.5 %collective-permute-start.18 = (bf16[32,1024]{1,0:T(8,128)(2,1)S(1)}, bf16[32,1024]{1,0:T(8,128)(2,1)S(1)}, u32[]{:S(2)}, u32[]{:S(2)}) collective-permute-start(bf16[32,1024]{1,0:T(8,128)(2,1)S(1)} %get-tuple-element.50), channel_id=1, source_target_pairs={{0,8},{8,16},{16,24},{24,0},{1,9},{9,17},{17,25},{25,1},{2,10},{10... | collective-permute-start | bytes 196616 | tf_op jit(solution)/shard_map/ppermute | solution.py:183
  206.6 9.0 %collective-permute-start.26 = (bf16[32,1024]{1,0:T(8,128)(2,1)S(1)}, bf16[32,1024]{1,0:T(8,128)(2,1)S(1)}, u32[]{:S(2)}, u32[]{:S(2)}) collective-permute-start(bf16[32,1024]{1,0:T(8,128)(2,1)S(1)} %get-tuple-element.48), channel_id=1, source_target_pairs={{0,24},{8,0},{16,8},{24,16},{1,25},{9,1},{17,9},{25,17},{2,26},{10... | collective-permute-start | bytes 196616 | tf_op jit(solution)/shard_map/ppermute | solution.py:183
  208.4 9.5 %collective-permute-start.27 = (bf16[32,1024]{1,0:T(8,128)(2,1)S(1)}, bf16[32,1024]{1,0:T(8,128)(2,1)S(1)}, u32[]{:S(2)}, u32[]{:S(2)}) collective-permute-start(bf16[32,1024]{1,0:T(8,128)(2,1)S(1)} %get-tuple-element.48), channel_id=1, source_target_pairs={{0,16},{8,24},{16,0},{24,8},{1,17},{9,25},{17,1},{25,9},{2,18},{10... | collective-permute-start | bytes 196616 | tf_op jit(solution)/shard_map/ppermute | solution.py:183
  209.0 10.6 %collective-permute-start.28 = (bf16[32,1024]{1,0:T(8,128)(2,1)S(1)}, bf16[32,1024]{1,0:T(8,128)(2,1)S(1)}, u32[]{:S(2)}, u32[]{:S(2)}) collective-permute-start(bf16[32,1024]{1,0:T(8,128)(2,1)S(1)} %get-tuple-element.48), channel_id=1, source_target_pairs={{0,8},{8,16},{16,24},{24,0},{1,9},{9,17},{17,25},{25,1},{2,10},{10... | collective-permute-start | bytes 196616 | tf_op jit(solution)/shard_map/ppermute | solution.py:183
  212.3 7.6 %collective-permute-start.46 = (bf16[32,1024]{1,0:T(8,128)(2,1)S(1)}, bf16[32,1024]{1,0:T(8,128)(2,1)S(1)}, u32[]{:S(2)}, u32[]{:S(2)}) collective-permute-start(bf16[32,1024]{1,0:T(8,128)(2,1)S(1)} %get-tuple-element.46), channel_id=1, source_target_pairs={{0,24},{8,0},{16,8},{24,16},{1,25},{9,1},{17,9},{25,17},{2,26},{10... | collective-permute-start | bytes 196616 | tf_op jit(solution)/shard_map/ppermute | solution.py:183
  213.0 10.5 %collective-permute-start.47 = (bf16[32,1024]{1,0:T(8,128)(2,1)S(1)}, bf16[32,1024]{1,0:T(8,128)(2,1)S(1)}, u32[]{:S(2)}, u32[]{:S(2)}) collective-permute-start(bf16[32,1024]{1,0:T(8,128)(2,1)S(1)} %get-tuple-element.46), channel_id=1, source_target_pairs={{0,16},{8,24},{16,0},{24,8},{1,17},{9,25},{17,1},{25,9},{2,18},{10... | collective-permute-start | bytes 196616 | tf_op jit(solution)/shard_map/ppermute | solution.py:183
  215.7 10.3 %collective-permute-start.48 = (bf16[32,1024]{1,0:T(8,128)(2,1)S(1)}, bf16[32,1024]{1,0:T(8,128)(2,1)S(1)}, u32[]{:S(2)}, u32[]{:S(2)}) collective-permute-start(bf16[32,1024]{1,0:T(8,128)(2,1)S(1)} %get-tuple-element.46), channel_id=1, source_target_pairs={{0,8},{8,16},{16,24},{24,0},{1,9},{9,17},{17,25},{25,1},{2,10},{10... | collective-permute-start | bytes 196616 | tf_op jit(solution)/shard_map/ppermute | solution.py:183
  217.9 8.2 %collective-permute-start.36 = (bf16[32,1024]{1,0:T(8,128)(2,1)S(1)}, bf16[32,1024]{1,0:T(8,128)(2,1)S(1)}, u32[]{:S(2)}, u32[]{:S(2)}) collective-permute-start(bf16[32,1024]{1,0:T(8,128)(2,1)S(1)} %get-tuple-element.44), channel_id=1, source_target_pairs={{0,24},{8,0},{16,8},{24,16},{1,25},{9,1},{17,9},{25,17},{2,26},{10... | collective-permute-start | bytes 196616 | tf_op jit(solution)/shard_map/ppermute | solution.py:183
  219.6 8.6 %collective-permute-start.37 = (bf16[32,1024]{1,0:T(8,128)(2,1)S(1)}, bf16[32,1024]{1,0:T(8,128)(2,1)S(1)}, u32[]{:S(2)}, u32[]{:S(2)}) collective-permute-start(bf16[32,1024]{1,0:T(8,128)(2,1)S(1)} %get-tuple-element.44), channel_id=1, source_target_pairs={{0,16},{8,24},{16,0},{24,8},{1,17},{9,25},{17,1},{25,9},{2,18},{10... | collective-permute-start | bytes 196616 | tf_op jit(solution)/shard_map/ppermute | solution.py:183
  219.9 8.3 %collective-permute-start.38 = (bf16[32,1024]{1,0:T(8,128)(2,1)S(1)}, bf16[32,1024]{1,0:T(8,128)(2,1)S(1)}, u32[]{:S(2)}, u32[]{:S(2)}) collective-permute-start(bf16[32,1024]{1,0:T(8,128)(2,1)S(1)} %get-tuple-element.44), channel_id=1, source_target_pairs={{0,8},{8,16},{16,24},{24,0},{1,9},{9,17},{17,25},{25,1},{2,10},{10... | collective-permute-start | bytes 196616 | tf_op jit(solution)/shard_map/ppermute | solution.py:183
  223.5 19.1 %collective-permute-start.19 = (bf16[128,1024]{1,0:T(8,128)(2,1)S(1)}, bf16[128,1024]{1,0:T(8,128)(2,1)S(1)}, u32[]{:S(2)}, u32[]{:S(2)}) collective-permute-start(bf16[128,1024]{1,0:T(8,128)(2,1)S(1)} %constant_dynamic-slice_fusion.3), channel_id=1, source_target_pairs={{0,1},{1,0},{2,3},{3,2},{4,5},{5,4},{6,7},{7,6},{8,9},{9,8},{10,11... | collective-permute-start | bytes 786440 | tf_op jit(solution)/shard_map/ppermute | solution.py:183
  225.9 21.1 %collective-permute-start.29 = (bf16[128,1024]{1,0:T(8,128)(2,1)S(1)}, bf16[128,1024]{1,0:T(8,128)(2,1)S(1)}, u32[]{:S(2)}, u32[]{:S(2)}) collective-permute-start(bf16[128,1024]{1,0:T(8,128)(2,1)S(1)} %constant_dynamic-slice_fusion.2), channel_id=1, source_target_pairs={{0,1},{1,0},{2,3},{3,2},{4,5},{5,4},{6,7},{7,6},{8,9},{9,8},{10,11... | collective-permute-start | bytes 786440 | tf_op jit(solution)/shard_map/ppermute | solution.py:183
  226.1 15.8 %collective-permute-start.49 = (bf16[128,1024]{1,0:T(8,128)(2,1)S(1)}, bf16[128,1024]{1,0:T(8,128)(2,1)S(1)}, u32[]{:S(2)}, u32[]{:S(2)}) collective-permute-start(bf16[128,1024]{1,0:T(8,128)(2,1)S(1)} %constant_dynamic-slice_fusion), channel_id=1, source_target_pairs={{0,1},{1,0},{2,3},{3,2},{4,5},{5,4},{6,7},{7,6},{8,9},{9,8},{10,11... | collective-permute-start | bytes 786440 | tf_op jit(solution)/shard_map/ppermute | solution.py:183
  228.3 16.4 %collective-permute-start.39 = (bf16[128,1024]{1,0:T(8,128)(2,1)S(1)}, bf16[128,1024]{1,0:T(8,128)(2,1)S(1)}, u32[]{:S(2)}, u32[]{:S(2)}) collective-permute-start(bf16[128,1024]{1,0:T(8,128)(2,1)S(1)} %constant_dynamic-slice_fusion.1), channel_id=1, source_target_pairs={{0,1},{1,0},{2,3},{3,2},{4,5},{5,4},{6,7},{7,6},{8,9},{9,8},{10,11... | collective-permute-start | bytes 786440 | tf_op jit(solution)/shard_map/ppermute | solution.py:183

commit v2 on v1

--- a/solution.py
+++ b/solution.py
@@ -71,6 +71,14 @@
     lower = (row >= col).astype(F32)
     sums = jnp.dot(lower, log_keep, precision=lax.Precision.HIGHEST, preferred_element_type=F32)
     return log_keep, sums, row, col
+
+
+def value_kernel(parts, tok, *refs):
+    depth = refs[0].shape[0]
+    total = mm(tok[:, :depth], refs[0][...])
+    for p in range(1, parts):
+        total += mm(tok[:, p * depth : (p + 1) * depth], refs[p][...])
+    refs[parts][...] = total
 
 
 def adjoint_kernel(heads, channels, mp, decay, cot, adj_out, tail_out, head_out, dec_out, carry, run):
@@ -146,15 +154,16 @@
     heads, channels, st, diff, adj, tail, dec, decp, decay, adj_in, st_in, q, k, iq, ik, cos, marked, opening,
     out, dq_out, dp_out,
 ):
-    d_prob = None
+    total = None
     for h in range(heads):
         lanes = slice(h * channels, (h + 1) * channels)
         one = slice(h, h + 1)
         came = st_in[:, lanes]
         out[:, lanes] = (st[:, lanes] + dec[:, one] * came).astype(BF16)
         full = adj[:, lanes] + tail[:, one] * adj_in[:, lanes]
-        part = decay[:, one] * jnp.sum(full * (diff[:, lanes] - decp[:, one] * came), -1, keepdims=True)
-        d_prob = part if d_prob is None else d_prob + part
+        part = decay[:, one] * (full * (diff[:, lanes] - decp[:, one] * came))
+        total = part if total is None else total + part
+    d_prob = jnp.sum(total, -1, keepdims=True)
     d_prob = jnp.where(opening[...] > 0, 0.0, marked[...] * d_prob)
     d_cos = -0.5 * d_prob
     a, b, c = iq[...], ik[...], cos[...]
@@ -163,14 +172,16 @@
     dp_out[...] = (d_cos * (q[...] * scale - (c * b * b) * k[...])).astype(BF16)
 
 
-def token_grad_kernel(width, place, dq, dk, dv, *refs):
-    del place
-    qk, up, out = refs
+def token_grad_kernel(width, parts, place, dq, dk, dv, *refs):
+    out = refs[2 * parts]
     dims = (((1,), (1,)), ((), ()))
-    total = lax.dot_general(dq[...], qk[:, :width], dims, preferred_element_type=F32)
-    total += lax.dot_general(dk[...], qk[:, width:], dims, preferred_element_type=F32)
-    total += lax.dot_general(dv[...], up[...], dims, preferred_element_type=F32)
-    out[...] = total.astype(BF16)
+    for p in range(parts):
+        @pl.when(pl.program_id(0) == p)
+        def _(qk=refs[p], up=refs[parts + p]):
+            total = lax.dot_general(dq[...], qk[:, :width], dims, preferred_element_type=F32)
+            total += lax.dot_general(dk[...], qk[:, width:], dims, preferred_element_type=F32)
+            total += lax.dot_general(dv[...], up[...], dims, preferred_element_type=F32)
+            out[...] = total.astype(BF16)
 
 
 def flipped(x, bit):
@@ -217,18 +228,28 @@
     return x[:half] + flipped(x[half:].astype(BF16), bit).astype(F32)
 
 
-def reduce_rows(left, right, bits, parts, ctx_first):
-    depth = right.shape[0] * 2 // parts
+def first_hop(left, right, bits, parts):
     x = left + flipped(right, bits[0]).astype(F32)
-    x = x.reshape(parts // 2, depth, x.shape[1])
-    if ctx_first:
-        x = spread_sum(x, "ctx")
+    return x.reshape(parts // 2, right.shape[0] * 2 // parts, x.shape[1])
+
+
+def pair_hops(x, bits):
     for bit in bits[1:]:
         x = halve(x, bit)
-    if not ctx_first:
-        x = spread_sum(x, "ctx")
-    x = spread_sum(x, "dp")[0].astype(BF16)
-    return collect(collect(x, "dp"), "ctx").astype(F32)
+    return x
+
+
+def second_hop(x, bits, ctx_first):
+    return spread_sum(x, "ctx") if ctx_first else pair_hops(x, bits)
+
+
+def third_hop(x, bits, ctx_first):
+    return pair_hops(x, bits) if ctx_first else spread_sum(x, "ctx")
+
+
+def joint_sum(first, second):
+    x = jnp.concatenate([first, second], 2)
+    return spread_sum(x, "dp")[0].astype(BF16)
 
 
 def per_device(tokens, bounds, decay_rates, w_query, w_key, w_up, grad_out):
@@ -246,11 +267,14 @@
     order = [sum(((p >> s) & 1) << (levels - 1 - s) for s in range(levels)) for p in range(parts)]
 
     held = {0: jnp.concatenate([w_query, w_key], 1)}
+    others = sorted(range(1, parts), key=lambda j: (bin(j).count("1"), -j))
+    for j in others:
+        held[j] = flipped(held[j ^ (j & -j)], j & -j)
+    w_up, *waited = lax.optimization_barrier((w_up, *[held[j] for j in others]))
+    held.update(zip(others, waited))
     held_up = {0: w_up}
-    for store in (held, held_up):
-        for j in sorted(range(1, parts), key=lambda j: (bin(j).count("1"), -j)):
-            bit = j & -j
-            store[j] = flipped(store[j ^ bit], bit)
+    for j in others:
+        held_up[j] = flipped(held_up[j ^ (j & -j)], j & -j)
     qk_shards = [held[j] for j in order]
     up_shards = [held_up[j] for j in order]
 
@@ -325,17 +349,29 @@
 
     half_rows = width // 2
 
-    def chain(x_t, d, ctx_first):
-        right = mm(x_t[half_rows:], d).astype(BF16)
-        left = mm(x_t[:half_rows], d)
-        return reduce_rows(left, right, bits, parts, ctx_first)
+    def terms(x_t, d):
+        return mm(x_t[:half_rows], d), mm(x_t[half_rows:], d).astype(BF16)
 
     cut = hidden // 2
-    up_a = chain(tok_t, d_values[:, :cut], False)
-    up_b = chain(tok_t, d_values[:, cut:], True)
-
-    up_full = jnp.concatenate(up_shards, 0)
-    values = mm(tok, up_full)
+    terms_a = terms(tok_t, d_values[:, :cut])
+    terms_b = terms(tok_t, d_values[:, cut:])
+    up_a = first_hop(*terms_a, bits, parts)
+    up_b = first_hop(*terms_b, bits, parts)
+    up_a, up_b, up_shards = lax.optimization_barrier((up_a, up_b, up_shards))
+    up_a = second_hop(up_a, bits, False)
+    up_b = second_hop(up_b, bits, True)
+
+    values = call(
+        functools.partial(value_kernel, parts),
+        (length // tile,),
+        [rows_of(tile, width)] + [whole((depth, hidden))] * parts,
+        rows_of(tile, hidden),
+        shape((length, hidden), F32),
+        [],
+        2 * length * width * hidden,
+        2 * width * hidden + 4 * length * hidden,
+        "values",
+    )(tok, *up_shards)
     states, diff, dec, decp, last_row = call(
         functools.partial(state_kernel, heads, channels),
         (blocks,),
@@ -362,15 +398,27 @@
         "finish",
     )(states, diff, adj, tail, dec, decp, decay, adj_in, st_in, q, k, iq, ik, cosine, marked, opening)
 
-    grad_query = chain(tok_t, d_query, False)
-    grad_key = chain(prev_t, d_prev, True)
+    up_a, up_b, d_query, d_prev = lax.optimization_barrier((up_a, up_b, d_query, d_prev))
+    terms_q, terms_k = terms(tok_t, d_query), terms(prev_t, d_prev)
+    terms_q, terms_k, d_query, d_prev = lax.optimization_barrier((terms_q, terms_k, d_query, d_prev))
+    part_q = first_hop(*terms_q, bits, parts)
+    part_k = first_hop(*terms_k, bits, parts)
+    up_a = third_hop(up_a, bits, False)
+    up_b = third_hop(up_b, bits, True)
+    up_a, up_b, part_q, part_k = lax.optimization_barrier((up_a, up_b, part_q, part_k))
+    up_joint = collect(joint_sum(up_a, up_b), "dp")
+    part_q = third_hop(second_hop(part_q, bits, False), bits, False)
+    part_k = third_hop(second_hop(part_k, bits, True), bits, True)
+    qk_joint = joint_sum(part_q, part_k)
+    up_joint, qk_joint = lax.optimization_barrier((up_joint, qk_joint))
+    grad_up = collect(up_joint, "ctx").astype(F32)
+    grad_qk = collect(collect(qk_joint, "dp"), "ctx").astype(F32)
 
     after = shifted(d_prev[:1], "ctx", -1)
     d_key = jnp.concatenate([d_prev[1:], after], 0)
-    qk_full = jnp.concatenate(qk_shards, 0)
     place = jnp.stack([me ^ j for j in order]).astype(jnp.int32)
     grad_tokens = pl.pallas_call(
-        functools.partial(token_grad_kernel, width),
+        functools.partial(token_grad_kernel, width, parts),
         grid_spec=pltpu.PrefetchScalarGridSpec(
             num_scalar_prefetch=1,
             grid=(parts,),
@@ -378,9 +426,9 @@
                 pl.BlockSpec((length, width), lambda i, s: (0, 0)),
                 pl.BlockSpec((length, width), lambda i, s: (0, 0)),
                 pl.BlockSpec((length, hidden), lambda i, s: (0, 0)),
-                pl.BlockSpec((depth, 2 * width), lambda i, s: (i, 0)),
-                pl.BlockSpec((depth, hidden), lambda i, s: (i, 0)),
-            ],
+            ]
+            + [pl.BlockSpec((depth, 2 * width), lambda i, s: (0, 0))] * parts
+            + [pl.BlockSpec((depth, hidden), lambda i, s: (0, 0))] * parts,
             out_specs=pl.BlockSpec((length, depth), lambda i, s: (0, s[i])),
         ),
         out_shape=shape((length, width), BF16),
@@ -391,13 +439,13 @@
             bytes_accessed=2 * width * (2 * width + hidden),
             transcendentals=0,
         ),
-    )(place, d_query, d_key, d_values, qk_full, up_full)
+    )(place, d_query, d_key, d_values, *qk_shards, *up_shards)
     return (
         dechunked.reshape(batch_local, length, hidden),
         grad_tokens.reshape(batch_local, length, width),
-        grad_query,
-        grad_key,
-        jnp.concatenate([up_a, up_b], 1),
+        grad_qk[:, :width],
+        grad_qk[:, width:],
+        grad_up,
     )
 
 

time: 249 us -> 217 us (0.87)
  starting transfers between devices: 65.5 us -> 45 us
  waiting for transfers between devices: 83.8 us -> 72.7 us
  local copies, waits for them, and re-layouts: 16.9 us -> 21.4 us
  Pallas kernels: 51.1 us -> 47.7 us
    ppermute x14, waiting for transfers between devices: 45.4 us -> 24.5 us  [flipped(): return lax.ppermute(x, 'fsdp', [(i, i ^ bit) for i in range(n)])]
    ppermute x32 -> x18, starting transfers between devices: 45.1 us -> 24.7 us  [turned(): return lax.ppermute(x, axis, [(i, (i + by) % n) for i in range(n)])]
    concatenate x4 -> x2, other arithmetic: 10.7 us -> 0.16 us  [joint_sum(): x = jnp.concatenate([first, second], 2)]
    pallas_call x1, Pallas kernels: 18.1 us -> 9.2 us  [per_device(): call(functools.partial(finish_kernel, heads, channels), (blocks,), [rows_...]
    add x0 -> x2, other arithmetic: none -> 5.88 us  [first_hop(): x = left + flipped(right, bits[0]).astype(F32)]
    pallas_call x1 -> x2, Pallas kernels: 8.47 us -> 13.9 us  [the longest x1 10 us: per_device(): pl.pallas_call(functools.partial(token_grad_kernel, width, parts), grid_s...]
    ppermute x4, waiting for transfers between devices: 0.01 us -> 5.42 us  [shifted(): lax.ppermute(x, axis, [(i, i + by) for i in range(n) if 0 <= i + by < n])]
    ppermute x32 -> x18, waiting for transfers between devices: 38.5 us -> 42.8 us  [turned(): return lax.ppermute(x, axis, [(i, (i + by) % n) for i in range(n)])]
  transfers between devices with their start and end apart: 50 -> 36, of which waited for: 14 -> 20; matrix products, arithmetic and copies ran while one was open for 15% -> 9% of each run, Pallas kernels for 5% -> 22%
where the time goes in v2:
time: 217 us; the launch traced here: 216 us
  waiting for transfers between devices  72.7 us (34%)
  Pallas kernels  47.7 us (22%)
  starting transfers between devices  45 us (21%)
  local copies, waits for them, and re-layouts  21.4 us (10%)
  other arithmetic  16.2 us (7%)
  matrix products  11.8 us (5%)
    ppermute x18, waiting for transfers between devices, turned(): return lax.ppermute(x, axis, [(i, (i + by) % n) for i in range(n)])  42.8 us
    ppermute x18, starting transfers between devices, turned(): return lax.ppermute(x, axis, [(i, (i + by) % n) for i in range(n)])  24.7 us
    ppermute x14, waiting for transfers between devices, flipped(): return lax.ppermute(x, 'fsdp', [(i, i ^ bit) for i in range(n)])  24.5 us
    unnamed x106, local copies, waits for them, and re-layouts  12.7 us
    dot_general x8, matrix products, mm(): lax.dot_general(a, b, (((1,), (0,)), ((), ())), preferred_element_type=F32)  11.8 us
    ppermute x14, starting transfers between devices, flipped(): return lax.ppermute(x, 'fsdp', [(i, i ^ bit) for i in range(n)])  10.3 us
    pallas_call x1, Pallas kernels, per_device(): pl.pallas_call(functools.partial(token_grad_kernel, width, parts), grid_s...  10 us
    ppermute x4, starting transfers between devices, shifted(): lax.ppermute(x, axis, [(i, i + by) for i in range(n) if 0 <= i + by < n])  9.99 us
  transfers between devices with their start and end apart: 36, of which 20 were waited for; matrix products, arithmetic and copies ran while one was open for 9% of the time, Pallas kernels for 22%

profile of v2, /device:TPU:0, one launch (start us, length us, event | category | flops | bytes accessed | tf_op | source)
XLA Modules:
  0.0 216.2 jit_solution(16306756682684802604)
XLA Ops:
  0.7 1.2 constant_dynamic-update-slice_fusion.1
  1.8 1.1 constant_dynamic-update-slice_fusion.refs_4_.refs_0_
  2.9 3.0 %collective-permute-start.1 = (bf16[256,2048]{1,0:T(8,128)(2,1)S(1)}, bf16[256,2048]{1,0:T(8,128)(2,1)S(1)}, u32[]{:S(2)}, u32[]{:S(2)}) collective-permute-start(bf16[256,2048]{1,0:T(8,128)(2,1)S(1)} %constant_dynamic-update-slice_fusion.refs_4_.refs_0_), channel_id=1, source_target_pairs={{0,4},{2,6},{4,0},{6,2},{1,5},{3,7},{5,1},{7,3},{8,12},{10,14},{12... | collective-permute-start | bytes 3145736 | tf_op jit(solution)/shard_map/ppermute | solution.py:189
  5.9 3.4 %collective-permute-start = (bf16[1,1024]{1,0:T(2,128)(2,1)S(1)}, bf16[1,1024]{1,0:T(2,128)(2,1)S(1)}, u32[]{:S(2)}, u32[]{:S(2)}) collective-permute-start(bf16[1,1024]{1,0:T(2,128)(2,1)S(1)} %slice_bitcast_fusion.1), channel_id=1, source_target_pairs={{0,1},{2,3},{4,5},{6,7},{8,9},{10,11},{12,13},{14,15},{16,17},{18,... | collective-permute-start | bytes 6152 | tf_op jit(solution)/shard_map/ppermute | solution.py:199
  9.8 19.3 %collective-permute-done.1.refs_5_.refs_1_ = bf16[256,2048]{1,0:T(8,128)(2,1)S(1)} collective-permute-done((bf16[256,2048]{1,0:T(8,128)(2,1)S(1)}, bf16[256,2048]{1,0:T(8,128)(2,1)S(1)}, u32[]{:S(2)}, u32[]{:S(2)}) %collective-permute-start.1) | collective-permute-done | bytes 1048608 | tf_op jit(solution)/shard_map/ppermute | solution.py:189
  30.3 1.2 fusion.45
  31.8 1.8 collective-permute-start.7
  33.6 5.5 %route.1 = (f32[512,1024]{1,0:T(8,128)}, f32[512,1024]{1,0:T(8,128)}, f32[512,1]{1,0:T(8,128)S(1)}, f32[512,1]{1,0:T(8,128)S(1)}, f32[512,1]{1,0:T(8,128)S(1)}, /*index=5*/f32[512,1]{1,0:T(8,128)S(1)}) custom-call(bf16[512,1024]{1,0:T(8,128)(2,1)S(1)} %get-tuple-element.112.refs_0_.tok, bf16[512,1024]{1,0:T(8,128)(2,1)S(1)} %get-tuple-element.110.refs_1_, ...), custom_call_target="tpu_custom_call" | custom-call | flops 2147483648 | bytes 10485760 | tf_op jit(solution)/shard_map/route/pallas_call | solution.py:301
  39.1 5.8 %adjoint.1 = (f32[512,2048]{1,0:T(8,128)}, f32[512,16]{1,0:T(8,128)S(1)}, f32[1,2048]{1,0:T(1,128)S(1)}, f32[1,16]{1,0:T(1,128)}) custom-call(f32[512,1]{1,0:T(8,128)S(1)} %get-tuple-element.53.mp, f32[1,16]{1,0:T(1,128)S(1)} %bitcast.102, bf16[512,2048]{1,0:T(8,128)(2,1)S(1)} %bitcast.106), custom_call_target="tpu_custom_call" | custom-call | flops 1073741824 | bytes 6291456 | tf_op jit(solution)/shard_map/adjoint/pallas_call | solution.py:318
  45.0 1.3 collective-permute-start.4
  46.3 4.2 %collective-permute-done.4.adj_in = f32[1,2048]{1,0:T(1,128)S(1)} collective-permute-done((f32[1,2048]{1,0:T(1,128)S(1)}, f32[1,2048]{1,0:T(1,128)S(1)}, u32[]{:S(2)}, u32[]{:S(2)}) %collective-permute-start.4) | collective-permute-done | bytes 8224 | tf_op jit(solution)/shard_map/ppermute | solution.py:199
  50.5 4.6 %value_grad.1.dv = bf16[512,2048]{1,0:T(8,128)(2,1)S(1)} custom-call(f32[512,2048]{1,0:T(8,128)} %get-tuple-element.55.adj, f32[512,16]{1,0:T(8,128)S(1)} %get-tuple-element.56.tail, f32[512,1]{1,0:T(8,128)S(1)} %get-tuple-element.53.mp, f32[1,16]{1,0:T(1,128)S(1)} %bitcast.103, f32[1,2048]{1,0:T(1,128)S(1)} %collective-permute-done.4.adj_in), custom_call_target="tpu_custom_call" | custom-call | flops 4194304 | bytes 6291456 | tf_op jit(solution)/shard_map/value_grad/pallas_call | solution.py:338
  58.6 2.0 convert_add_fusion.2
  61.6 1.0 copy-done.10
  63.1 1.0 copy-done.12
  65.9 2.1 fusion.10
  68.4 1.2 copy-done.11
  69.6 1.2 copy-done.13
  70.8 3.9 %values.1 = f32[512,2048]{1,0:T(8,128)} custom-call(bf16[512,1024]{1,0:T(8,128)(2,1)S(1)} %get-tuple-element.112.refs_0_.tok, bf16[256,2048]{1,0:T(8,128)(2,1)S(1)} %copy-done.7, bf16[256,2048]{1,0:T(8,128)(2,1)S(1)} %copy-done.9, bf16[256,2048]{1,0:T(8,128)(2,1)S(1)} %copy-done.11, bf16[256,2048]{1,0:T(8,128)(2,1)S(1)} %copy-done.13), custom_call_target="tpu_custom_call" | custom-call | flops 2147483648 | bytes 8388608 | tf_op jit(solution)/shard_map/values/pallas_call | solution.py:364
  74.8 8.5 %state.1 = (f32[512,2048]{1,0:T(8,128)S(1)}, f32[512,2048]{1,0:T(8,128)}, f32[512,16]{1,0:T(8,128)S(1)}, f32[512,16]{1,0:T(8,128)S(1)}, f32[1,2048]{1,0:T(1,128)S(1)}) custom-call(f32[512,1]{1,0:T(8,128)S(1)} %copy-done.25, f32[1,16]{1,0:T(1,128)S(1)} %bitcast.104, f32[512,2048]{1,0:T(8,128)} %values.1), custom_call_target="tpu_custom_call" | custom-call | flops 1610612736 | bytes 12582912 | tf_op jit(solution)/shard_map/state/pallas_call | solution.py:375
  83.3 2.1 copy-done.1
  86.8 3.7 %collective-permute-start.10 = (f32[1,2048]{1,0:T(1,128)S(1)}, f32[1,2048]{1,0:T(1,128)S(1)}, u32[]{:S(2)}, u32[]{:S(2)}) collective-permute-start(f32[1,2048]{1,0:T(1,128)S(1)} %get-tuple-element.67), channel_id=1, source_target_pairs={{0,1},{2,3},{4,5},{6,7},{8,9},{10,11},{12,13},{14,15},{16,17},{18,... | collective-permute-start | bytes 24584 | tf_op jit(solution)/shard_map/ppermute | solution.py:199
  90.6 1.2 collective-permute-done.10.st_in
  91.7 0.9 copy-done.19
  92.7 0.9 copy-done.21
  93.6 0.9 copy-done.23
  94.6 9.2 %finish.1 = (bf16[512,2048]{1,0:T(8,128)(2,1)}, bf16[512,1024]{1,0:T(8,128)(2,1)S(1)}, bf16[512,1024]{1,0:T(8,128)(2,1)S(1)}) custom-call(f32[512,2048]{1,0:T(8,128)} %copy-done.1, f32[512,2048]{1,0:T(8,128)} %get-tuple-element.64.diff, f32[512,2048]{1,0:T(8,128)} %get-tuple-element.55.adj, f32[512,16]{1,0:T(8,128)S(1)} %get-tuple-element.56.tail, ...), custom_call_target="tpu_custom_call" | custom-call | flops 20971520 | bytes 20971520 | tf_op jit(solution)/shard_map/finish/pallas_call | solution.py:388
  103.8 1.3 convert_add_fusion.5
  105.5 1.2 bitcast_add_fusion.1
  106.8 1.7 convolution_convert_fusion
  108.5 2.1 fusion.13
  110.5 1.7 convolution_convert_fusion.1
  112.3 2.0 fusion.18
  115.1 2.3 %collective-permute-start.14 = (bf16[1,128,1024]{2,1,0:T(8,128)(2,1)}, bf16[1,128,1024]{2,1,0:T(8,128)(2,1)S(1)}, u32[]{:S(2)}, u32[]{:S(2)}) collective-permute-start(bf16[1,128,1024]{2,1,0:T(8,128)(2,1)} %fusion.22), channel_id=1, source_target_pairs={{0,1},{1,0},{2,3},{3,2},{4,5},{5,4},{6,7},{7,6},{8,9},{9,8},{10,11... | collective-permute-start | bytes 786440 | tf_op jit(solution)/shard_map/ppermute | solution.py:194
  118.3 1.1 collective-permute-start.15
  119.5 5.1 %collective-permute-done.14 = bf16[1,128,1024]{2,1,0:T(8,128)(2,1)S(1)} collective-permute-done((bf16[1,128,1024]{2,1,0:T(8,128)(2,1)}, bf16[1,128,1024]{2,1,0:T(8,128)(2,1)S(1)}, u32[]{:S(2)}, u32[]{:S(2)}) %collective-permute-start.14) | collective-permute-done | bytes 262176 | tf_op jit(solution)/shard_map/ppermute | solution.py:194
  124.6 2.5 %collective-permute-done.15 = bf16[1,128,1024]{2,1,0:T(8,128)(2,1)} collective-permute-done((bf16[1,128,1024]{2,1,0:T(8,128)(2,1)}, bf16[1,128,1024]{2,1,0:T(8,128)(2,1)}, u32[]{:S(2)}, u32[]{:S(2)}) %collective-permute-start.15) | collective-permute-done | bytes 262176 | tf_op jit(solution)/shard_map/ppermute | solution.py:189
  127.1 1.2 convert_add_fusion.6
  128.3 3.0 %convert_add_fusion = f32[512,1024]{1,0:T(8,128)} fusion(f32[512,1024]{1,0:T(8,128)S(1)} %copy-done.33, bf16[512,1024]{1,0:T(8,128)(2,1)} %collective-permute-done.17), kind=kLoop, calls=%fused_computation.4 | loop fusion | flops 1048576 | bytes 5242880 | tf_op jit(solution)/shard_map/add | solution.py:232
  131.4 2.9 %convert_add_fusion.1 = f32[512,1024]{1,0:T(8,128)} fusion(f32[512,1024]{1,0:T(8,128)S(1)} %copy-done.32, bf16[512,1024]{1,0:T(8,128)(2,1)} %collective-permute-done.16), kind=kLoop, calls=%fused_computation.5 | loop fusion | flops 1048576 | bytes 5242880 | tf_op jit(solution)/shard_map/add | solution.py:232
  135.1 1.6 collective-permute-start.18
  136.6 2.6 %collective-permute-start.19 = (bf16[1,32,2048]{2,1,0:T(8,128)(2,1)}, bf16[1,32,2048]{2,1,0:T(8,128)(2,1)S(1)}, u32[]{:S(2)}, u32[]{:S(2)}) collective-permute-start(bf16[1,32,2048]{2,1,0:T(8,128)(2,1)} %get-tuple-element.108), channel_id=1, source_target_pairs={{0,16},{8,24},{16,0},{24,8},{1,17},{9,25},{17,1},{25,9},{2,18},{10... | collective-permute-start | bytes 393224 | tf_op jit(solution)/shard_map/ppermute | solution.py:194
  139.2 1.3 collective-permute-start.20
  141.0 1.6 collective-permute-start.13
  142.5 1.1 collective-permute-done.18
  143.7 4.1 %collective-permute-done.19 = bf16[1,32,2048]{2,1,0:T(8,128)(2,1)S(1)} collective-permute-done((bf16[1,32,2048]{2,1,0:T(8,128)(2,1)}, bf16[1,32,2048]{2,1,0:T(8,128)(2,1)S(1)}, u32[]{:S(2)}, u32[]{:S(2)}) %collective-permute-start.19) | collective-permute-done | bytes 131104 | tf_op jit(solution)/shard_map/ppermute | solution.py:194
  147.9 4.3 %collective-permute-start.21 = (bf16[32,2048]{1,0:T(8,128)(2,1)S(1)}, bf16[32,2048]{1,0:T(8,128)(2,1)S(1)}, u32[]{:S(2)}, u32[]{:S(2)}) collective-permute-start(bf16[32,2048]{1,0:T(8,128)(2,1)S(1)} %get-tuple-element.96), channel_id=1, source_target_pairs={{0,24},{8,0},{16,8},{24,16},{1,25},{9,1},{17,9},{25,17},{2,26},{10... | collective-permute-start | bytes 393224 | tf_op jit(solution)/shard_map/ppermute | solution.py:194
  152.4 1.2 collective-permute-start.24
  154.4 1.3 collective-permute-done.21
  155.7 8.7 %collective-permute-done.22 = bf16[32,2048]{1,0:T(8,128)(2,1)S(1)} collective-permute-done((bf16[32,2048]{1,0:T(8,128)(2,1)S(1)}, bf16[32,2048]{1,0:T(8,128)(2,1)S(1)}, u32[]{:S(2)}, u32[]{:S(2)}) %collective-permute-start.22) | collective-permute-done | bytes 131104 | tf_op jit(solution)/shard_map/ppermute | solution.py:194
  165.6 0.9 collective-permute-start.27
  166.6 5.6 %collective-permute-done.25 = bf16[1,128,1024]{2,1,0:T(8,128)(2,1)S(1)} collective-permute-done((bf16[1,128,1024]{2,1,0:T(8,128)(2,1)S(1)}, bf16[1,128,1024]{2,1,0:T(8,128)(2,1)S(1)}, u32[]{:S(2)}, u32[]{:S(2)}) %collective-permute-start.25) | collective-permute-done | bytes 262176 | tf_op jit(solution)/shard_map/ppermute | solution.py:194
  174.8 2.8 %collective-permute-start.30 = (bf16[1,32,2048]{2,1,0:T(8,128)(2,1)S(1)}, bf16[1,32,2048]{2,1,0:T(8,128)(2,1)S(1)}, u32[]{:S(2)}, u32[]{:S(2)}) collective-permute-start(bf16[1,32,2048]{2,1,0:T(8,128)(2,1)S(1)} %get-tuple-element.104), channel_id=1, source_target_pairs={{0,24},{8,0},{16,8},{24,16},{1,25},{9,1},{17,9},{25,17},{2,26},{10... | collective-permute-start | bytes 393224 | tf_op jit(solution)/shard_map/ppermute | solution.py:194
  177.7 4.0 %collective-permute-done.28 = bf16[1,32,2048]{2,1,0:T(8,128)(2,1)S(1)} collective-permute-done((bf16[1,32,2048]{2,1,0:T(8,128)(2,1)S(1)}, bf16[1,32,2048]{2,1,0:T(8,128)(2,1)S(1)}, u32[]{:S(2)}, u32[]{:S(2)}) %collective-permute-start.28) | collective-permute-done | bytes 131104 | tf_op jit(solution)/shard_map/ppermute | solution.py:194
  181.6 3.1 %collective-permute-done.29 = bf16[1,32,2048]{2,1,0:T(8,128)(2,1)S(1)} collective-permute-done((bf16[1,32,2048]{2,1,0:T(8,128)(2,1)S(1)}, bf16[1,32,2048]{2,1,0:T(8,128)(2,1)S(1)}, u32[]{:S(2)}, u32[]{:S(2)}) %collective-permute-start.29) | collective-permute-done | bytes 131104 | tf_op jit(solution)/shard_map/ppermute | solution.py:194
  184.8 3.0 %collective-permute-start.31 = (bf16[32,2048]{1,0:T(8,128)(2,1)S(1)}, bf16[32,2048]{1,0:T(8,128)(2,1)S(1)}, u32[]{:S(2)}, u32[]{:S(2)}) collective-permute-start(bf16[32,2048]{1,0:T(8,128)(2,1)S(1)} %fusion.44), channel_id=1, source_target_pairs={{0,24},{8,0},{16,8},{24,16},{1,25},{9,1},{17,9},{25,17},{2,26},{10... | collective-permute-start | bytes 393224 | tf_op jit(solution)/shard_map/ppermute | solution.py:194
  188.7 1.1 collective-permute-start.35
  189.8 1.9 collective-permute-done.31
  191.7 7.9 %collective-permute-done.32 = bf16[32,2048]{1,0:T(8,128)(2,1)S(1)} collective-permute-done((bf16[32,2048]{1,0:T(8,128)(2,1)S(1)}, bf16[32,2048]{1,0:T(8,128)(2,1)S(1)}, u32[]{:S(2)}, u32[]{:S(2)}) %collective-permute-start.32) | collective-permute-done | bytes 131104 | tf_op jit(solution)/shard_map/ppermute | solution.py:194
  199.8 1.5 collective-permute-start.34
  201.3 10.0 %token_grad.1 = bf16[512,1024]{1,0:T(8,128)(2,1)} custom-call(s32[4]{0:T(128)S(1)} %pad_add_fusion.place, bf16[512,1024]{1,0:T(8,128)(2,1)S(1)} %get-tuple-element.81.dq, bf16[512,1024]{1,0:T(8,128)(2,1)S(1)} %pad_maximum_fusion.2.dk, bf16[512,2048]{1,0:T(8,128)(2,1)} %copy-done, bf16[256,2048]{1,0:T(8,128)(2,1)S(1)} %copy-done.27, ...), custom_call_target="tpu_custom_call" | custom-call | flops 4294967296 | bytes 8388608 | tf_op jit(solution)/shard_map/token_grad/pallas_call | solution.py:420
  211.3 2.4 %fusion.2 = f32[256,2048]{1,0:T(8,128)} fusion(s32[]{:T(128)S(6)} %select_n.78, bf16[128,2048]{1,0:T(8,128)(2,1)S(1)} %constant_dynamic-slice_fusion.1, bf16[128,2048]{1,0:T(8,128)(2,1)S(1)} %collective-permute-done.35), kind=kLoop, calls=%fused_computation.20 | loop fusion | flops 3145728 | bytes 3145732 | tf_op jit(solution)/shard_map/convert_element_type | solution.py:414
  213.7 1.1 fusion.5
  214.8 1.5 fusion.48
  (175 shorter events, 19.5 us)
Async XLA Ops:
  0.6 5.3 %copy-start.41 = (bf16[1,512,1024]{2,1,0:T(8,128)(2,1)S(1)}, bf16[1,512,1024]{2,1,0:T(8,128)(2,1)}, u32[]{:S(2)}) copy-start(bf16[1,512,1024]{2,1,0:T(8,128)(2,1)} %param.7) | copy-start | bytes 3145732
  0.6 8.8 %copy-start.45 = (s32[1,512]{1,0:T(1,128)S(1)}, s32[1,512]{1,0:T(1,128)}, u32[]{:S(2)}) copy-start(s32[1,512]{1,0:T(1,128)} %param.8) | copy-start | bytes 6148
  2.9 30.6 %copy-start.26 = (bf16[256,2048]{1,0:T(8,128)(2,1)}, bf16[256,2048]{1,0:T(8,128)(2,1)S(1)}, u32[]{:S(2)}) copy-start(bf16[256,2048]{1,0:T(8,128)(2,1)S(1)} %constant_dynamic-update-slice_fusion.refs_4_.refs_0_) | copy-start | bytes 3145732
  2.9 26.2 %collective-permute-start.1 = (bf16[256,2048]{1,0:T(8,128)(2,1)S(1)}, bf16[256,2048]{1,0:T(8,128)(2,1)S(1)}, u32[]{:S(2)}, u32[]{:S(2)}) collective-permute-start(bf16[256,2048]{1,0:T(8,128)(2,1)S(1)} %constant_dynamic-update-slice_fusion.refs_4_.refs_0_), channel_id=1, source_target_pairs={{0,4},{2,6},{4,0},{6,2},{1,5},{3,7},{5,1},{7,3},{8,12},{10,14},{12... | collective-permute-start | bytes 3145736 | tf_op jit(solution)/shard_map/ppermute | solution.py:189
  5.9 25.6 %collective-permute-start.2 = (bf16[256,2048]{1,0:T(8,128)(2,1)S(1)}, bf16[256,2048]{1,0:T(8,128)(2,1)}, u32[]{:S(2)}, u32[]{:S(2)}) collective-permute-start(bf16[256,2048]{1,0:T(8,128)(2,1)S(1)} %constant_dynamic-update-slice_fusion.refs_4_.refs_0_), channel_id=1, source_target_pairs={{0,2},{2,0},{4,6},{6,4},{1,3},{3,1},{5,7},{7,5},{8,10},{10,8},{12,... | collective-permute-start | bytes 3145736 | tf_op jit(solution)/shard_map/ppermute | solution.py:189
  5.9 23.6 %collective-permute-start = (bf16[1,1024]{1,0:T(2,128)(2,1)S(1)}, bf16[1,1024]{1,0:T(2,128)(2,1)S(1)}, u32[]{:S(2)}, u32[]{:S(2)}) collective-permute-start(bf16[1,1024]{1,0:T(2,128)(2,1)S(1)} %slice_bitcast_fusion.1), channel_id=1, source_target_pairs={{0,1},{2,3},{4,5},{6,7},{8,9},{10,11},{12,13},{14,15},{16,17},{18,... | collective-permute-start | bytes 6152 | tf_op jit(solution)/shard_map/ppermute | solution.py:199
  9.7 19.7 %copy-start.42 = (bf16[1,512,1024]{2,1,0:T(8,128)(2,1)S(1)}, bf16[1,512,1024]{2,1,0:T(8,128)(2,1)}, u32[]{:S(2)}) copy-start(bf16[1,512,1024]{2,1,0:T(8,128)(2,1)} %param.7) | copy-start | bytes 3145732
  29.1 4.4 %copy-start.30 = (bf16[256,2048]{1,0:T(8,128)(2,1)}, bf16[256,2048]{1,0:T(8,128)(2,1)S(1)}, u32[]{:S(2)}) copy-start(bf16[256,2048]{1,0:T(8,128)(2,1)S(1)} %collective-permute-done.1.refs_5_.refs_1_) | copy-start | bytes 3145732
  29.1 2.7 %collective-permute-start.3 = (bf16[256,2048]{1,0:T(8,128)(2,1)S(1)}, bf16[256,2048]{1,0:T(8,128)(2,1)S(1)}, u32[]{:S(2)}, u32[]{:S(2)}) collective-permute-start(bf16[256,2048]{1,0:T(8,128)(2,1)S(1)} %collective-permute-done.1.refs_5_.refs_1_), channel_id=1, source_target_pairs={{0,2},{2,0},{4,6},{6,4},{1,3},{3,1},{5,7},{7,5},{8,10},{10,8},{12,... | collective-permute-start | bytes 3145736 | tf_op jit(solution)/shard_map/ppermute | solution.py:189
  29.4 31.3 %copy-start.34 = (bf16[1024,512]{0,1:T(8,128)(2,1)}, bf16[1024,512]{0,1:T(8,128)(2,1)S(1)}, u32[]{:S(2)}) copy-start(bf16[1024,512]{0,1:T(8,128)(2,1)S(1)} %get-tuple-element.54) | copy-start | bytes 3145732
  29.4 4.1 %copy-start.2 = (f32[512,1]{1,0:T(8,128)}, f32[512,1]{1,0:T(8,128)S(1)}, u32[]{:S(2)}) copy-start(f32[512,1]{1,0:T(8,128)S(1)} %fusion.36.refs_2_.marked) | copy-start | bytes 6148
  29.5 4.0 %copy-start.4 = (f32[512,1]{1,0:T(8,128)}, f32[512,1]{1,0:T(8,128)S(1)}, u32[]{:S(2)}) copy-start(f32[512,1]{1,0:T(8,128)S(1)} %fusion.35.refs_3_.opening) | copy-start | bytes 6148
  31.8 25.6 %collective-permute-start.7 = (bf16[256,2048]{1,0:T(8,128)(2,1)S(1)}, bf16[256,2048]{1,0:T(8,128)(2,1)S(1)}, u32[]{:S(2)}, u32[]{:S(2)}) collective-permute-start(bf16[256,2048]{1,0:T(8,128)(2,1)S(1)} %copy-done.6), channel_id=1, source_target_pairs={{0,4},{2,6},{4,0},{6,2},{1,5},{3,7},{5,1},{7,3},{8,12},{10,14},{12... | collective-permute-start | bytes 3145736 | tf_op jit(solution)/shard_map/ppermute | solution.py:189
  33.5 5.6 %copy-start.28 = (f32[16]{0:T(128)S(1)}, f32[16]{0:T(128)}, u32[]{:S(2)}) copy-start(f32[16]{0:T(128)} %param.9) | copy-start | bytes 196
  33.5 5.6 %copy-start.29 = (bf16[1,512,2048]{2,1,0:T(8,128)(2,1)S(1)}, bf16[1,512,2048]{2,1,0:T(8,128)(2,1)}, u32[]{:S(2)}) copy-start(bf16[1,512,2048]{2,1,0:T(8,128)(2,1)} %param.13) | copy-start | bytes 6291460
  39.1 16.0 %copy-start.14 = (f32[512,1]{1,0:T(8,128)}, f32[512,1]{1,0:T(8,128)S(1)}, u32[]{:S(2)}) copy-start(f32[512,1]{1,0:T(8,128)S(1)} %get-tuple-element.70.iq) | copy-start | bytes 6148
  39.1 16.0 %copy-start.16 = (f32[512,1]{1,0:T(8,128)}, f32[512,1]{1,0:T(8,128)S(1)}, u32[]{:S(2)}) copy-start(f32[512,1]{1,0:T(8,128)S(1)} %get-tuple-element.71.ik) | copy-start | bytes 6148
  39.1 16.1 %copy-start.18 = (f32[512,1]{1,0:T(8,128)}, f32[512,1]{1,0:T(8,128)S(1)}, u32[]{:S(2)}) copy-start(f32[512,1]{1,0:T(8,128)S(1)} %get-tuple-element.72.cos) | copy-start | bytes 6148
  39.1 16.1 %copy-start.24 = (f32[512,1]{1,0:T(8,128)}, f32[512,1]{1,0:T(8,128)S(1)}, u32[]{:S(2)}) copy-start(f32[512,1]{1,0:T(8,128)S(1)} %get-tuple-element.53.mp) | copy-start | bytes 6148
  45.0 5.5 %collective-permute-start.4 = (f32[1,2048]{1,0:T(1,128)S(1)}, f32[1,2048]{1,0:T(1,128)S(1)}, u32[]{:S(2)}, u32[]{:S(2)}) collective-permute-start(f32[1,2048]{1,0:T(1,128)S(1)} %get-tuple-element.57), channel_id=1, source_target_pairs={{1,0},{3,2},{5,4},{7,6},{9,8},{11,10},{13,12},{15,14},{17,16},{19,... | collective-permute-start | bytes 24584 | tf_op jit(solution)/shard_map/ppermute | solution.py:199
  55.2 5.5 %copy-start = (bf16[512,2048]{1,0:T(8,128)(2,1)}, bf16[512,2048]{1,0:T(8,128)(2,1)S(1)}, u32[]{:S(2)}) copy-start(bf16[512,2048]{1,0:T(8,128)(2,1)S(1)} %value_grad.1.dv) | copy-start | bytes 6291460
  55.9 2.7 %collective-permute-start.6 = (bf16[512,1024]{1,0:T(8,128)(2,1)S(1)}, bf16[512,1024]{1,0:T(8,128)(2,1)S(1)}, u32[]{:S(2)}, u32[]{:S(2)}) collective-permute-start(bf16[512,1024]{1,0:T(8,128)(2,1)S(1)} %convolution_convert_fusion.2), channel_id=1, source_target_pairs={{0,2},{2,0},{4,6},{6,4},{1,3},{3,1},{5,7},{7,5},{8,10},{10,8},{12,... | collective-permute-start | bytes 3145736 | tf_op jit(solution)/shard_map/ppermute | solution.py:189
  56.7 4.0 %collective-permute-start.5 = (bf16[512,1024]{1,0:T(8,128)(2,1)S(1)}, bf16[512,1024]{1,0:T(8,128)(2,1)S(1)}, u32[]{:S(2)}, u32[]{:S(2)}) collective-permute-start(bf16[512,1024]{1,0:T(8,128)(2,1)S(1)} %convolution_convert_fusion.3), channel_id=1, source_target_pairs={{0,2},{2,0},{4,6},{6,4},{1,3},{3,1},{5,7},{7,5},{8,10},{10,8},{12,... | collective-permute-start | bytes 3145736 | tf_op jit(solution)/shard_map/ppermute | solution.py:189
  57.3 4.3 %collective-permute-start.8 = (bf16[256,2048]{1,0:T(8,128)(2,1)S(1)}, bf16[256,2048]{1,0:T(8,128)(2,1)S(1)}, u32[]{:S(2)}, u32[]{:S(2)}) collective-permute-start(bf16[256,2048]{1,0:T(8,128)(2,1)S(1)} %copy-done.6), channel_id=1, source_target_pairs={{0,2},{2,0},{4,6},{6,4},{1,3},{3,1},{5,7},{7,5},{8,10},{10,8},{12,... | collective-permute-start | bytes 3145736 | tf_op jit(solution)/shard_map/ppermute | solution.py:189
  57.4 5.8 %collective-permute-start.9 = (bf16[256,2048]{1,0:T(8,128)(2,1)S(1)}, bf16[256,2048]{1,0:T(8,128)(2,1)S(1)}, u32[]{:S(2)}, u32[]{:S(2)}) collective-permute-start(bf16[256,2048]{1,0:T(8,128)(2,1)S(1)} %collective-permute-done.7.refs_1_.refs_5_), channel_id=1, source_target_pairs={{0,2},{2,0},{4,6},{6,4},{1,3},{3,1},{5,7},{7,5},{8,10},{10,8},{12,... | collective-permute-start | bytes 3145736 | tf_op jit(solution)/shard_map/ppermute | solution.py:189
  61.5 6.9 %copy-start.7 = (bf16[256,2048]{1,0:T(8,128)(2,1)S(1)}, bf16[256,2048]{1,0:T(8,128)(2,1)}, u32[]{:S(2)}) copy-start(bf16[256,2048]{1,0:T(8,128)(2,1)} %refs_4_) | copy-start | bytes 3145732
  61.5 6.9 %copy-start.9 = (bf16[256,2048]{1,0:T(8,128)(2,1)S(1)}, bf16[256,2048]{1,0:T(8,128)(2,1)}, u32[]{:S(2)}) copy-start(bf16[256,2048]{1,0:T(8,128)(2,1)} %copy-done.8) | copy-start | bytes 3145732
  65.0 38.8 %collective-permute-start.11 = (bf16[1,256,1024]{2,1,0:T(8,128)(2,1)}, bf16[1,256,1024]{2,1,0:T(8,128)(2,1)}, u32[]{:S(2)}, u32[]{:S(2)}) collective-permute-start(bf16[1,256,1024]{2,1,0:T(8,128)(2,1)} %slice.140), channel_id=1, source_target_pairs={{0,4},{2,6},{4,0},{6,2},{1,5},{3,7},{5,1},{7,3},{8,12},{10,14},{12... | collective-permute-start | bytes 1572872 | tf_op jit(solution)/shard_map/ppermute | solution.py:189
  68.0 37.1 %collective-permute-start.12 = (bf16[2,128,1024]{2,1,0:T(8,128)(2,1)}, bf16[2,128,1024]{2,1,0:T(8,128)(2,1)}, u32[]{:S(2)}, u32[]{:S(2)}) collective-permute-start(bf16[2,128,1024]{2,1,0:T(8,128)(2,1)} %fusion.10), channel_id=1, source_target_pairs={{0,1},{1,0},{2,3},{3,2},{4,5},{5,4},{6,7},{7,6},{8,9},{9,8},{10,11... | collective-permute-start | bytes 1572872 | tf_op jit(solution)/shard_map/ppermute | solution.py:194
  74.8 17.0 %copy-start.3 = (f32[512,1]{1,0:T(8,128)S(1)}, f32[512,1]{1,0:T(8,128)}, u32[]{:S(2)}) copy-start(f32[512,1]{1,0:T(8,128)} %copy-done.2) | copy-start | bytes 6148
  74.8 17.0 %copy-start.5 = (f32[512,1]{1,0:T(8,128)S(1)}, f32[512,1]{1,0:T(8,128)}, u32[]{:S(2)}) copy-start(f32[512,1]{1,0:T(8,128)} %copy-done.4) | copy-start | bytes 6148
  74.8 17.0 %copy-start.15 = (f32[512,1]{1,0:T(8,128)S(1)}, f32[512,1]{1,0:T(8,128)}, u32[]{:S(2)}) copy-start(f32[512,1]{1,0:T(8,128)} %copy-done.14) | copy-start | bytes 6148
  74.8 17.0 %copy-start.17 = (f32[512,1]{1,0:T(8,128)S(1)}, f32[512,1]{1,0:T(8,128)}, u32[]{:S(2)}) copy-start(f32[512,1]{1,0:T(8,128)} %copy-done.16) | copy-start | bytes 6148
  86.8 4.9 %collective-permute-start.10 = (f32[1,2048]{1,0:T(1,128)S(1)}, f32[1,2048]{1,0:T(1,128)S(1)}, u32[]{:S(2)}, u32[]{:S(2)}) collective-permute-start(f32[1,2048]{1,0:T(1,128)S(1)} %get-tuple-element.67), channel_id=1, source_target_pairs={{0,1},{2,3},{4,5},{6,7},{8,9},{10,11},{12,13},{14,15},{16,17},{18,... | collective-permute-start | bytes 24584 | tf_op jit(solution)/shard_map/ppermute | solution.py:199
  94.6 9.2 %copy-start.38 = (f32[512,1024]{1,0:T(8,128)S(1)}, f32[512,1024]{1,0:T(8,128)}, u32[]{:S(2)}) copy-start(f32[512,1024]{1,0:T(8,128)} %copy-done.37) | copy-start | bytes 6291460
  106.8 10.8 %copy-start.43 = (f32[2,128,1024]{2,1,0:T(8,128)}, f32[2,128,1024]{2,1,0:T(8,128)S(1)}, u32[]{:S(2)}) copy-start(f32[2,128,1024]{2,1,0:T(8,128)S(1)} %bitcast_add_fusion.1) | copy-start | bytes 3145732
  114.3 14.0 %collective-permute-start.17 = (bf16[512,1024]{1,0:T(8,128)(2,1)}, bf16[512,1024]{1,0:T(8,128)(2,1)}, u32[]{:S(2)}, u32[]{:S(2)}) collective-permute-start(bf16[512,1024]{1,0:T(8,128)(2,1)} %convolution_convert_fusion), channel_id=1, source_target_pairs={{0,2},{2,0},{4,6},{6,4},{1,3},{3,1},{5,7},{7,5},{8,10},{10,8},{12,... | collective-permute-start | bytes 3145736 | tf_op jit(solution)/shard_map/ppermute | solution.py:189
  115.1 9.5 %collective-permute-start.14 = (bf16[1,128,1024]{2,1,0:T(8,128)(2,1)}, bf16[1,128,1024]{2,1,0:T(8,128)(2,1)S(1)}, u32[]{:S(2)}, u32[]{:S(2)}) collective-permute-start(bf16[1,128,1024]{2,1,0:T(8,128)(2,1)} %fusion.22), channel_id=1, source_target_pairs={{0,1},{1,0},{2,3},{3,2},{4,5},{5,4},{6,7},{7,6},{8,9},{9,8},{10,11... | collective-permute-start | bytes 786440 | tf_op jit(solution)/shard_map/ppermute | solution.py:194
  117.4 14.0 %collective-permute-start.16 = (bf16[512,1024]{1,0:T(8,128)(2,1)}, bf16[512,1024]{1,0:T(8,128)(2,1)}, u32[]{:S(2)}, u32[]{:S(2)}) collective-permute-start(bf16[512,1024]{1,0:T(8,128)(2,1)} %convolution_convert_fusion.1), channel_id=1, source_target_pairs={{0,2},{2,0},{4,6},{6,4},{1,3},{3,1},{5,7},{7,5},{8,10},{10,8},{12,... | collective-permute-start | bytes 3145736 | tf_op jit(solution)/shard_map/ppermute | solution.py:189
  118.3 8.8 %collective-permute-start.15 = (bf16[1,128,1024]{2,1,0:T(8,128)(2,1)}, bf16[1,128,1024]{2,1,0:T(8,128)(2,1)}, u32[]{:S(2)}, u32[]{:S(2)}) collective-permute-start(bf16[1,128,1024]{2,1,0:T(8,128)(2,1)} %slice.142), channel_id=1, source_target_pairs={{0,4},{2,6},{4,0},{6,2},{1,5},{3,7},{5,1},{7,3},{8,12},{10,14},{12... | collective-permute-start | bytes 786440 | tf_op jit(solution)/shard_map/ppermute | solution.py:189
  119.5 8.9 %copy-start.33 = (f32[512,1024]{1,0:T(8,128)S(1)}, f32[512,1024]{1,0:T(8,128)}, u32[]{:S(2)}) copy-start(f32[512,1024]{1,0:T(8,128)} %fusion.13) | copy-start | bytes 6291460
  135.1 8.6 %collective-permute-start.18 = (bf16[1,32,2048]{2,1,0:T(8,128)(2,1)}, bf16[1,32,2048]{2,1,0:T(8,128)(2,1)S(1)}, u32[]{:S(2)}, u32[]{:S(2)}) collective-permute-start(bf16[1,32,2048]{2,1,0:T(8,128)(2,1)} %get-tuple-element.106), channel_id=1, source_target_pairs={{0,8},{8,16},{16,24},{24,0},{1,9},{9,17},{17,25},{25,1},{2,10},{10... | collective-permute-start | bytes 393224 | tf_op jit(solution)/shard_map/ppermute | solution.py:194
  136.6 11.1 %collective-permute-start.19 = (bf16[1,32,2048]{2,1,0:T(8,128)(2,1)}, bf16[1,32,2048]{2,1,0:T(8,128)(2,1)S(1)}, u32[]{:S(2)}, u32[]{:S(2)}) collective-permute-start(bf16[1,32,2048]{2,1,0:T(8,128)(2,1)} %get-tuple-element.108), channel_id=1, source_target_pairs={{0,16},{8,24},{16,0},{24,8},{1,17},{9,25},{17,1},{25,9},{2,18},{10... | collective-permute-start | bytes 393224 | tf_op jit(solution)/shard_map/ppermute | solution.py:194
  139.2 8.6 %collective-permute-start.20 = (bf16[1,32,2048]{2,1,0:T(8,128)(2,1)}, bf16[1,32,2048]{2,1,0:T(8,128)(2,1)S(1)}, u32[]{:S(2)}, u32[]{:S(2)}) collective-permute-start(bf16[1,32,2048]{2,1,0:T(8,128)(2,1)} %get-tuple-element.107), channel_id=1, source_target_pairs={{0,24},{8,0},{16,8},{24,16},{1,25},{9,1},{17,9},{25,17},{2,26},{10... | collective-permute-start | bytes 393224 | tf_op jit(solution)/shard_map/ppermute | solution.py:194
  140.7 11.6 %copy-start.36 = (f32[512,1024]{1,0:T(8,128)S(1)}, f32[512,1024]{1,0:T(8,128)}, u32[]{:S(2)}) copy-start(f32[512,1024]{1,0:T(8,128)} %convert_add_fusion.1) | copy-start | bytes 6291460
  140.9 12.7 %copy-start.39 = (f32[512,1024]{1,0:T(8,128)S(1)}, f32[512,1024]{1,0:T(8,128)}, u32[]{:S(2)}) copy-start(f32[512,1024]{1,0:T(8,128)} %convert_add_fusion) | copy-start | bytes 6291460
  141.0 11.2 %collective-permute-start.13 = (bf16[1,1024]{1,0:T(2,128)(2,1)S(1)}, bf16[1,1024]{1,0:T(2,128)(2,1)S(1)}, u32[]{:S(2)}, u32[]{:S(2)}) collective-permute-start(bf16[1,1024]{1,0:T(2,128)(2,1)S(1)} %slice.87), channel_id=1, source_target_pairs={{1,0},{3,2},{5,4},{7,6},{9,8},{11,10},{13,12},{15,14},{17,16},{19,... | collective-permute-start | bytes 6152 | tf_op jit(solution)/shard_map/ppermute | solution.py:199
  147.9 7.8 %collective-permute-start.21 = (bf16[32,2048]{1,0:T(8,128)(2,1)S(1)}, bf16[32,2048]{1,0:T(8,128)(2,1)S(1)}, u32[]{:S(2)}, u32[]{:S(2)}) collective-permute-start(bf16[32,2048]{1,0:T(8,128)(2,1)S(1)} %get-tuple-element.96), channel_id=1, source_target_pairs={{0,24},{8,0},{16,8},{24,16},{1,25},{9,1},{17,9},{25,17},{2,26},{10... | collective-permute-start | bytes 393224 | tf_op jit(solution)/shard_map/ppermute | solution.py:194
  152.4 12.1 %collective-permute-start.24 = (bf16[1,256,1024]{2,1,0:T(8,128)(2,1)S(1)}, bf16[1,256,1024]{2,1,0:T(8,128)(2,1)S(1)}, u32[]{:S(2)}, u32[]{:S(2)}) collective-permute-start(bf16[1,256,1024]{2,1,0:T(8,128)(2,1)S(1)} %slice.139), channel_id=1, source_target_pairs={{0,4},{2,6},{4,0},{6,2},{1,5},{3,7},{5,1},{7,3},{8,12},{10,14},{12... | collective-permute-start | bytes 1572872 | tf_op jit(solution)/shard_map/ppermute | solution.py:189
  153.7 11.8 %collective-permute-start.26 = (bf16[2,128,1024]{2,1,0:T(8,128)(2,1)S(1)}, bf16[2,128,1024]{2,1,0:T(8,128)(2,1)S(1)}, u32[]{:S(2)}, u32[]{:S(2)}) collective-permute-start(bf16[2,128,1024]{2,1,0:T(8,128)(2,1)S(1)} %fusion.11), channel_id=1, source_target_pairs={{0,1},{1,0},{2,3},{3,2},{4,5},{5,4},{6,7},{7,6},{8,9},{9,8},{10,11... | collective-permute-start | bytes 1572872 | tf_op jit(solution)/shard_map/ppermute | solution.py:194
  153.7 10.7 %collective-permute-start.22 = (bf16[32,2048]{1,0:T(8,128)(2,1)S(1)}, bf16[32,2048]{1,0:T(8,128)(2,1)S(1)}, u32[]{:S(2)}, u32[]{:S(2)}) collective-permute-start(bf16[32,2048]{1,0:T(8,128)(2,1)S(1)} %get-tuple-element.96), channel_id=1, source_target_pairs={{0,16},{8,24},{16,0},{24,8},{1,17},{9,25},{17,1},{25,9},{2,18},{10... | collective-permute-start | bytes 393224 | tf_op jit(solution)/shard_map/ppermute | solution.py:194
  154.2 10.2 %collective-permute-start.23 = (bf16[32,2048]{1,0:T(8,128)(2,1)S(1)}, bf16[32,2048]{1,0:T(8,128)(2,1)S(1)}, u32[]{:S(2)}, u32[]{:S(2)}) collective-permute-start(bf16[32,2048]{1,0:T(8,128)(2,1)S(1)} %get-tuple-element.96), channel_id=1, source_target_pairs={{0,8},{8,16},{16,24},{24,0},{1,9},{9,17},{17,25},{25,1},{2,10},{10... | collective-permute-start | bytes 393224 | tf_op jit(solution)/shard_map/ppermute | solution.py:194
  164.7 7.4 %collective-permute-start.25 = (bf16[1,128,1024]{2,1,0:T(8,128)(2,1)S(1)}, bf16[1,128,1024]{2,1,0:T(8,128)(2,1)S(1)}, u32[]{:S(2)}, u32[]{:S(2)}) collective-permute-start(bf16[1,128,1024]{2,1,0:T(8,128)(2,1)S(1)} %fusion.23), channel_id=1, source_target_pairs={{0,1},{1,0},{2,3},{3,2},{4,5},{5,4},{6,7},{7,6},{8,9},{9,8},{10,11... | collective-permute-start | bytes 786440 | tf_op jit(solution)/shard_map/ppermute | solution.py:194
  165.6 7.5 %collective-permute-start.27 = (bf16[1,128,1024]{2,1,0:T(8,128)(2,1)S(1)}, bf16[1,128,1024]{2,1,0:T(8,128)(2,1)S(1)}, u32[]{:S(2)}, u32[]{:S(2)}) collective-permute-start(bf16[1,128,1024]{2,1,0:T(8,128)(2,1)S(1)} %slice.141), channel_id=1, source_target_pairs={{0,4},{2,6},{4,0},{6,2},{1,5},{3,7},{5,1},{7,3},{8,12},{10,14},{12... | collective-permute-start | bytes 786440 | tf_op jit(solution)/shard_map/ppermute | solution.py:189
  173.4 8.3 %collective-permute-start.28 = (bf16[1,32,2048]{2,1,0:T(8,128)(2,1)S(1)}, bf16[1,32,2048]{2,1,0:T(8,128)(2,1)S(1)}, u32[]{:S(2)}, u32[]{:S(2)}) collective-permute-start(bf16[1,32,2048]{2,1,0:T(8,128)(2,1)S(1)} %get-tuple-element.103), channel_id=1, source_target_pairs={{0,8},{8,16},{16,24},{24,0},{1,9},{9,17},{17,25},{25,1},{2,10},{10... | collective-permute-start | bytes 393224 | tf_op jit(solution)/shard_map/ppermute | solution.py:194
  173.8 10.9 %collective-permute-start.29 = (bf16[1,32,2048]{2,1,0:T(8,128)(2,1)S(1)}, bf16[1,32,2048]{2,1,0:T(8,128)(2,1)S(1)}, u32[]{:S(2)}, u32[]{:S(2)}) collective-permute-start(bf16[1,32,2048]{2,1,0:T(8,128)(2,1)S(1)} %get-tuple-element.105), channel_id=1, source_target_pairs={{0,16},{8,24},{16,0},{24,8},{1,17},{9,25},{17,1},{25,9},{2,18},{10... | collective-permute-start | bytes 393224 | tf_op jit(solution)/shard_map/ppermute | solution.py:194
  174.8 9.9 %collective-permute-start.30 = (bf16[1,32,2048]{2,1,0:T(8,128)(2,1)S(1)}, bf16[1,32,2048]{2,1,0:T(8,128)(2,1)S(1)}, u32[]{:S(2)}, u32[]{:S(2)}) collective-permute-start(bf16[1,32,2048]{2,1,0:T(8,128)(2,1)S(1)} %get-tuple-element.104), channel_id=1, source_target_pairs={{0,24},{8,0},{16,8},{24,16},{1,25},{9,1},{17,9},{25,17},{2,26},{10... | collective-permute-start | bytes 393224 | tf_op jit(solution)/shard_map/ppermute | solution.py:194
  177.7 23.6 %copy-start.27 = (bf16[256,2048]{1,0:T(8,128)(2,1)S(1)}, bf16[256,2048]{1,0:T(8,128)(2,1)}, u32[]{:S(2)}) copy-start(bf16[256,2048]{1,0:T(8,128)(2,1)} %copy-done.26) | copy-start | bytes 3145732
  177.7 23.6 %copy-start.31 = (bf16[256,2048]{1,0:T(8,128)(2,1)S(1)}, bf16[256,2048]{1,0:T(8,128)(2,1)}, u32[]{:S(2)}) copy-start(bf16[256,2048]{1,0:T(8,128)(2,1)} %copy-done.30) | copy-start | bytes 3145732
  184.8 6.9 %collective-permute-start.31 = (bf16[32,2048]{1,0:T(8,128)(2,1)S(1)}, bf16[32,2048]{1,0:T(8,128)(2,1)S(1)}, u32[]{:S(2)}, u32[]{:S(2)}) collective-permute-start(bf16[32,2048]{1,0:T(8,128)(2,1)S(1)} %fusion.44), channel_id=1, source_target_pairs={{0,24},{8,0},{16,8},{24,16},{1,25},{9,1},{17,9},{25,17},{2,26},{10... | collective-permute-start | bytes 393224 | tf_op jit(solution)/shard_map/ppermute | solution.py:194
  187.8 11.9 %collective-permute-start.32 = (bf16[32,2048]{1,0:T(8,128)(2,1)S(1)}, bf16[32,2048]{1,0:T(8,128)(2,1)S(1)}, u32[]{:S(2)}, u32[]{:S(2)}) collective-permute-start(bf16[32,2048]{1,0:T(8,128)(2,1)S(1)} %fusion.44), channel_id=1, source_target_pairs={{0,16},{8,24},{16,0},{24,8},{1,17},{9,25},{17,1},{25,9},{2,18},{10... | collective-permute-start | bytes 393224 | tf_op jit(solution)/shard_map/ppermute | solution.py:194
  188.7 10.9 %collective-permute-start.33 = (bf16[32,2048]{1,0:T(8,128)(2,1)S(1)}, bf16[32,2048]{1,0:T(8,128)(2,1)S(1)}, u32[]{:S(2)}, u32[]{:S(2)}) collective-permute-start(bf16[32,2048]{1,0:T(8,128)(2,1)S(1)} %fusion.44), channel_id=1, source_target_pairs={{0,8},{8,16},{16,24},{24,0},{1,9},{9,17},{17,25},{25,1},{2,10},{10... | collective-permute-start | bytes 393224 | tf_op jit(solution)/shard_map/ppermute | solution.py:194
  188.7 22.6 %collective-permute-start.35 = (bf16[128,2048]{1,0:T(8,128)(2,1)S(1)}, bf16[128,2048]{1,0:T(8,128)(2,1)S(1)}, u32[]{:S(2)}, u32[]{:S(2)}) collective-permute-start(bf16[128,2048]{1,0:T(8,128)(2,1)S(1)} %constant_dynamic-slice_fusion.1), channel_id=1, source_target_pairs={{0,1},{1,0},{2,3},{3,2},{4,5},{5,4},{6,7},{7,6},{8,9},{9,8},{10,11... | collective-permute-start | bytes 1572872 | tf_op jit(solution)/shard_map/ppermute | solution.py:194
  199.8 13.9 %collective-permute-start.34 = (bf16[128,2048]{1,0:T(8,128)(2,1)S(1)}, bf16[128,2048]{1,0:T(8,128)(2,1)S(1)}, u32[]{:S(2)}, u32[]{:S(2)}) collective-permute-start(bf16[128,2048]{1,0:T(8,128)(2,1)S(1)} %constant_dynamic-slice_fusion), channel_id=1, source_target_pairs={{0,1},{1,0},{2,3},{3,2},{4,5},{5,4},{6,7},{7,6},{8,9},{9,8},{10,11... | collective-permute-start | bytes 1572872 | tf_op jit(solution)/shard_map/ppermute | solution.py:194
  (19 other events, 33.9 us)

commit v3 on v2

--- a/solution.py
+++ b/solution.py
@@ -405,10 +405,12 @@
     part_k = first_hop(*terms_k, bits, parts)
     up_a = third_hop(up_a, bits, False)
     up_b = third_hop(up_b, bits, True)
+    part_q = second_hop(part_q, bits, False)
+    part_k = second_hop(part_k, bits, True)
     up_a, up_b, part_q, part_k = lax.optimization_barrier((up_a, up_b, part_q, part_k))
     up_joint = collect(joint_sum(up_a, up_b), "dp")
-    part_q = third_hop(second_hop(part_q, bits, False), bits, False)
-    part_k = third_hop(second_hop(part_k, bits, True), bits, True)
+    part_q = third_hop(part_q, bits, False)
+    part_k = third_hop(part_k, bits, True)
     qk_joint = joint_sum(part_q, part_k)
     up_joint, qk_joint = lax.optimization_barrier((up_joint, qk_joint))
     grad_up = collect(up_joint, "ctx").astype(F32)

time: 217 us -> 210 us (0.968)
  waiting for transfers between devices: 72.7 us -> 65.2 us
  starting transfers between devices: 45 us -> 48.9 us
  other arithmetic: 16.2 us -> 13.5 us
    ppermute x18, waiting for transfers between devices: 42.8 us -> 36.2 us  [turned(): return lax.ppermute(x, axis, [(i, (i + by) % n) for i in range(n)])]
    ppermute x18, starting transfers between devices: 24.7 us -> 28.8 us  [turned(): return lax.ppermute(x, axis, [(i, (i + by) % n) for i in range(n)])]
    add x2, other arithmetic: 5.88 us -> 3.23 us  [first_hop(): x = left + flipped(right, bits[0]).astype(F32)]
    unnamed x106 -> x102, local copies, waits for them, and re-layouts: 12.7 us -> 12.8 us
  transfers between devices with their start and end apart: 36 -> 36, of which waited for: 20 -> 16; matrix products, arithmetic and copies ran while one was open for 9% -> 9% of each run, Pallas kernels for 22% -> 23%
where the time goes in v3:
time: 210 us; the launch traced here: 209 us
  waiting for transfers between devices  65.2 us (31%)
  starting transfers between devices  48.9 us (23%)
  Pallas kernels  47.7 us (23%)
  local copies, waits for them, and re-layouts  20.7 us (10%)
  other arithmetic  13.5 us (6%)
  matrix products  11.8 us (6%)
    ppermute x18, waiting for transfers between devices, turned(): return lax.ppermute(x, axis, [(i, (i + by) % n) for i in range(n)])  36.2 us
    ppermute x18, starting transfers between devices, turned(): return lax.ppermute(x, axis, [(i, (i + by) % n) for i in range(n)])  28.8 us
    ppermute x14, waiting for transfers between devices, flipped(): return lax.ppermute(x, 'fsdp', [(i, i ^ bit) for i in range(n)])  23.5 us
    unnamed x102, local copies, waits for them, and re-layouts  12.8 us
    dot_general x8, matrix products, mm(): lax.dot_general(a, b, (((1,), (0,)), ((), ())), preferred_element_type=F32)  11.8 us
    ppermute x14, starting transfers between devices, flipped(): return lax.ppermute(x, 'fsdp', [(i, i ^ bit) for i in range(n)])  10.4 us
    pallas_call x1, Pallas kernels, per_device(): pl.pallas_call(functools.partial(token_grad_kernel, width, parts), grid_s...  10 us
    ppermute x4, starting transfers between devices, shifted(): lax.ppermute(x, axis, [(i, i + by) for i in range(n) if 0 <= i + by < n])  9.71 us
  transfers between devices with their start and end apart: 36, of which 16 were waited for; matrix products, arithmetic and copies ran while one was open for 9% of the time, Pallas kernels for 23%

profile of v3, /device:TPU:0, one launch (start us, length us, event | category | flops | bytes accessed | tf_op | source)
XLA Modules:
  0.0 209.2 jit_solution(16882901679109918521)
XLA Ops:
  0.7 1.2 constant_dynamic-update-slice_fusion.1
  1.8 1.1 constant_dynamic-update-slice_fusion.refs_4_.refs_0_
  2.9 3.0 %collective-permute-start.1 = (bf16[256,2048]{1,0:T(8,128)(2,1)S(1)}, bf16[256,2048]{1,0:T(8,128)(2,1)S(1)}, u32[]{:S(2)}, u32[]{:S(2)}) collective-permute-start(bf16[256,2048]{1,0:T(8,128)(2,1)S(1)} %constant_dynamic-update-slice_fusion.refs_4_.refs_0_), channel_id=1, source_target_pairs={{0,4},{2,6},{4,0},{6,2},{1,5},{3,7},{5,1},{7,3},{8,12},{10,14},{12... | collective-permute-start | bytes 3145736 | tf_op jit(solution)/shard_map/ppermute | solution.py:189
  5.9 3.4 %collective-permute-start = (bf16[1,1024]{1,0:T(2,128)(2,1)S(1)}, bf16[1,1024]{1,0:T(2,128)(2,1)S(1)}, u32[]{:S(2)}, u32[]{:S(2)}) collective-permute-start(bf16[1,1024]{1,0:T(2,128)(2,1)S(1)} %slice_bitcast_fusion.2), channel_id=1, source_target_pairs={{0,1},{2,3},{4,5},{6,7},{8,9},{10,11},{12,13},{14,15},{16,17},{18,... | collective-permute-start | bytes 6152 | tf_op jit(solution)/shard_map/ppermute | solution.py:199
  9.8 19.3 %collective-permute-done.1.refs_5_.refs_1_ = bf16[256,2048]{1,0:T(8,128)(2,1)S(1)} collective-permute-done((bf16[256,2048]{1,0:T(8,128)(2,1)S(1)}, bf16[256,2048]{1,0:T(8,128)(2,1)S(1)}, u32[]{:S(2)}, u32[]{:S(2)}) %collective-permute-start.1) | collective-permute-done | bytes 1048608 | tf_op jit(solution)/shard_map/ppermute | solution.py:189
  30.3 1.2 fusion.47
  31.8 1.8 collective-permute-start.7
  33.6 5.6 %route.1 = (f32[512,1024]{1,0:T(8,128)}, f32[512,1024]{1,0:T(8,128)}, f32[512,1]{1,0:T(8,128)S(1)}, f32[512,1]{1,0:T(8,128)S(1)}, f32[512,1]{1,0:T(8,128)S(1)}, /*index=5*/f32[512,1]{1,0:T(8,128)S(1)}) custom-call(bf16[512,1024]{1,0:T(8,128)(2,1)S(1)} %get-tuple-element.112.refs_0_.tok, bf16[512,1024]{1,0:T(8,128)(2,1)S(1)} %get-tuple-element.110.refs_1_, ...), custom_call_target="tpu_custom_call" | custom-call | flops 2147483648 | bytes 10485760 | tf_op jit(solution)/shard_map/route/pallas_call | solution.py:301
  39.2 5.8 %adjoint.1 = (f32[512,2048]{1,0:T(8,128)}, f32[512,16]{1,0:T(8,128)S(1)}, f32[1,2048]{1,0:T(1,128)S(1)}, f32[1,16]{1,0:T(1,128)}) custom-call(f32[512,1]{1,0:T(8,128)S(1)} %get-tuple-element.53.mp, f32[1,16]{1,0:T(1,128)S(1)} %bitcast.106, bf16[512,2048]{1,0:T(8,128)(2,1)S(1)} %bitcast.110), custom_call_target="tpu_custom_call" | custom-call | flops 1073741824 | bytes 6291456 | tf_op jit(solution)/shard_map/adjoint/pallas_call | solution.py:318
  45.0 1.3 collective-permute-start.4
  46.3 4.2 %collective-permute-done.4.adj_in = f32[1,2048]{1,0:T(1,128)S(1)} collective-permute-done((f32[1,2048]{1,0:T(1,128)S(1)}, f32[1,2048]{1,0:T(1,128)S(1)}, u32[]{:S(2)}, u32[]{:S(2)}) %collective-permute-start.4) | collective-permute-done | bytes 8224 | tf_op jit(solution)/shard_map/ppermute | solution.py:199
  50.5 4.6 %value_grad.1.dv = bf16[512,2048]{1,0:T(8,128)(2,1)S(1)} custom-call(f32[512,2048]{1,0:T(8,128)} %get-tuple-element.55.adj, f32[512,16]{1,0:T(8,128)S(1)} %get-tuple-element.56.tail, f32[512,1]{1,0:T(8,128)S(1)} %get-tuple-element.53.mp, f32[1,16]{1,0:T(1,128)S(1)} %bitcast.107, f32[1,2048]{1,0:T(1,128)S(1)} %collective-permute-done.4.adj_in), custom_call_target="tpu_custom_call" | custom-call | flops 4194304 | bytes 6291456 | tf_op jit(solution)/shard_map/value_grad/pallas_call | solution.py:338
  58.7 2.1 convert_add_fusion.2
  61.7 1.1 copy-done.10
  63.2 1.0 copy-done.12
  65.9 2.1 %fusion.11 = bf16[2,128,1024]{2,1,0:T(8,128)(2,1)} fusion(f32[2,2,128,1024]{3,2,1,0:T(8,128)} %bitcast.113, s32[]{:T(128)S(6)} %select_n.72), kind=kLoop, calls=%fused_computation.47 | loop fusion | bytes 1048580 | tf_op jit(solution)/shard_map/convert_element_type | solution.py:213
  68.4 1.2 copy-done.11
  69.6 1.2 copy-done.13
  70.8 3.9 %values.1 = f32[512,2048]{1,0:T(8,128)} custom-call(bf16[512,1024]{1,0:T(8,128)(2,1)S(1)} %get-tuple-element.112.refs_0_.tok, bf16[256,2048]{1,0:T(8,128)(2,1)S(1)} %copy-done.7, bf16[256,2048]{1,0:T(8,128)(2,1)S(1)} %copy-done.9, bf16[256,2048]{1,0:T(8,128)(2,1)S(1)} %copy-done.11, bf16[256,2048]{1,0:T(8,128)(2,1)S(1)} %copy-done.13), custom_call_target="tpu_custom_call" | custom-call | flops 2147483648 | bytes 8388608 | tf_op jit(solution)/shard_map/values/pallas_call | solution.py:364
  74.8 8.5 %state.1 = (f32[512,2048]{1,0:T(8,128)S(1)}, f32[512,2048]{1,0:T(8,128)}, f32[512,16]{1,0:T(8,128)S(1)}, f32[512,16]{1,0:T(8,128)S(1)}, f32[1,2048]{1,0:T(1,128)S(1)}) custom-call(f32[512,1]{1,0:T(8,128)S(1)} %copy-done.25, f32[1,16]{1,0:T(1,128)S(1)} %bitcast.108, f32[512,2048]{1,0:T(8,128)} %values.1), custom_call_target="tpu_custom_call" | custom-call | flops 1610612736 | bytes 12582912 | tf_op jit(solution)/shard_map/state/pallas_call | solution.py:375
  83.3 2.1 copy-done.1
  86.8 3.7 %collective-permute-start.10 = (f32[1,2048]{1,0:T(1,128)S(1)}, f32[1,2048]{1,0:T(1,128)S(1)}, u32[]{:S(2)}, u32[]{:S(2)}) collective-permute-start(f32[1,2048]{1,0:T(1,128)S(1)} %get-tuple-element.67), channel_id=1, source_target_pairs={{0,1},{2,3},{4,5},{6,7},{8,9},{10,11},{12,13},{14,15},{16,17},{18,... | collective-permute-start | bytes 24584 | tf_op jit(solution)/shard_map/ppermute | solution.py:199
  90.6 1.2 collective-permute-done.10.st_in
  91.8 0.9 copy-done.19
  92.7 0.9 copy-done.21
  93.7 0.9 copy-done.23
  94.6 9.2 %finish.1 = (bf16[512,2048]{1,0:T(8,128)(2,1)}, bf16[512,1024]{1,0:T(8,128)(2,1)S(1)}, bf16[512,1024]{1,0:T(8,128)(2,1)S(1)}) custom-call(f32[512,2048]{1,0:T(8,128)} %copy-done.1, f32[512,2048]{1,0:T(8,128)} %get-tuple-element.64.diff, f32[512,2048]{1,0:T(8,128)} %get-tuple-element.55.adj, f32[512,16]{1,0:T(8,128)S(1)} %get-tuple-element.56.tail, ...), custom_call_target="tpu_custom_call" | custom-call | flops 20971520 | bytes 20971520 | tf_op jit(solution)/shard_map/finish/pallas_call | solution.py:388
  103.8 1.3 convert_add_fusion.4
  105.6 2.2 %bitcast_add_fusion.1 = f32[2,128,1024]{2,1,0:T(8,128)} fusion(bf16[2,128,1024]{2,1,0:T(8,128)(2,1)} %collective-permute-done.12, f32[2,2,128,1024]{3,2,1,0:T(8,128)S(1)} %bitcast.114, s32[]{:T(128)S(6)} %select_n.71), kind=kLoop, calls=%fused_computation.36 | loop fusion | flops 524288 | bytes 2621444 | tf_op jit(solution)/shard_map/add | solution.py:213
  107.8 1.7 convolution_convert_fusion
  109.5 2.1 fusion.15
  111.5 1.7 convolution_convert_fusion.1
  113.3 2.0 fusion.20
  116.2 1.2 slice.150
  117.5 1.2 collective-permute-start.15
  118.7 2.4 %collective-permute-start.14 = (bf16[1,128,1024]{2,1,0:T(8,128)(2,1)S(1)}, bf16[1,128,1024]{2,1,0:T(8,128)(2,1)S(1)}, u32[]{:S(2)}, u32[]{:S(2)}) collective-permute-start(bf16[1,128,1024]{2,1,0:T(8,128)(2,1)S(1)} %fusion.24), channel_id=1, source_target_pairs={{0,1},{1,0},{2,3},{3,2},{4,5},{5,4},{6,7},{7,6},{8,9},{9,8},{10,11... | collective-permute-start | bytes 786440 | tf_op jit(solution)/shard_map/ppermute | solution.py:194
  121.1 1.3 collective-permute-start.13
  122.4 1.6 convert_add_fusion
  124.0 2.7 %collective-permute-start.19 = (bf16[2,128,1024]{2,1,0:T(8,128)(2,1)S(1)}, bf16[2,128,1024]{2,1,0:T(8,128)(2,1)S(1)}, u32[]{:S(2)}, u32[]{:S(2)}) collective-permute-start(bf16[2,128,1024]{2,1,0:T(8,128)(2,1)S(1)} %fusion.12), channel_id=1, source_target_pairs={{0,1},{1,0},{2,3},{3,2},{4,5},{5,4},{6,7},{7,6},{8,9},{9,8},{10,11... | collective-permute-start | bytes 1572872 | tf_op jit(solution)/shard_map/ppermute | solution.py:194
  126.7 1.7 convert_add_fusion.1
  129.7 8.9 %collective-permute-done.19 = bf16[2,128,1024]{2,1,0:T(8,128)(2,1)S(1)} collective-permute-done((bf16[2,128,1024]{2,1,0:T(8,128)(2,1)S(1)}, bf16[2,128,1024]{2,1,0:T(8,128)(2,1)S(1)}, u32[]{:S(2)}, u32[]{:S(2)}) %collective-permute-start.19) | collective-permute-done | bytes 524320 | tf_op jit(solution)/shard_map/ppermute | solution.py:194
  138.7 2.5 %collective-permute-done.17 = bf16[1,256,1024]{2,1,0:T(8,128)(2,1)S(1)} collective-permute-done((bf16[1,256,1024]{2,1,0:T(8,128)(2,1)S(1)}, bf16[1,256,1024]{2,1,0:T(8,128)(2,1)S(1)}, u32[]{:S(2)}, u32[]{:S(2)}) %collective-permute-start.17) | collective-permute-done | bytes 524320 | tf_op jit(solution)/shard_map/ppermute | solution.py:189
  141.6 1.6 collective-permute-start.20
  143.2 2.6 %collective-permute-start.21 = (bf16[1,32,2048]{2,1,0:T(8,128)(2,1)S(1)}, bf16[1,32,2048]{2,1,0:T(8,128)(2,1)S(1)}, u32[]{:S(2)}, u32[]{:S(2)}) collective-permute-start(bf16[1,32,2048]{2,1,0:T(8,128)(2,1)S(1)} %get-tuple-element.108), channel_id=1, source_target_pairs={{0,16},{8,24},{16,0},{24,8},{1,17},{9,25},{17,1},{25,9},{2,18},{10... | collective-permute-start | bytes 393224 | tf_op jit(solution)/shard_map/ppermute | solution.py:194
  145.8 1.3 collective-permute-start.22
  147.7 0.9 collective-permute-start.27
  148.7 1.1 collective-permute-done.20
  149.8 3.3 %collective-permute-done.21 = bf16[1,32,2048]{2,1,0:T(8,128)(2,1)S(1)} collective-permute-done((bf16[1,32,2048]{2,1,0:T(8,128)(2,1)S(1)}, bf16[1,32,2048]{2,1,0:T(8,128)(2,1)S(1)}, u32[]{:S(2)}, u32[]{:S(2)}) %collective-permute-start.21) | collective-permute-done | bytes 131104 | tf_op jit(solution)/shard_map/ppermute | solution.py:194
  153.2 3.9 %collective-permute-start.23 = (bf16[32,2048]{1,0:T(8,128)(2,1)S(1)}, bf16[32,2048]{1,0:T(8,128)(2,1)S(1)}, u32[]{:S(2)}, u32[]{:S(2)}) collective-permute-start(bf16[32,2048]{1,0:T(8,128)(2,1)S(1)} %get-tuple-element.96), channel_id=1, source_target_pairs={{0,24},{8,0},{16,8},{24,16},{1,25},{9,1},{17,9},{25,17},{2,26},{10... | collective-permute-start | bytes 393224 | tf_op jit(solution)/shard_map/ppermute | solution.py:194
  158.0 2.9 %collective-permute-start.28 = (bf16[1,32,2048]{2,1,0:T(8,128)(2,1)S(1)}, bf16[1,32,2048]{2,1,0:T(8,128)(2,1)S(1)}, u32[]{:S(2)}, u32[]{:S(2)}) collective-permute-start(bf16[1,32,2048]{2,1,0:T(8,128)(2,1)S(1)} %get-tuple-element.103), channel_id=1, source_target_pairs={{0,8},{8,16},{16,24},{24,0},{1,9},{9,17},{17,25},{25,1},{2,10},{10... | collective-permute-start | bytes 393224 | tf_op jit(solution)/shard_map/ppermute | solution.py:194
  160.9 1.3 collective-permute-start.29
  162.2 3.0 %collective-permute-start.30 = (bf16[1,32,2048]{2,1,0:T(8,128)(2,1)S(1)}, bf16[1,32,2048]{2,1,0:T(8,128)(2,1)S(1)}, u32[]{:S(2)}, u32[]{:S(2)}) collective-permute-start(bf16[1,32,2048]{2,1,0:T(8,128)(2,1)S(1)} %get-tuple-element.104), channel_id=1, source_target_pairs={{0,24},{8,0},{16,8},{24,16},{1,25},{9,1},{17,9},{25,17},{2,26},{10... | collective-permute-start | bytes 393224 | tf_op jit(solution)/shard_map/ppermute | solution.py:194
  165.3 10.5 %collective-permute-done.24 = bf16[32,2048]{1,0:T(8,128)(2,1)S(1)} collective-permute-done((bf16[32,2048]{1,0:T(8,128)(2,1)S(1)}, bf16[32,2048]{1,0:T(8,128)(2,1)S(1)}, u32[]{:S(2)}, u32[]{:S(2)}) %collective-permute-start.24) | collective-permute-done | bytes 131104 | tf_op jit(solution)/shard_map/ppermute | solution.py:194
  176.0 2.6 %collective-permute-done.29 = bf16[1,32,2048]{2,1,0:T(8,128)(2,1)S(1)} collective-permute-done((bf16[1,32,2048]{2,1,0:T(8,128)(2,1)S(1)}, bf16[1,32,2048]{2,1,0:T(8,128)(2,1)S(1)}, u32[]{:S(2)}, u32[]{:S(2)}) %collective-permute-start.29) | collective-permute-done | bytes 131104 | tf_op jit(solution)/shard_map/ppermute | solution.py:194
  178.8 1.6 collective-permute-start.31
  180.4 1.8 collective-permute-start.32
  182.2 1.0 collective-permute-start.35
  183.2 1.0 collective-permute-done.31
  184.3 8.6 %collective-permute-done.32 = bf16[32,2048]{1,0:T(8,128)(2,1)S(1)} collective-permute-done((bf16[32,2048]{1,0:T(8,128)(2,1)S(1)}, bf16[32,2048]{1,0:T(8,128)(2,1)S(1)}, u32[]{:S(2)}, u32[]{:S(2)}) %collective-permute-start.32) | collective-permute-done | bytes 131104 | tf_op jit(solution)/shard_map/ppermute | solution.py:194
  193.0 1.2 collective-permute-start.34
  194.3 10.0 %token_grad.1 = bf16[512,1024]{1,0:T(8,128)(2,1)} custom-call(s32[4]{0:T(128)S(1)} %pad_add_fusion.place, bf16[512,1024]{1,0:T(8,128)(2,1)S(1)} %get-tuple-element.81.dq, bf16[512,1024]{1,0:T(8,128)(2,1)S(1)} %pad_maximum_fusion.2.dk, bf16[512,2048]{1,0:T(8,128)(2,1)} %copy-done, bf16[256,2048]{1,0:T(8,128)(2,1)S(1)} %copy-done.27, ...), custom_call_target="tpu_custom_call" | custom-call | flops 4294967296 | bytes 8388608 | tf_op jit(solution)/shard_map/token_grad/pallas_call | solution.py:422
  204.3 2.4 %fusion.2 = f32[256,2048]{1,0:T(8,128)} fusion(s32[]{:T(128)S(6)} %select_n.78, bf16[128,2048]{1,0:T(8,128)(2,1)S(1)} %constant_dynamic-slice_fusion.1, bf16[128,2048]{1,0:T(8,128)(2,1)S(1)} %collective-permute-done.35), kind=kLoop, calls=%fused_computation.20 | loop fusion | flops 3145728 | bytes 3145732 | tf_op jit(solution)/shard_map/convert_element_type | solution.py:416
  206.7 1.1 fusion.5
  207.7 1.5 fusion.50
  (171 shorter events, 15.1 us)
Async XLA Ops:
  0.6 5.3 %copy-start.39 = (bf16[1,512,1024]{2,1,0:T(8,128)(2,1)S(1)}, bf16[1,512,1024]{2,1,0:T(8,128)(2,1)}, u32[]{:S(2)}) copy-start(bf16[1,512,1024]{2,1,0:T(8,128)(2,1)} %param.7) | copy-start | bytes 3145732
  0.6 8.8 %copy-start.43 = (s32[1,512]{1,0:T(1,128)S(1)}, s32[1,512]{1,0:T(1,128)}, u32[]{:S(2)}) copy-start(s32[1,512]{1,0:T(1,128)} %param.8) | copy-start | bytes 6148
  2.9 30.6 %copy-start.26 = (bf16[256,2048]{1,0:T(8,128)(2,1)}, bf16[256,2048]{1,0:T(8,128)(2,1)S(1)}, u32[]{:S(2)}) copy-start(bf16[256,2048]{1,0:T(8,128)(2,1)S(1)} %constant_dynamic-update-slice_fusion.refs_4_.refs_0_) | copy-start | bytes 3145732
  2.9 26.2 %collective-permute-start.1 = (bf16[256,2048]{1,0:T(8,128)(2,1)S(1)}, bf16[256,2048]{1,0:T(8,128)(2,1)S(1)}, u32[]{:S(2)}, u32[]{:S(2)}) collective-permute-start(bf16[256,2048]{1,0:T(8,128)(2,1)S(1)} %constant_dynamic-update-slice_fusion.refs_4_.refs_0_), channel_id=1, source_target_pairs={{0,4},{2,6},{4,0},{6,2},{1,5},{3,7},{5,1},{7,3},{8,12},{10,14},{12... | collective-permute-start | bytes 3145736 | tf_op jit(solution)/shard_map/ppermute | solution.py:189
  5.9 25.6 %collective-permute-start.2 = (bf16[256,2048]{1,0:T(8,128)(2,1)S(1)}, bf16[256,2048]{1,0:T(8,128)(2,1)}, u32[]{:S(2)}, u32[]{:S(2)}) collective-permute-start(bf16[256,2048]{1,0:T(8,128)(2,1)S(1)} %constant_dynamic-update-slice_fusion.refs_4_.refs_0_), channel_id=1, source_target_pairs={{0,2},{2,0},{4,6},{6,4},{1,3},{3,1},{5,7},{7,5},{8,10},{10,8},{12,... | collective-permute-start | bytes 3145736 | tf_op jit(solution)/shard_map/ppermute | solution.py:189
  5.9 23.6 %collective-permute-start = (bf16[1,1024]{1,0:T(2,128)(2,1)S(1)}, bf16[1,1024]{1,0:T(2,128)(2,1)S(1)}, u32[]{:S(2)}, u32[]{:S(2)}) collective-permute-start(bf16[1,1024]{1,0:T(2,128)(2,1)S(1)} %slice_bitcast_fusion.2), channel_id=1, source_target_pairs={{0,1},{2,3},{4,5},{6,7},{8,9},{10,11},{12,13},{14,15},{16,17},{18,... | collective-permute-start | bytes 6152 | tf_op jit(solution)/shard_map/ppermute | solution.py:199
  9.7 19.7 %copy-start.40 = (bf16[1,512,1024]{2,1,0:T(8,128)(2,1)S(1)}, bf16[1,512,1024]{2,1,0:T(8,128)(2,1)}, u32[]{:S(2)}) copy-start(bf16[1,512,1024]{2,1,0:T(8,128)(2,1)} %param.7) | copy-start | bytes 3145732
  29.1 4.4 %copy-start.30 = (bf16[256,2048]{1,0:T(8,128)(2,1)}, bf16[256,2048]{1,0:T(8,128)(2,1)S(1)}, u32[]{:S(2)}) copy-start(bf16[256,2048]{1,0:T(8,128)(2,1)S(1)} %collective-permute-done.1.refs_5_.refs_1_) | copy-start | bytes 3145732
  29.1 2.7 %collective-permute-start.3 = (bf16[256,2048]{1,0:T(8,128)(2,1)S(1)}, bf16[256,2048]{1,0:T(8,128)(2,1)S(1)}, u32[]{:S(2)}, u32[]{:S(2)}) collective-permute-start(bf16[256,2048]{1,0:T(8,128)(2,1)S(1)} %collective-permute-done.1.refs_5_.refs_1_), channel_id=1, source_target_pairs={{0,2},{2,0},{4,6},{6,4},{1,3},{3,1},{5,7},{7,5},{8,10},{10,8},{12,... | collective-permute-start | bytes 3145736 | tf_op jit(solution)/shard_map/ppermute | solution.py:189
  29.4 31.4 %copy-start.34 = (bf16[1024,512]{0,1:T(8,128)(2,1)}, bf16[1024,512]{0,1:T(8,128)(2,1)S(1)}, u32[]{:S(2)}) copy-start(bf16[1024,512]{0,1:T(8,128)(2,1)S(1)} %get-tuple-element.54) | copy-start | bytes 3145732
  29.4 4.1 %copy-start.2 = (f32[512,1]{1,0:T(8,128)}, f32[512,1]{1,0:T(8,128)S(1)}, u32[]{:S(2)}) copy-start(f32[512,1]{1,0:T(8,128)S(1)} %fusion.38.refs_2_.marked) | copy-start | bytes 6148
  29.5 4.0 %copy-start.4 = (f32[512,1]{1,0:T(8,128)}, f32[512,1]{1,0:T(8,128)S(1)}, u32[]{:S(2)}) copy-start(f32[512,1]{1,0:T(8,128)S(1)} %fusion.37.refs_3_.opening) | copy-start | bytes 6148
  31.8 25.6 %collective-permute-start.7 = (bf16[256,2048]{1,0:T(8,128)(2,1)S(1)}, bf16[256,2048]{1,0:T(8,128)(2,1)S(1)}, u32[]{:S(2)}, u32[]{:S(2)}) collective-permute-start(bf16[256,2048]{1,0:T(8,128)(2,1)S(1)} %copy-done.6), channel_id=1, source_target_pairs={{0,4},{2,6},{4,0},{6,2},{1,5},{3,7},{5,1},{7,3},{8,12},{10,14},{12... | collective-permute-start | bytes 3145736 | tf_op jit(solution)/shard_map/ppermute | solution.py:189
  33.5 5.6 %copy-start.28 = (f32[16]{0:T(128)S(1)}, f32[16]{0:T(128)}, u32[]{:S(2)}) copy-start(f32[16]{0:T(128)} %param.9) | copy-start | bytes 196
  33.5 5.6 %copy-start.29 = (bf16[1,512,2048]{2,1,0:T(8,128)(2,1)S(1)}, bf16[1,512,2048]{2,1,0:T(8,128)(2,1)}, u32[]{:S(2)}) copy-start(bf16[1,512,2048]{2,1,0:T(8,128)(2,1)} %param.13) | copy-start | bytes 6291460
  39.1 16.0 %copy-start.14 = (f32[512,1]{1,0:T(8,128)}, f32[512,1]{1,0:T(8,128)S(1)}, u32[]{:S(2)}) copy-start(f32[512,1]{1,0:T(8,128)S(1)} %get-tuple-element.70.iq) | copy-start | bytes 6148
  39.1 16.0 %copy-start.16 = (f32[512,1]{1,0:T(8,128)}, f32[512,1]{1,0:T(8,128)S(1)}, u32[]{:S(2)}) copy-start(f32[512,1]{1,0:T(8,128)S(1)} %get-tuple-element.71.ik) | copy-start | bytes 6148
  39.1 16.0 %copy-start.18 = (f32[512,1]{1,0:T(8,128)}, f32[512,1]{1,0:T(8,128)S(1)}, u32[]{:S(2)}) copy-start(f32[512,1]{1,0:T(8,128)S(1)} %get-tuple-element.72.cos) | copy-start | bytes 6148
  39.1 16.1 %copy-start.24 = (f32[512,1]{1,0:T(8,128)}, f32[512,1]{1,0:T(8,128)S(1)}, u32[]{:S(2)}) copy-start(f32[512,1]{1,0:T(8,128)S(1)} %get-tuple-element.53.mp) | copy-start | bytes 6148
  45.0 5.5 %collective-permute-start.4 = (f32[1,2048]{1,0:T(1,128)S(1)}, f32[1,2048]{1,0:T(1,128)S(1)}, u32[]{:S(2)}, u32[]{:S(2)}) collective-permute-start(f32[1,2048]{1,0:T(1,128)S(1)} %get-tuple-element.57), channel_id=1, source_target_pairs={{1,0},{3,2},{5,4},{7,6},{9,8},{11,10},{13,12},{15,14},{17,16},{19,... | collective-permute-start | bytes 24584 | tf_op jit(solution)/shard_map/ppermute | solution.py:199
  55.2 5.5 %copy-start = (bf16[512,2048]{1,0:T(8,128)(2,1)}, bf16[512,2048]{1,0:T(8,128)(2,1)S(1)}, u32[]{:S(2)}) copy-start(bf16[512,2048]{1,0:T(8,128)(2,1)S(1)} %value_grad.1.dv) | copy-start | bytes 6291460
  55.9 2.7 %collective-permute-start.6 = (bf16[512,1024]{1,0:T(8,128)(2,1)S(1)}, bf16[512,1024]{1,0:T(8,128)(2,1)S(1)}, u32[]{:S(2)}, u32[]{:S(2)}) collective-permute-start(bf16[512,1024]{1,0:T(8,128)(2,1)S(1)} %convolution_convert_fusion.2), channel_id=1, source_target_pairs={{0,2},{2,0},{4,6},{6,4},{1,3},{3,1},{5,7},{7,5},{8,10},{10,8},{12,... | collective-permute-start | bytes 3145736 | tf_op jit(solution)/shard_map/ppermute | solution.py:189
  56.7 4.0 %collective-permute-start.5 = (bf16[512,1024]{1,0:T(8,128)(2,1)S(1)}, bf16[512,1024]{1,0:T(8,128)(2,1)S(1)}, u32[]{:S(2)}, u32[]{:S(2)}) collective-permute-start(bf16[512,1024]{1,0:T(8,128)(2,1)S(1)} %convolution_convert_fusion.3), channel_id=1, source_target_pairs={{0,2},{2,0},{4,6},{6,4},{1,3},{3,1},{5,7},{7,5},{8,10},{10,8},{12,... | collective-permute-start | bytes 3145736 | tf_op jit(solution)/shard_map/ppermute | solution.py:189
  57.3 4.3 %collective-permute-start.8 = (bf16[256,2048]{1,0:T(8,128)(2,1)S(1)}, bf16[256,2048]{1,0:T(8,128)(2,1)S(1)}, u32[]{:S(2)}, u32[]{:S(2)}) collective-permute-start(bf16[256,2048]{1,0:T(8,128)(2,1)S(1)} %copy-done.6), channel_id=1, source_target_pairs={{0,2},{2,0},{4,6},{6,4},{1,3},{3,1},{5,7},{7,5},{8,10},{10,8},{12,... | collective-permute-start | bytes 3145736 | tf_op jit(solution)/shard_map/ppermute | solution.py:189
  57.4 5.8 %collective-permute-start.9 = (bf16[256,2048]{1,0:T(8,128)(2,1)S(1)}, bf16[256,2048]{1,0:T(8,128)(2,1)S(1)}, u32[]{:S(2)}, u32[]{:S(2)}) collective-permute-start(bf16[256,2048]{1,0:T(8,128)(2,1)S(1)} %collective-permute-done.7.refs_1_.refs_5_), channel_id=1, source_target_pairs={{0,2},{2,0},{4,6},{6,4},{1,3},{3,1},{5,7},{7,5},{8,10},{10,8},{12,... | collective-permute-start | bytes 3145736 | tf_op jit(solution)/shard_map/ppermute | solution.py:189
  61.5 6.9 %copy-start.7 = (bf16[256,2048]{1,0:T(8,128)(2,1)S(1)}, bf16[256,2048]{1,0:T(8,128)(2,1)}, u32[]{:S(2)}) copy-start(bf16[256,2048]{1,0:T(8,128)(2,1)} %refs_4_) | copy-start | bytes 3145732
  61.5 6.9 %copy-start.9 = (bf16[256,2048]{1,0:T(8,128)(2,1)S(1)}, bf16[256,2048]{1,0:T(8,128)(2,1)}, u32[]{:S(2)}) copy-start(bf16[256,2048]{1,0:T(8,128)(2,1)} %copy-done.8) | copy-start | bytes 3145732
  65.0 38.8 %collective-permute-start.11 = (bf16[1,256,1024]{2,1,0:T(8,128)(2,1)}, bf16[1,256,1024]{2,1,0:T(8,128)(2,1)}, u32[]{:S(2)}, u32[]{:S(2)}) collective-permute-start(bf16[1,256,1024]{2,1,0:T(8,128)(2,1)} %slice.148), channel_id=1, source_target_pairs={{0,4},{2,6},{4,0},{6,2},{1,5},{3,7},{5,1},{7,3},{8,12},{10,14},{12... | collective-permute-start | bytes 1572872 | tf_op jit(solution)/shard_map/ppermute | solution.py:189
  68.0 37.1 %collective-permute-start.12 = (bf16[2,128,1024]{2,1,0:T(8,128)(2,1)}, bf16[2,128,1024]{2,1,0:T(8,128)(2,1)}, u32[]{:S(2)}, u32[]{:S(2)}) collective-permute-start(bf16[2,128,1024]{2,1,0:T(8,128)(2,1)} %fusion.11), channel_id=1, source_target_pairs={{0,1},{1,0},{2,3},{3,2},{4,5},{5,4},{6,7},{7,6},{8,9},{9,8},{10,11... | collective-permute-start | bytes 1572872 | tf_op jit(solution)/shard_map/ppermute | solution.py:194
  70.8 3.9 %copy-start.25 = (f32[512,1]{1,0:T(8,128)S(1)}, f32[512,1]{1,0:T(8,128)}, u32[]{:S(2)}) copy-start(f32[512,1]{1,0:T(8,128)} %copy-done.24) | copy-start | bytes 6148
  74.8 17.0 %copy-start.3 = (f32[512,1]{1,0:T(8,128)S(1)}, f32[512,1]{1,0:T(8,128)}, u32[]{:S(2)}) copy-start(f32[512,1]{1,0:T(8,128)} %copy-done.2) | copy-start | bytes 6148
  74.8 17.0 %copy-start.5 = (f32[512,1]{1,0:T(8,128)S(1)}, f32[512,1]{1,0:T(8,128)}, u32[]{:S(2)}) copy-start(f32[512,1]{1,0:T(8,128)} %copy-done.4) | copy-start | bytes 6148
  74.8 17.0 %copy-start.15 = (f32[512,1]{1,0:T(8,128)S(1)}, f32[512,1]{1,0:T(8,128)}, u32[]{:S(2)}) copy-start(f32[512,1]{1,0:T(8,128)} %copy-done.14) | copy-start | bytes 6148
  74.8 17.0 %copy-start.17 = (f32[512,1]{1,0:T(8,128)S(1)}, f32[512,1]{1,0:T(8,128)}, u32[]{:S(2)}) copy-start(f32[512,1]{1,0:T(8,128)} %copy-done.16) | copy-start | bytes 6148
  86.8 4.9 %collective-permute-start.10 = (f32[1,2048]{1,0:T(1,128)S(1)}, f32[1,2048]{1,0:T(1,128)S(1)}, u32[]{:S(2)}, u32[]{:S(2)}) collective-permute-start(f32[1,2048]{1,0:T(1,128)S(1)} %get-tuple-element.67), channel_id=1, source_target_pairs={{0,1},{2,3},{4,5},{6,7},{8,9},{10,11},{12,13},{14,15},{16,17},{18,... | collective-permute-start | bytes 24584 | tf_op jit(solution)/shard_map/ppermute | solution.py:199
  94.6 9.2 %copy-start.37 = (f32[512,1024]{1,0:T(8,128)S(1)}, f32[512,1024]{1,0:T(8,128)}, u32[]{:S(2)}) copy-start(f32[512,1024]{1,0:T(8,128)} %copy-done.36) | copy-start | bytes 6291460
  103.8 4.0 %copy-start.42 = (bf16[1024,512]{0,1:T(8,128)(2,1)S(1)}, bf16[1024,512]{0,1:T(8,128)(2,1)}, u32[]{:S(2)}) copy-start(bf16[1024,512]{0,1:T(8,128)(2,1)} %get-tuple-element.79) | copy-start | bytes 3145732
  115.3 7.0 %collective-permute-start.18 = (bf16[512,1024]{1,0:T(8,128)(2,1)}, bf16[512,1024]{1,0:T(8,128)(2,1)}, u32[]{:S(2)}, u32[]{:S(2)}) collective-permute-start(bf16[512,1024]{1,0:T(8,128)(2,1)} %convolution_convert_fusion), channel_id=1, source_target_pairs={{0,2},{2,0},{4,6},{6,4},{1,3},{3,1},{5,7},{7,5},{8,10},{10,8},{12,... | collective-permute-start | bytes 3145736 | tf_op jit(solution)/shard_map/ppermute | solution.py:189
  115.3 11.4 %collective-permute-start.16 = (bf16[512,1024]{1,0:T(8,128)(2,1)}, bf16[512,1024]{1,0:T(8,128)(2,1)}, u32[]{:S(2)}, u32[]{:S(2)}) collective-permute-start(bf16[512,1024]{1,0:T(8,128)(2,1)} %convolution_convert_fusion.1), channel_id=1, source_target_pairs={{0,2},{2,0},{4,6},{6,4},{1,3},{3,1},{5,7},{7,5},{8,10},{10,8},{12,... | collective-permute-start | bytes 3145736 | tf_op jit(solution)/shard_map/ppermute | solution.py:189
  115.8 6.5 %copy-start.33 = (f32[512,1024]{1,0:T(8,128)S(1)}, f32[512,1024]{1,0:T(8,128)}, u32[]{:S(2)}) copy-start(f32[512,1024]{1,0:T(8,128)} %fusion.15) | copy-start | bytes 6291460
  117.5 12.1 %collective-permute-start.15 = (bf16[1,128,1024]{2,1,0:T(8,128)(2,1)S(1)}, bf16[1,128,1024]{2,1,0:T(8,128)(2,1)S(1)}, u32[]{:S(2)}, u32[]{:S(2)}) collective-permute-start(bf16[1,128,1024]{2,1,0:T(8,128)(2,1)S(1)} %slice.150), channel_id=1, source_target_pairs={{0,4},{2,6},{4,0},{6,2},{1,5},{3,7},{5,1},{7,3},{8,12},{10,14},{12... | collective-permute-start | bytes 786440 | tf_op jit(solution)/shard_map/ppermute | solution.py:189
  118.7 8.0 %copy-start.32 = (f32[512,1024]{1,0:T(8,128)S(1)}, f32[512,1024]{1,0:T(8,128)}, u32[]{:S(2)}) copy-start(f32[512,1024]{1,0:T(8,128)} %fusion.20) | copy-start | bytes 6291460
  118.7 10.7 %collective-permute-start.14 = (bf16[1,128,1024]{2,1,0:T(8,128)(2,1)S(1)}, bf16[1,128,1024]{2,1,0:T(8,128)(2,1)S(1)}, u32[]{:S(2)}, u32[]{:S(2)}) collective-permute-start(bf16[1,128,1024]{2,1,0:T(8,128)(2,1)S(1)} %fusion.24), channel_id=1, source_target_pairs={{0,1},{1,0},{2,3},{3,2},{4,5},{5,4},{6,7},{7,6},{8,9},{9,8},{10,11... | collective-permute-start | bytes 786440 | tf_op jit(solution)/shard_map/ppermute | solution.py:194
  121.1 26.1 %collective-permute-start.13 = (bf16[1,1024]{1,0:T(2,128)(2,1)S(1)}, bf16[1,1024]{1,0:T(2,128)(2,1)S(1)}, u32[]{:S(2)}, u32[]{:S(2)}) collective-permute-start(bf16[1,1024]{1,0:T(2,128)(2,1)S(1)} %slice.91), channel_id=1, source_target_pairs={{1,0},{3,2},{5,4},{7,6},{9,8},{11,10},{13,12},{15,14},{17,16},{19,... | collective-permute-start | bytes 6152 | tf_op jit(solution)/shard_map/ppermute | solution.py:199
  124.0 14.6 %collective-permute-start.19 = (bf16[2,128,1024]{2,1,0:T(8,128)(2,1)S(1)}, bf16[2,128,1024]{2,1,0:T(8,128)(2,1)S(1)}, u32[]{:S(2)}, u32[]{:S(2)}) collective-permute-start(bf16[2,128,1024]{2,1,0:T(8,128)(2,1)S(1)} %fusion.12), channel_id=1, source_target_pairs={{0,1},{1,0},{2,3},{3,2},{4,5},{5,4},{6,7},{7,6},{8,9},{9,8},{10,11... | collective-permute-start | bytes 1572872 | tf_op jit(solution)/shard_map/ppermute | solution.py:194
  128.5 12.8 %collective-permute-start.17 = (bf16[1,256,1024]{2,1,0:T(8,128)(2,1)S(1)}, bf16[1,256,1024]{2,1,0:T(8,128)(2,1)S(1)}, u32[]{:S(2)}, u32[]{:S(2)}) collective-permute-start(bf16[1,256,1024]{2,1,0:T(8,128)(2,1)S(1)} %fusion.13), channel_id=1, source_target_pairs={{0,4},{2,6},{4,0},{6,2},{1,5},{3,7},{5,1},{7,3},{8,12},{10,14},{12... | collective-permute-start | bytes 1572872 | tf_op jit(solution)/shard_map/ppermute | solution.py:189
  141.6 8.2 %collective-permute-start.20 = (bf16[1,32,2048]{2,1,0:T(8,128)(2,1)S(1)}, bf16[1,32,2048]{2,1,0:T(8,128)(2,1)S(1)}, u32[]{:S(2)}, u32[]{:S(2)}) collective-permute-start(bf16[1,32,2048]{2,1,0:T(8,128)(2,1)S(1)} %get-tuple-element.106), channel_id=1, source_target_pairs={{0,8},{8,16},{16,24},{24,0},{1,9},{9,17},{17,25},{25,1},{2,10},{10... | collective-permute-start | bytes 393224 | tf_op jit(solution)/shard_map/ppermute | solution.py:194
  143.2 9.9 %collective-permute-start.21 = (bf16[1,32,2048]{2,1,0:T(8,128)(2,1)S(1)}, bf16[1,32,2048]{2,1,0:T(8,128)(2,1)S(1)}, u32[]{:S(2)}, u32[]{:S(2)}) collective-permute-start(bf16[1,32,2048]{2,1,0:T(8,128)(2,1)S(1)} %get-tuple-element.108), channel_id=1, source_target_pairs={{0,16},{8,24},{16,0},{24,8},{1,17},{9,25},{17,1},{25,9},{2,18},{10... | collective-permute-start | bytes 393224 | tf_op jit(solution)/shard_map/ppermute | solution.py:194
  145.8 7.3 %collective-permute-start.22 = (bf16[1,32,2048]{2,1,0:T(8,128)(2,1)S(1)}, bf16[1,32,2048]{2,1,0:T(8,128)(2,1)S(1)}, u32[]{:S(2)}, u32[]{:S(2)}) collective-permute-start(bf16[1,32,2048]{2,1,0:T(8,128)(2,1)S(1)} %get-tuple-element.107), channel_id=1, source_target_pairs={{0,24},{8,0},{16,8},{24,16},{1,25},{9,1},{17,9},{25,17},{2,26},{10... | collective-permute-start | bytes 393224 | tf_op jit(solution)/shard_map/ppermute | solution.py:194
  147.3 10.4 %collective-permute-start.26 = (bf16[1,128,1024]{2,1,0:T(8,128)(2,1)S(1)}, bf16[1,128,1024]{2,1,0:T(8,128)(2,1)S(1)}, u32[]{:S(2)}, u32[]{:S(2)}) collective-permute-start(bf16[1,128,1024]{2,1,0:T(8,128)(2,1)S(1)} %fusion.25), channel_id=1, source_target_pairs={{0,1},{1,0},{2,3},{3,2},{4,5},{5,4},{6,7},{7,6},{8,9},{9,8},{10,11... | collective-permute-start | bytes 786440 | tf_op jit(solution)/shard_map/ppermute | solution.py:194
  147.7 10.0 %collective-permute-start.27 = (bf16[1,128,1024]{2,1,0:T(8,128)(2,1)S(1)}, bf16[1,128,1024]{2,1,0:T(8,128)(2,1)S(1)}, u32[]{:S(2)}, u32[]{:S(2)}) collective-permute-start(bf16[1,128,1024]{2,1,0:T(8,128)(2,1)S(1)} %slice.149), channel_id=1, source_target_pairs={{0,4},{2,6},{4,0},{6,2},{1,5},{3,7},{5,1},{7,3},{8,12},{10,14},{12... | collective-permute-start | bytes 786440 | tf_op jit(solution)/shard_map/ppermute | solution.py:189
  153.2 9.1 %collective-permute-start.23 = (bf16[32,2048]{1,0:T(8,128)(2,1)S(1)}, bf16[32,2048]{1,0:T(8,128)(2,1)S(1)}, u32[]{:S(2)}, u32[]{:S(2)}) collective-permute-start(bf16[32,2048]{1,0:T(8,128)(2,1)S(1)} %get-tuple-element.96), channel_id=1, source_target_pairs={{0,24},{8,0},{16,8},{24,16},{1,25},{9,1},{17,9},{25,17},{2,26},{10... | collective-permute-start | bytes 393224 | tf_op jit(solution)/shard_map/ppermute | solution.py:194
  157.0 18.7 %collective-permute-start.24 = (bf16[32,2048]{1,0:T(8,128)(2,1)S(1)}, bf16[32,2048]{1,0:T(8,128)(2,1)S(1)}, u32[]{:S(2)}, u32[]{:S(2)}) collective-permute-start(bf16[32,2048]{1,0:T(8,128)(2,1)S(1)} %get-tuple-element.96), channel_id=1, source_target_pairs={{0,16},{8,24},{16,0},{24,8},{1,17},{9,25},{17,1},{25,9},{2,18},{10... | collective-permute-start | bytes 393224 | tf_op jit(solution)/shard_map/ppermute | solution.py:194
  157.5 18.3 %collective-permute-start.25 = (bf16[32,2048]{1,0:T(8,128)(2,1)S(1)}, bf16[32,2048]{1,0:T(8,128)(2,1)S(1)}, u32[]{:S(2)}, u32[]{:S(2)}) collective-permute-start(bf16[32,2048]{1,0:T(8,128)(2,1)S(1)} %get-tuple-element.96), channel_id=1, source_target_pairs={{0,8},{8,16},{16,24},{24,0},{1,9},{9,17},{17,25},{25,1},{2,10},{10... | collective-permute-start | bytes 393224 | tf_op jit(solution)/shard_map/ppermute | solution.py:194
  158.0 18.0 %collective-permute-start.28 = (bf16[1,32,2048]{2,1,0:T(8,128)(2,1)S(1)}, bf16[1,32,2048]{2,1,0:T(8,128)(2,1)S(1)}, u32[]{:S(2)}, u32[]{:S(2)}) collective-permute-start(bf16[1,32,2048]{2,1,0:T(8,128)(2,1)S(1)} %get-tuple-element.103), channel_id=1, source_target_pairs={{0,8},{8,16},{16,24},{24,0},{1,9},{9,17},{17,25},{25,1},{2,10},{10... | collective-permute-start | bytes 393224 | tf_op jit(solution)/shard_map/ppermute | solution.py:194
  160.9 17.6 %collective-permute-start.29 = (bf16[1,32,2048]{2,1,0:T(8,128)(2,1)S(1)}, bf16[1,32,2048]{2,1,0:T(8,128)(2,1)S(1)}, u32[]{:S(2)}, u32[]{:S(2)}) collective-permute-start(bf16[1,32,2048]{2,1,0:T(8,128)(2,1)S(1)} %get-tuple-element.105), channel_id=1, source_target_pairs={{0,16},{8,24},{16,0},{24,8},{1,17},{9,25},{17,1},{25,9},{2,18},{10... | collective-permute-start | bytes 393224 | tf_op jit(solution)/shard_map/ppermute | solution.py:194
  162.2 16.4 %collective-permute-start.30 = (bf16[1,32,2048]{2,1,0:T(8,128)(2,1)S(1)}, bf16[1,32,2048]{2,1,0:T(8,128)(2,1)S(1)}, u32[]{:S(2)}, u32[]{:S(2)}) collective-permute-start(bf16[1,32,2048]{2,1,0:T(8,128)(2,1)S(1)} %get-tuple-element.104), channel_id=1, source_target_pairs={{0,24},{8,0},{16,8},{24,16},{1,25},{9,1},{17,9},{25,17},{2,26},{10... | collective-permute-start | bytes 393224 | tf_op jit(solution)/shard_map/ppermute | solution.py:194
  175.9 18.3 %copy-start.27 = (bf16[256,2048]{1,0:T(8,128)(2,1)S(1)}, bf16[256,2048]{1,0:T(8,128)(2,1)}, u32[]{:S(2)}) copy-start(bf16[256,2048]{1,0:T(8,128)(2,1)} %copy-done.26) | copy-start | bytes 3145732
  175.9 18.3 %copy-start.31 = (bf16[256,2048]{1,0:T(8,128)(2,1)S(1)}, bf16[256,2048]{1,0:T(8,128)(2,1)}, u32[]{:S(2)}) copy-start(bf16[256,2048]{1,0:T(8,128)(2,1)} %copy-done.30) | copy-start | bytes 3145732
  178.8 5.5 %collective-permute-start.31 = (bf16[32,2048]{1,0:T(8,128)(2,1)S(1)}, bf16[32,2048]{1,0:T(8,128)(2,1)S(1)}, u32[]{:S(2)}, u32[]{:S(2)}) collective-permute-start(bf16[32,2048]{1,0:T(8,128)(2,1)S(1)} %fusion.46), channel_id=1, source_target_pairs={{0,24},{8,0},{16,8},{24,16},{1,25},{9,1},{17,9},{25,17},{2,26},{10... | collective-permute-start | bytes 393224 | tf_op jit(solution)/shard_map/ppermute | solution.py:194
  180.4 12.5 %collective-permute-start.32 = (bf16[32,2048]{1,0:T(8,128)(2,1)S(1)}, bf16[32,2048]{1,0:T(8,128)(2,1)S(1)}, u32[]{:S(2)}, u32[]{:S(2)}) collective-permute-start(bf16[32,2048]{1,0:T(8,128)(2,1)S(1)} %fusion.46), channel_id=1, source_target_pairs={{0,16},{8,24},{16,0},{24,8},{1,17},{9,25},{17,1},{25,9},{2,18},{10... | collective-permute-start | bytes 393224 | tf_op jit(solution)/shard_map/ppermute | solution.py:194
  182.2 10.7 %collective-permute-start.33 = (bf16[32,2048]{1,0:T(8,128)(2,1)S(1)}, bf16[32,2048]{1,0:T(8,128)(2,1)S(1)}, u32[]{:S(2)}, u32[]{:S(2)}) collective-permute-start(bf16[32,2048]{1,0:T(8,128)(2,1)S(1)} %fusion.46), channel_id=1, source_target_pairs={{0,8},{8,16},{16,24},{24,0},{1,9},{9,17},{17,25},{25,1},{2,10},{10... | collective-permute-start | bytes 393224 | tf_op jit(solution)/shard_map/ppermute | solution.py:194
  182.2 22.1 %collective-permute-start.35 = (bf16[128,2048]{1,0:T(8,128)(2,1)S(1)}, bf16[128,2048]{1,0:T(8,128)(2,1)S(1)}, u32[]{:S(2)}, u32[]{:S(2)}) collective-permute-start(bf16[128,2048]{1,0:T(8,128)(2,1)S(1)} %constant_dynamic-slice_fusion.1), channel_id=1, source_target_pairs={{0,1},{1,0},{2,3},{3,2},{4,5},{5,4},{6,7},{7,6},{8,9},{9,8},{10,11... | collective-permute-start | bytes 1572872 | tf_op jit(solution)/shard_map/ppermute | solution.py:194
  193.0 13.6 %collective-permute-start.34 = (bf16[128,2048]{1,0:T(8,128)(2,1)S(1)}, bf16[128,2048]{1,0:T(8,128)(2,1)S(1)}, u32[]{:S(2)}, u32[]{:S(2)}) collective-permute-start(bf16[128,2048]{1,0:T(8,128)(2,1)S(1)} %constant_dynamic-slice_fusion), channel_id=1, source_target_pairs={{0,1},{1,0},{2,3},{3,2},{4,5},{5,4},{6,7},{7,6},{8,9},{9,8},{10,11... | collective-permute-start | bytes 1572872 | tf_op jit(solution)/shard_map/ppermute | solution.py:194
  (17 other events, 25.2 us)
